TPU v7x, 32 devices: a whole 2x2x4 slice. The times are simulated.
32 devices in a mesh: section: 2 (over x), dp: 16 (over z, y, core).
Axes of the slice: x: 2, y: 2, z: 4, core: 2. Of those that a mesh axis runs over, the one named last changes fastest.
Arguments:
- hidden: bfloat16 [2, 2048, 8192], P('section', 'dp'), may hold values from -6 to 6
- gain_table: bfloat16 [10, 8192], replicated, may hold values from 0.099609375 to 1.8984375
- layer_counts: int32 [2], P('section'), may hold values from 1 to 8, 10 in all
- positions: int32 [2, 2048], P('section', 'dp'), may hold values from 0 to 8191, as said below
- queries: bfloat16 [2, 2048, 4096], P('section', 'dp'), may hold values from -35 to 35
- keys: bfloat16 [2, 2048, 512], P('section', 'dp'), may hold values from -10 to 10
- value_weight: bfloat16 [2, 8192, 512], P('section', 'dp'), may hold values from -0.0625 to 0.0625
- out_grad: bfloat16 [2, 2048, 4096], P('section', 'dp'), may hold values from -6 to 6
Outputs:
- query_grad: bfloat16 [2, 2048, 4096], P('section', 'dp')
- key_grad: bfloat16 [2, 2048, 512], P('section', 'dp')
- value_weight_grad: bfloat16 [2, 8192, 512], P('section', 'dp')
- upstream_grad: bfloat16 [2, 2048, 8192], P('section', 'dp')
Inputs may be any that keep to these rules, and one draw needn't show every extreme that they name: Within each device's block of 128 tokens the positions rise by 1 to 3 from token to token.
All inputs are finite; a program needn't handle non-finite values. No bound on the sum of `layer_counts` on one device may be relied on, other than what follows from the above.
Results may differ from a plain program's by a relative error of at most 0.02.
Values may be sent and summed in bfloat16 or wider, within the bound.
No kernel may reach another device: no remote copies, remote signals or barrier semaphores. Data moves between devices by JAX's collectives and lax.ppermute only.
A program may use at most 128 MiB of HBM per device.

v0:
```python
import math

import jax
import jax.numpy as jnp
from jax import lax
from jax.sharding import PartitionSpec as P

HQ = 32
HK = 4
HD = 128


def carried_in(value, axis, join, neutral):
    count, mine = (lax.axis_size(axis), lax.axis_index(axis))
    pieces = lax.all_gather(value, axis)
    subtotal = jnp.full_like(value, 0) + jnp.asarray(neutral, value.dtype)

    def turn(position, subtotal):
        longer = join(subtotal, pieces[position])
        return jnp.where(position < mine, longer, subtotal)

    return lax.fori_loop(0, count - 1, turn, subtotal)


def passed_along(block, axis, distance):
    devices = range(lax.axis_size(axis))
    route = [(i - distance, i) for i in devices if i - distance in devices]
    return lax.ppermute(block, axis, route)


def rope_angles(places, width):
    half = width // 2
    steps = jnp.arange(half, dtype=jnp.float32)
    freq = jnp.exp(steps * (-2.0 * math.log(500000.0) / width))
    angle = places.astype(jnp.float32)[:, None] * freq[None, :]
    return (jnp.cos(angle), jnp.sin(angle))


def rotate(values, cosine, sine, heads, width):
    rows_here = values.shape[0]
    split = values.reshape(rows_here, heads, 2, width // 2)
    first = split[:, :, 0, :]
    second = split[:, :, 1, :]
    cosine = cosine[:, None, :]
    sine = sine[:, None, :]
    turned = jnp.stack([first * cosine - second * sine, first * sine + second * cosine], axis=2)
    return turned.reshape(rows_here, heads * width)


def add_counts(earlier, later):
    return earlier + later


def shards(hidden, gain_table, layer_counts, positions, queries, keys, value_weight, out_grad):
    tokens_in = hidden[0]
    places = positions[0]
    weight = value_weight[0]
    rows_here = tokens_in.shape[0]
    share = HQ // HK
    scale = HD ** (-0.5)
    before = carried_in(layer_counts, "section", add_counts, jnp.zeros_like(layer_counts))
    last = before[0] + layer_counts[0] - 1
    table_rows = jnp.arange(gain_table.shape[0], dtype=jnp.int32)
    gain_f = jnp.sum(
        jnp.where((table_rows == last)[:, None], gain_table.astype(jnp.float32), 0.0), axis=0
    )
    hidden_f = tokens_in.astype(jnp.float32)
    inverse = lax.rsqrt(jnp.mean(hidden_f * hidden_f, axis=-1, keepdims=True) + 1e-05)
    normed = (hidden_f * inverse * gain_f).astype(jnp.bfloat16)
    columns = normed
    values = jnp.dot(
        columns,
        lax.all_gather(weight, "dp", axis=0, tiled=True),
        preferred_element_type=jnp.float32,
    ).astype(jnp.bfloat16)
    cosine, sine = rope_angles(places, HD)
    q_rot = rotate(queries[0].astype(jnp.float32), cosine, sine, HQ, HD).astype(jnp.bfloat16)
    k_rot = rotate(keys[0].astype(jnp.float32), cosine, sine, HK, HD).astype(jnp.bfloat16)
    q_four = q_rot.reshape(rows_here, HK, share, HD)
    k_three = k_rot.reshape(rows_here, HK, HD)
    v_three = values.reshape(rows_here, HK, HD)
    d_four = out_grad[0].reshape(rows_here, HK, share, HD)
    scores = (
        jnp.einsum("tgrd,ugd->grtu", q_four, k_three, preferred_element_type=jnp.float32) * scale
    )
    later = jnp.arange(rows_here)[:, None] >= jnp.arange(rows_here)[None, :]
    scores = jnp.where(later, scores, -1e30)
    top = jnp.max(scores, axis=-1, keepdims=True)
    expo = jnp.exp(scores - top)
    probs = expo / jnp.sum(expo, axis=-1, keepdims=True)
    probs_low = probs.astype(jnp.bfloat16)
    attended = jnp.einsum("grtu,ugd->tgrd", probs_low, v_three, preferred_element_type=jnp.float32)
    delta = jnp.sum(d_four.astype(jnp.float32) * attended, axis=-1)
    delta = jnp.transpose(delta, (1, 2, 0))[..., None]
    d_probs = jnp.einsum("tgrd,ugd->grtu", d_four, v_three, preferred_element_type=jnp.float32)
    d_scores = (probs * (d_probs - delta) * scale).astype(jnp.bfloat16)
    dq_rot = jnp.einsum("grtu,ugd->tgrd", d_scores, k_three, preferred_element_type=jnp.float32)
    dk_rot = jnp.einsum("grtu,tgrd->ugd", d_scores, q_four, preferred_element_type=jnp.float32)
    d_values = jnp.einsum("grtu,tgrd->ugd", probs_low, d_four, preferred_element_type=jnp.float32)
    query_grad = rotate(dq_rot.reshape(rows_here, HQ * HD), cosine, -sine, HQ, HD).astype(
        jnp.bfloat16
    )
    key_grad = rotate(dk_rot.reshape(rows_here, HK * HD), cosine, -sine, HK, HD).astype(
        jnp.bfloat16
    )
    values_grad = d_values.reshape(rows_here, HK * HD).astype(jnp.bfloat16)
    columns = normed
    weight_grad = lax.psum_scatter(
        jnp.einsum("td,te->de", columns, values_grad, preferred_element_type=jnp.float32).astype(
            jnp.bfloat16
        ),
        "dp",
        scatter_dimension=0,
        tiled=True,
    ).astype(jnp.float32)
    weight_grad = weight_grad.astype(jnp.bfloat16)
    d_normed = jnp.einsum(
        "te,de->td",
        values_grad,
        lax.all_gather(weight, "dp", axis=0, tiled=True),
        preferred_element_type=jnp.float32,
    )
    scaled = gain_f * d_normed
    local_grad = inverse * scaled - hidden_f * inverse**3 * jnp.mean(
        hidden_f * scaled, axis=-1, keepdims=True
    )
    local_grad = local_grad.astype(jnp.bfloat16)
    upstream = passed_along(local_grad, "section", -1)
    return (query_grad[None], key_grad[None], weight_grad[None], upstream[None])


def solution(mesh):
    in_specs = (
        P("section", "dp", None),
        P(),
        P("section"),
        P("section", "dp"),
        P("section", "dp", None),
        P("section", "dp", None),
        P("section", "dp", None),
        P("section", "dp", None),
    )
    out_specs = (
        P("section", "dp", None),
        P("section", "dp", None),
        P("section", "dp", None),
        P("section", "dp", None),
    )
    return jax.shard_map(shards, mesh=mesh, in_specs=in_specs, out_specs=out_specs, check_vma=False)
```

profile of v0, /device:TPU:0, one launch (start us, length us, event | category | flops | bytes accessed | tf_op | source)
XLA Modules:
  0.0 214.6 jit_solution(12217851902262697932)
XLA Ops:
  7.2 0.0 all-gather.4.cloned.1.call-start
  7.2 0.7 all-gather.4.cloned.1.call-update
  7.9 0.0 reduce-scatter.2.cloned.1.call-start
  8.6 1.2 dynamic-slice
  9.8 0.8 dynamic-update-slice
  10.6 5.2 %all-reduce = s32[2]{0:T(128)S(1)} all-reduce(s32[2]{0:T(128)S(1)} %dynamic-update-slice), channel_id=2, replica_groups=mesh['section'=2,'dp'=16] {'section'}, use_global_device_ids=true, to_apply=%add | all-reduce | flops 2 | bytes 16
  15.8 1.0 copy.32
  16.9 1.6 copy.33
  18.5 0.0 copy-start.4
  18.5 0.2 convert.36
  18.8 0.0 copy-start.2
  18.8 2.3 %copy.36 = bf16[1,128,4096]{1,2,0:T(8,128)(2,1)} copy(bf16[1,128,4096]{2,1,0:T(8,128)(2,1)} %param.15) | data formatting | bytes 2097152 | tf_op args[7]
  21.2 0.0 copy-done.4
  21.2 0.2 fusion.41
  21.5 0.0 copy-done.2
  21.5 0.2 select_reduce_fusion
  21.7 0.3 subtract_convert_fusion.1
  22.0 0.1 pad_maximum_fusion
  22.1 2.2 %fusion.46 = (f32[4,8,128]{2,1,0:T(8,128)S(1)}, f32[4,8,128,128]{2,3,1,0:T(8,128)}) fusion(pred[128,128]{0,1:T(8,128)(4,1)S(1)} %iota_compare_fusion, bf16[128,4,128,1]{0,2,3,1:T(8,128)(2,1)S(1)} %bitcast.125, bf16[128,4,8,128]{0,3,2,1:T(8,128)(2,1)S(1)} %bitcast.116), kind=kOutput, calls=%fused_computation.69 | convolution fusion | flops 136315008 | bytes 3309568 | tf_op jit(solution)/shard_map/sub | solution.py:89
  24.2 0.0 copy-start
  24.2 2.5 %fusion.29 = bf16[4,128,128]{1,2,0:T(8,128)(2,1)S(1)} fusion(bf16[128,4,8,128]{0,3,2,1:T(8,128)(2,1)} %bitcast.120, f32[4,8,128,128]{2,3,1,0:T(8,128)} %get-tuple-element.39, f32[4,8,128]{2,1,0:T(8,128)S(1)} %get-tuple-element.38), kind=kOutput, calls=%fused_computation.36 | convolution fusion | flops 135331840 | bytes 3293184 | tf_op jit(solution)/shard_map/grtu,tgrd->ugd/dot_general | solution.py:99
  26.7 61.1 %all-gather.4.cloned.1.call-done = bf16[1,8192,512]{2,1,0:T(8,128)(2,1)} async-done(((bf16[1,512,512]{2,1,0:T(8,128)(2,1)}), bf16[1,8192,512]{2,1,0:T(8,128)(2,1)}) %all-gather.4.cloned.1.call-update) | async-done | bytes 8388624 | tf_op jit(solution)/shard_map/all_gather | solution.py:73
  87.8 0.0 copy-done
  87.8 8.2 %fusion.14 = (f32[128]{0:T(128)S(1)}, f32[128]{0:T(128)S(1)}, f32[128,8192]{1,0:T(8,128)}) fusion(bf16[1,128,8192]{2,1,0:T(8,128)(2,1)S(1)} %copy-done, bf16[128,512]{0,1:T(8,128)(2,1)S(1)} %bitcast.123, bf16[1,8192,512]{2,1,0:T(8,128)(2,1)} %all-gather.4.cloned.1.call-done, f32[8192]{0:T(1024)S(1)} %select_reduce_fusion), kind=kOutput, calls=%fused_computation.18 | convolution fusion | flops 1080033024 | bytes 14844928 | tf_op jit(solution)/shard_map/te,de->td/dot_general | solution.py:117
  96.0 5.7 %convolution_convert_fusion = bf16[8192,512]{1,0:T(8,128)(2,1)} fusion(bf16[128,512]{0,1:T(8,128)(2,1)S(1)} %bitcast.124, bf16[1,128,8192]{2,1,0:T(8,128)(2,1)S(1)} %copy-done, f32[8192]{0:T(1024)S(1)} %select_reduce_fusion, f32[128]{0:T(128)S(1)} %get-tuple-element.37), kind=kOutput, calls=%fused_computation.1 | convolution fusion | flops 1082130432 | bytes 10650112 | tf_op jit(solution)/shard_map/td,te->de/dot_general | solution.py:109
  101.7 0.0 reduce-scatter.2.cloned.1.call-update
  101.7 5.3 %fusion.30 = bf16[128,512]{1,0:T(8,128)(2,1)} fusion(bf16[1,8192,512]{2,1,0:T(8,128)(2,1)} %all-gather.4.cloned.1.call-done, bf16[1,128,8192]{2,1,0:T(8,128)(2,1)S(1)} %copy-done, f32[8192]{0:T(1024)S(1)} %select_reduce_fusion, f32[128]{0:T(128)S(1)} %get-tuple-element.37), kind=kOutput, calls=%fused_computation.37 | convolution fusion | flops 1078001664 | bytes 10650112 | tf_op jit(solution)/shard_map/dot_general | solution.py:71
  107.1 1.0 reshape.180
  108.0 0.8 copy.50
  108.8 0.0 copy-start.1
  108.8 0.0 copy-start.3
  108.8 0.0 copy-start.5
  108.8 5.2 %fusion.13 = bf16[128,8192]{1,0:T(8,128)(2,1)} fusion(bf16[1,128,8192]{2,1,0:T(8,128)(2,1)S(1)} %copy-done, f32[128,8192]{1,0:T(8,128)} %get-tuple-element.40, f32[128]{0:T(128)S(1)} %get-tuple-element.41, f32[128]{0:T(128)S(1)} %get-tuple-element.36, f32[128]{0:T(128)S(1)} %get-tuple-element.37), kind=kLoop, calls=%fused_computation.17 | loop fusion | flops 6291456 | bytes 8390144 | tf_op jit(solution)/shard_map/convert_element_type | solution.py:127
  114.0 1.5 collective-permute-start
  115.4 0.0 copy-done.1
  115.4 0.0 copy-done.3
  115.5 0.0 copy-done.5
  115.5 0.5 fusion.20
  116.0 0.6 fusion.23
  116.6 0.4 fusion.48
  117.1 0.8 copy.45
  117.9 0.4 fusion.47
  118.3 0.3 subtract_convert_fusion
  118.6 0.1 pad_maximum_fusion.1
  118.7 1.3 copy.44
  120.0 43.9 %collective-permute-done = bf16[128,8192]{1,0:T(8,128)(2,1)} collective-permute-done((bf16[128,8192]{1,0:T(8,128)(2,1)}, bf16[128,8192]{1,0:T(8,128)(2,1)}, u32[]{:S(2)}, u32[]{:S(2)}) %collective-permute-start) | collective-permute-done | bytes 2097184 | tf_op jit(solution)/shard_map/ppermute | solution.py:28
  164.0 40.7 %reduce-scatter.2.cloned.1.call-done = bf16[512,512]{1,0:T(8,128)(2,1)} async-done(((bf16[8192,512]{1,0:T(8,128)(2,1)}), bf16[512,512]{1,0:T(8,128)(2,1)}) %reduce-scatter.2.cloned.1.call-update) | async-done | bytes 524304 | tf_op jit(solution)/shard_map/reduce_scatter | solution.py:108
  204.7 3.1 %copy.67 = bf16[1,128,8192]{2,1,0:T(8,128)(2,1)} copy(bf16[1,128,8192]{2,1,0:T(8,128)(2,1)} %bitcast.40) | data formatting | bytes 4194304
  (11 shorter events, 0.2 us)
Async XLA Ops:
  7.2 80.6 %all-gather.4.cloned.1.call-start = ((), (), s32[]{:S(2)}) async-start(), calls=%async_computation.2 | async-start | bytes 8912896 | tf_op jit(solution)/shard_map/all_gather | solution.py:73
  7.9 196.8 %reduce-scatter.2.cloned.1.call-start = ((), (), s32[]{:S(2)}) async-start(), calls=%async_computation.1 | async-start | bytes 8912896 | tf_op jit(solution)/shard_map/reduce_scatter | solution.py:108
  18.5 2.6 %copy-start.4 = (s32[1,128]{1,0:T(1,128)S(1)}, s32[1,128]{1,0:T(1,128)}, u32[]{:S(2)}) copy-start(s32[1,128]{1,0:T(1,128)} %param.11) | copy-start | bytes 1540
  18.8 2.7 %copy-start.2 = (bf16[10,8192]{1,0:T(8,128)(2,1)S(1)}, bf16[10,8192]{1,0:T(8,128)(2,1)}, u32[]{:S(2)}) copy-start(bf16[10,8192]{1,0:T(8,128)(2,1)} %param.9) | copy-start | bytes 491524
  24.2 63.6 %copy-start = (bf16[1,128,8192]{2,1,0:T(8,128)(2,1)S(1)}, bf16[1,128,8192]{2,1,0:T(8,128)(2,1)}, u32[]{:S(2)}) copy-start(bf16[1,128,8192]{2,1,0:T(8,128)(2,1)} %param.8) | copy-start | bytes 6291460
  108.8 6.6 %copy-start.1 = (bf16[1,128,4096]{1,2,0:T(8,128)(2,1)S(1)}, bf16[1,128,4096]{1,2,0:T(8,128)(2,1)}, u32[]{:S(2)}) copy-start(bf16[1,128,4096]{1,2,0:T(8,128)(2,1)} %copy.36) | copy-start | bytes 3145732
  108.8 6.7 %copy-start.3 = (bf16[128,4,128,1]{0,2,3,1:T(8,128)(2,1)S(1)}, bf16[128,4,128,1]{0,2,3,1:T(8,128)(2,1)}, u32[]{:S(2)}) copy-start(bf16[128,4,128,1]{0,2,3,1:T(8,128)(2,1)} %copy.50) | copy-start | bytes 393220
  108.8 6.7 %copy-start.5 = (f32[4,8,128,128]{2,3,1,0:T(8,128)S(1)}, f32[4,8,128,128]{2,3,1,0:T(8,128)}, u32[]{:S(2)}) copy-start(f32[4,8,128,128]{2,3,1,0:T(8,128)} %get-tuple-element.39) | copy-start | bytes 6291460
  114.0 50.0 %collective-permute-start = (bf16[128,8192]{1,0:T(8,128)(2,1)}, bf16[128,8192]{1,0:T(8,128)(2,1)}, u32[]{:S(2)}, u32[]{:S(2)}) collective-permute-start(bf16[128,8192]{1,0:T(8,128)(2,1)} %fusion.13), channel_id=1, source_target_pairs={{16,0},{17,1},{18,2},{19,3},{20,4},{21,5},{22,6},{23,7},{24,8},{25... | collective-permute-start | bytes 6291464 | tf_op jit(solution)/shard_map/ppermute | solution.py:28
Sparse Core Ops, SparseCore 0:
  10.2 77.5 all-gather.3
  101.8 102.8 reduce-scatter.1
where the time goes:
time: 215 us
  waiting for transfers between devices  146 us (68%)
  matrix products  25.8 us (12%)
  between operations  15 us (7%)
  local copies, waits for them, and re-layouts  13.9 us (6%)
  other arithmetic  6.78 us (3%)
  blocking collectives  5.19 us (2%)
    all_gather x1, waiting for transfers between devices, shards(): lax.all_gather(weight, 'dp', axis=0, tiled=True)  61.1 us
    ppermute x1, waiting for transfers between devices, passed_along(): return lax.ppermute(block, axis, route)  43.9 us
    reduce_scatter x1, waiting for transfers between devices, shards(): lax.psum_scatter(jnp.einsum('td,te->de', columns, values_grad, preferred_...  40.7 us
    unnamed x21, local copies, waits for them, and re-layouts  12.2 us
    dot_general x1, matrix products, shards(): jnp.einsum('te,de->td', values_grad, lax.all_gather(weight, 'dp', axis=0,...  8.2 us
    dot_general x1, matrix products, shards(): jnp.einsum('td,te->de', columns, values_grad, preferred_element_type=jnp....  5.68 us
    dot_general x1, matrix products, shards(): jnp.dot(columns, lax.all_gather(weight, 'dp', axis=0, tiled=True), prefer...  5.35 us
    unnamed x1, blocking collectives  5.19 us
  transfers between devices with their start and end apart: 3, of which 3 were waited for; matrix products, arithmetic and copies ran while one was open for 14% of the time, Pallas kernels for 0%

commit v1 on v0

v1 whole, which is shorter than its diff:
```python
import functools
import math

import jax
import jax.numpy as jnp
from jax import lax
from jax.experimental import pallas as pl
from jax.experimental.pallas import tpu as pltpu
from jax.sharding import PartitionSpec as P

HQ = 32
HK = 4
HD = 128
SHARE = HQ // HK
EPS = 1e-05
F32 = jnp.float32
BF16 = jnp.bfloat16
VMEM_LIMIT = 48 * 1024 * 1024


def params(**more):
    return pltpu.CompilerParams(vmem_limit_bytes=VMEM_LIMIT, **more)


def mm(a, b, contract):
    return lax.dot_general(a, b, ((contract[:1], contract[1:]), ((), ())), preferred_element_type=F32)


def sds(shape, dtype):
    return jax.ShapeDtypeStruct(shape, dtype)


def rope_tables(places):
    half = HD // 2
    steps = jnp.arange(half, dtype=F32)
    freq = jnp.exp(steps * (-2.0 * math.log(500000.0) / HD))
    angle = places.astype(F32)[:, None] * freq[None, :]
    cosine, sine = jnp.cos(angle), jnp.sin(angle)
    return jnp.concatenate([cosine, cosine], 1), jnp.concatenate([-sine, sine], 1)


def turn(x, cosine, sine):
    return x * cosine + pltpu.roll(x, HD // 2, 1) * sine


def turn_back(x, cosine, sine):
    return x * cosine - pltpu.roll(x, HD // 2, 1) * sine


def prep_kernel(where, mine_in, theirs_in, gain_m, gain_t, mine, theirs, gain_out, inverse, total, *, width):
    step = pl.program_id(0)
    rows = lax.broadcasted_iota(jnp.int32, gain_m.shape, 0) == where[0]
    g_m = jnp.sum(jnp.where(rows, gain_m[...].astype(F32), 0.0), axis=0, keepdims=True)
    g_t = jnp.sum(jnp.where(rows, gain_t[...].astype(F32), 0.0), axis=0, keepdims=True)
    h_m = mine_in[...].astype(F32)
    h_t = theirs_in[...].astype(F32)
    mine[0] = (h_m * g_m).astype(BF16)
    theirs[0] = (h_t * g_t).astype(BF16)
    gain_out[0] = g_m
    part = jnp.sum(h_m * h_m + h_t * h_t, axis=1, keepdims=True)

    @pl.when(step == 0)
    def _():
        total[...] = jnp.broadcast_to(part, total.shape)

    @pl.when(step > 0)
    def _():
        total[...] += jnp.broadcast_to(part, total.shape)

    @pl.when(step == pl.num_programs(0) - 1)
    def _():
        inverse[...] = lax.rsqrt(total[...] / width + EPS)


def prep(where, hidden, gain_table, chips, rows):
    tokens, width = hidden.shape
    layers = gain_table.shape[0]
    mine = lambda r, where: (0, where[1 + r])
    theirs = lambda r, where: (0, where[1 + chips + r])
    return pl.pallas_call(
        functools.partial(prep_kernel, width=width),
        grid_spec=pltpu.PrefetchScalarGridSpec(
            num_scalar_prefetch=1,
            grid=(chips,),
            in_specs=[
                pl.BlockSpec((tokens, rows), mine),
                pl.BlockSpec((tokens, rows), theirs),
                pl.BlockSpec((layers, rows), mine),
                pl.BlockSpec((layers, rows), theirs),
            ],
            out_specs=[
                pl.BlockSpec((1, tokens, rows), lambda r, where: (r, 0, 0)),
                pl.BlockSpec((1, tokens, rows), lambda r, where: (r, 0, 0)),
                pl.BlockSpec((1, 1, rows), lambda r, where: (r, 0, 0)),
                pl.BlockSpec((tokens, HD), lambda r, where: (0, 0)),
            ],
            scratch_shapes=[pltpu.VMEM((tokens, HD), F32)],
        ),
        out_shape=[
            sds((chips, tokens, rows), BF16),
            sds((chips, tokens, rows), BF16),
            sds((chips, 1, rows), F32),
            sds((tokens, HD), F32),
        ],
        compiler_params=params(),
        name="prep",
    )(where, hidden, hidden, gain_table, gain_table)


def stacked(ref):
    return jnp.concatenate([ref[:, h * HD : (h + 1) * HD] for h in range(SHARE)], axis=0)


def probs_kernel(q_ref, k_ref, d_ref, cosine, sine, inverse, probs, q_out, k_out, vgs):
    cos, sin = cosine[...], sine[...]
    tokens = k_ref.shape[0]
    k_rot = turn(k_ref[...].astype(F32), cos, sin).astype(BF16)
    q_rot = jnp.concatenate(
        [turn(q_ref[:, h * HD : (h + 1) * HD].astype(F32), cos, sin).astype(BF16) for h in range(SHARE)],
        axis=0,
    )
    q_out[0] = q_rot
    k_out[0] = k_rot
    scores = mm(k_rot, q_rot, (1, 1)) * (HD**-0.5)
    key_at = lax.broadcasted_iota(jnp.int32, (tokens, tokens), 0)
    query_at = lax.broadcasted_iota(jnp.int32, (tokens, tokens), 1)
    seen = key_at <= query_at
    lows = []
    for h in range(SHARE):
        s = jnp.where(seen, scores[:, h * tokens : (h + 1) * tokens], -1e30)
        e = jnp.exp(s - jnp.max(s, axis=0, keepdims=True))
        p = e / jnp.sum(e, axis=0, keepdims=True)
        probs[0, :, h * tokens : (h + 1) * tokens] = p
        lows.append(p.astype(BF16))
    grad = mm(jnp.concatenate(lows, axis=1), stacked(d_ref), (1, 0))
    vgs[...] = (grad * inverse[...]).astype(BF16)


def attention_probs(queries, keys, out_grad, cosine, sine, inverse):
    tokens = queries.shape[0]
    group = pl.BlockSpec((tokens, SHARE * HD), lambda g: (0, g))
    head = pl.BlockSpec((tokens, HD), lambda g: (0, g))
    table = pl.BlockSpec((tokens, HD), lambda g: (0, 0))
    return pl.pallas_call(
        probs_kernel,
        grid=(HK,),
        in_specs=[group, head, group, table, table, table],
        out_specs=[
            pl.BlockSpec((1, tokens, SHARE * tokens), lambda g: (g, 0, 0)),
            pl.BlockSpec((1, SHARE * tokens, HD), lambda g: (g, 0, 0)),
            pl.BlockSpec((1, tokens, HD), lambda g: (g, 0, 0)),
            head,
        ],
        out_shape=[
            sds((HK, tokens, SHARE * tokens), F32),
            sds((HK, SHARE * tokens, HD), BF16),
            sds((HK, tokens, HD), BF16),
            sds((tokens, HK * HD), BF16),
        ],
        compiler_params=params(),
        name="probs",
    )(queries, keys, out_grad, cosine, sine, inverse)


def back_kernel(probs, q_rot, k_rot, d_ref, u_one, u_two, cosine, sine, inverse, dq, dk):
    cos, sin = cosine[...], sine[...]
    tokens = k_rot.shape[1]
    values = ((u_one[...] + u_two[...]) * inverse[...]).astype(BF16)
    d_probs = mm(values, stacked(d_ref), (1, 1))
    p = probs[0]
    delta = jnp.sum(p.astype(BF16).astype(F32) * d_probs, axis=0, keepdims=True)
    d_scores = (p * (d_probs - delta) * (HD**-0.5)).astype(BF16)
    dk[...] = turn_back(mm(d_scores, q_rot[0], (1, 0)), cos, sin).astype(BF16)
    key = k_rot[0]
    for h in range(SHARE):
        part = mm(d_scores[:, h * tokens : (h + 1) * tokens], key, (0, 0))
        dq[:, h * HD : (h + 1) * HD] = turn_back(part, cos, sin).astype(BF16)


def attention_back(probs, q_rot, k_rot, out_grad, u_one, u_two, cosine, sine, inverse):
    tokens = out_grad.shape[0]
    group = pl.BlockSpec((tokens, SHARE * HD), lambda g: (0, g))
    head = pl.BlockSpec((tokens, HD), lambda g: (0, g))
    table = pl.BlockSpec((tokens, HD), lambda g: (0, 0))
    return pl.pallas_call(
        back_kernel,
        grid=(HK,),
        in_specs=[
            pl.BlockSpec((1, tokens, SHARE * tokens), lambda g: (g, 0, 0)),
            pl.BlockSpec((1, SHARE * tokens, HD), lambda g: (g, 0, 0)),
            pl.BlockSpec((1, tokens, HD), lambda g: (g, 0, 0)),
            group,
            head,
            head,
            table,
            table,
            table,
        ],
        out_specs=[group, head],
        out_shape=[sds((tokens, HQ * HD), BF16), sds((tokens, HK * HD), BF16)],
        compiler_params=params(),
        name="back",
    )(probs, q_rot, k_rot, out_grad, u_one, u_two, cosine, sine, inverse)


def values_kernel(*refs, blocks, last):
    mine, theirs = refs[0], refs[1]
    weights = refs[2 : 2 + len(blocks)]
    rest = refs[2 + len(blocks) :]
    tokens = mine.shape[1]
    acc = None
    for r, w in zip(blocks, weights, strict=True):
        left = jnp.concatenate([mine[r], theirs[r]], axis=0)
        part = mm(left, w[...], (1, 0))
        acc = part if acc is None else acc + part
    if not last:
        rest[0][...] = acc
        return
    before, vgs_m, vgs_t, u_mine, u_theirs, dots = rest
    acc = acc + before[...]
    u_mine[...] = acc[:tokens]
    u_theirs[...] = acc[tokens:]
    dot_m = jnp.sum(acc[:tokens] * vgs_m[...].astype(F32), axis=1, keepdims=True)
    dot_t = jnp.sum(acc[tokens:] * vgs_t[...].astype(F32), axis=1, keepdims=True)
    dots[:tokens, :] = jnp.broadcast_to(dot_m, (tokens, HD))
    dots[tokens:, :] = jnp.broadcast_to(dot_t, (tokens, HD))


def values_some(mine, theirs, blocks, weights):
    tokens, wide = mine.shape[1], weights[0].shape[1]
    return pl.pallas_call(
        functools.partial(values_kernel, blocks=blocks, last=False),
        out_shape=sds((2 * tokens, wide), F32),
        compiler_params=params(),
        name="values_some",
    )(mine, theirs, *weights)


def values_last(mine, theirs, blocks, weights, before, vgs_m, vgs_t):
    tokens, wide = mine.shape[1], weights[0].shape[1]
    return pl.pallas_call(
        functools.partial(values_kernel, blocks=blocks, last=True),
        out_shape=[sds((tokens, wide), F32), sds((tokens, wide), F32), sds((2 * tokens, HD), F32)],
        compiler_params=params(),
        name="values_last",
    )(mine, theirs, *weights, before, vgs_m, vgs_t)


def local_kernel(*refs, blocks, width):
    (mine, theirs, vgs_m, vgs_t, gain, inv_m, inv_t, own, got) = refs[:9]
    weights = refs[9 : 9 + len(blocks)]
    out_m, out_t = refs[9 + len(blocks) :]
    tokens, rows = mine.shape[1:]
    c_m = inv_m[...] * inv_m[...] * (own[:tokens, :] + got[tokens:, :]) / width
    c_t = inv_t[...] * inv_t[...] * (own[tokens:, :] + got[:tokens, :]) / width
    c_m = jnp.concatenate([c_m] * (rows // HD), axis=1)
    c_t = jnp.concatenate([c_t] * (rows // HD), axis=1)
    left = jnp.concatenate([vgs_m[...], vgs_t[...]], axis=0)
    for i, (r, w) in enumerate(zip(blocks, weights, strict=True)):
        g = gain[r]
        over = 1.0 / g
        part = mm(left, w[...], (1, 1))
        out_m[:, i * rows : (i + 1) * rows] = (part[:tokens] * g - mine[r].astype(F32) * over * c_m).astype(BF16)
        out_t[:, i * rows : (i + 1) * rows] = (part[tokens:] * g - theirs[r].astype(F32) * over * c_t).astype(BF16)


def local_grads(mine, theirs, vgs_m, vgs_t, gain, inv_m, inv_t, own, got, blocks, weights, width):
    tokens, rows = mine.shape[1:]
    out = sds((tokens, len(blocks) * rows), BF16)
    return pl.pallas_call(
        functools.partial(local_kernel, blocks=blocks, width=width),
        out_shape=[out, out],
        compiler_params=params(),
        name="local_grad",
    )(mine, theirs, vgs_m, vgs_t, gain, inv_m, inv_t, own, got, *weights)


def weight_kernel(*refs, ahead, behind, step, steps):
    mine, theirs, vgs_m, vgs_t = refs[:4]
    right = jnp.concatenate([vgs_m[...], vgs_t[...]], axis=0)
    rows = mine.shape[2]
    half = rows // 2

    def part(r):
        return mm(jnp.concatenate([mine[r], theirs[r]], axis=0), right, (0, 0))

    if step == 0:
        both = part(ahead)
        refs[4][...] = both[:half].astype(BF16)
        refs[5][...] = both[half:].astype(BF16)
        return
    from_f, from_b = refs[4][...].astype(F32), refs[5][...].astype(F32)
    if step == steps:
        total = part(0)
        if steps > 1:
            total = total + from_f + from_b
        else:
            total = total + jnp.concatenate([from_f, from_b], axis=0)
        refs[6][...] = total.astype(BF16)
        return
    f, b = part(ahead), part(behind)
    if step == 1:
        f = jnp.concatenate([f[:half] + from_f, f[half:]], axis=0)
        b = jnp.concatenate([b[:half], b[half:] + from_b], axis=0)
    else:
        f, b = f + from_f, b + from_b
    refs[6][...] = f.astype(BF16)
    refs[7][...] = b.astype(BF16)


def weight_step(mine, theirs, vgs_m, vgs_t, arrived, step, steps):
    chips, _, rows = mine.shape
    wide = vgs_m.shape[1]
    if step == 0:
        out = [sds((rows // 2, wide), BF16)] * 2
    elif step == steps:
        out = sds((rows, wide), BF16)
    else:
        out = [sds((rows, wide), BF16)] * 2
    return pl.pallas_call(
        functools.partial(
            weight_kernel, ahead=steps - step, behind=chips - steps + step, step=step, steps=steps
        ),
        out_shape=out,
        compiler_params=params(),
        name="weight_step",
    )(mine, theirs, vgs_m, vgs_t, *arrived)


def join_kernel(where, *refs, blocks, rows):
    pieces, out, sem = refs[:-2], refs[-2], refs[-1]
    copies = []
    chips = sum(len(b) for b in blocks)
    for i, held in enumerate(blocks):
        for side in range(2):
            for j, r in enumerate(held):
                column = pl.multiple_of(where[1 + side * chips + r] * rows, rows)
                copies.append(
                    pltpu.make_async_copy(
                        pieces[2 * i + side].at[:, j * rows : (j + 1) * rows],
                        out.at[:, pl.ds(column, rows)],
                        sem.at[len(copies)],
                    )
                )
    for copy in copies:
        copy.start()
    for copy in copies:
        copy.wait()


def join(where, pieces, blocks, rows, tokens, width):
    return pl.pallas_call(
        functools.partial(join_kernel, blocks=blocks, rows=rows),
        in_specs=[pl.BlockSpec(memory_space=pltpu.SMEM)] + [pl.BlockSpec(memory_space=pl.ANY)] * len(pieces),
        out_specs=pl.BlockSpec(memory_space=pl.ANY),
        out_shape=sds((tokens, width), BF16),
        scratch_shapes=[pltpu.SemaphoreType.DMA((width // rows,))],
        compiler_params=params(),
        name="join",
    )(where, *pieces)


def last_layer(layer_counts, layers):
    sections, mine = lax.axis_size("section"), lax.axis_index("section")
    own = layer_counts[0]
    total = own
    if sections > 2:
        reach = 1
        while reach < sections:
            route = [(i, i + reach) for i in range(sections - reach)]
            total = total + lax.ppermute(total, "section", route)
            reach *= 2
    return jnp.where(mine == sections - 1, layers, total) - 1


def shards(hidden, gain_table, layer_counts, positions, queries, keys, value_weight, out_grad):
    tokens_in, weight = hidden[0], value_weight[0]
    tokens, width = tokens_in.shape
    rows = weight.shape[0]
    sections = lax.axis_size("section")
    devices = lax.axis_size("dp")
    chips = devices // 2
    ring = list(range(0, chips, 2)) + list(range(1, chips, 2))[::-1]
    place_of = [ring.index(c) for c in range(chips)]
    me = lax.axis_index("dp")
    chip, core = me // 2, me % 2
    place = jnp.asarray(place_of, jnp.int32)[chip]
    around = jnp.asarray(ring + ring, jnp.int32)
    order = lax.dynamic_slice(around, (place,), (chips,)) * 2

    def hop(d, by):
        return 2 * ring[(place_of[d // 2] + by) % chips] + d % 2

    forth = [(d, hop(d, 1)) for d in range(devices)]
    back = [(d, hop(d, -1)) for d in range(devices)]
    swap = [(d, d ^ 1) for d in range(devices)]
    down = [(s * devices + d, (s - 1) * devices + d) for s in range(1, sections) for d in range(devices)]
    cross = [(s * devices + d, (s - 1) * devices + (d ^ 1)) for s in range(1, sections) for d in range(devices)]

    last = last_layer(layer_counts, gain_table.shape[0])
    where = jnp.concatenate([last[None], order + core, order + 1 - core]).astype(jnp.int32)
    mine, send, gain, inverse = prep(where, tokens_in, gain_table, chips, rows)
    theirs = lax.ppermute(send, "dp", swap)
    inverse_t = lax.ppermute(inverse, "dp", swap)
    cosine, sine = rope_tables(positions[0])
    probs, q_rot, k_rot, vgs = attention_probs(queries[0], keys[0], out_grad[0], cosine, sine, inverse)
    vgs_t = lax.ppermute(vgs, "dp", swap)

    held = {0: weight}
    half = chips // 2
    f = b = weight
    for step in range(1, half):
        f = lax.ppermute(f, "dp", forth)
        b = lax.ppermute(b, "dp", back)
        held[chips - step] = f
        held[step] = b
    top = lax.ppermute(f[: rows // 2], "dp", forth)
    bottom = lax.ppermute(b[rows // 2 :], "dp", back)
    early = [r for r in range(chips) if r != half]
    part = values_some(mine, theirs, early, [held[r] for r in early])
    held[half] = jnp.concatenate([top, bottom], axis=0)
    u_mine, u_send, dots = values_last(mine, theirs, [half], [held[half]], part, vgs, vgs_t)
    u_got = lax.ppermute(u_send, "dp", swap)
    dots_got = lax.ppermute(dots, "dp", swap)

    pieces, blocks = [], []
    for at in range(0, chips, 2):
        some = [at, at + 1]
        out_m, out_t = local_grads(
            mine, theirs, vgs, vgs_t, gain, inverse, inverse_t, dots, dots_got, some, [held[r] for r in some], width
        )
        pieces += [lax.ppermute(out_m, ("section", "dp"), down), lax.ppermute(out_t, ("section", "dp"), cross)]
        blocks.append(some)
    upstream = join(where, pieces, blocks, rows, tokens, width)

    vgs_ring, _ = lax.optimization_barrier((vgs, dots))
    arrived = []
    for step in range(half):
        f, b = weight_step(mine, theirs, vgs_ring, vgs_t, arrived, step, half)
        arrived = [lax.ppermute(f, "dp", forth), lax.ppermute(b, "dp", back)]
    weight_grad = weight_step(mine, theirs, vgs_ring, vgs_t, arrived, half, half)

    query_grad, key_grad = attention_back(
        probs, q_rot, k_rot, out_grad[0], u_mine, u_got, cosine, sine, inverse
    )
    return (query_grad[None], key_grad[None], weight_grad[None], upstream[None])


def solution(mesh):
    split = P("section", "dp", None)
    in_specs = (split, P(), P("section"), P("section", "dp"), split, split, split, split)
    out_specs = (split,) * 4
    return jax.shard_map(shards, mesh=mesh, in_specs=in_specs, out_specs=out_specs, check_vma=False)
```

time: 215 us -> 135 us (0.63)
  waiting for transfers between devices: 146 us -> 77.2 us
  starting transfers between devices: 1.54 us -> 28.6 us
  matrix products: 25.8 us -> 0 us
  Pallas kernels: 0 us -> 18.1 us
  between operations: 15 us -> 3.61 us
  local copies, waits for them, and re-layouts: 13.9 us -> 6.09 us
  other arithmetic: 6.78 us -> 1.24 us
  blocking collectives: 5.19 us -> 0 us
    all_gather x1 -> x0, waiting for transfers between devices: 61.1 us -> none  [shards(): lax.all_gather(weight, 'dp', axis=0, tiled=True)]
    reduce_scatter x1 -> x0, waiting for transfers between devices: 40.7 us -> none  [shards(): lax.psum_scatter(jnp.einsum('td,te->de', columns, values_grad, preferred_...]
    ppermute x1 -> x29, waiting for transfers between devices: 43.9 us -> 77.2 us  [the longest x8 25.1 us: shards(): arrived = [lax.ppermute(f, 'dp', forth), lax.ppermute(b, 'dp', back)]]
    ppermute x1 -> x29, starting transfers between devices: 1.46 us -> 28.6 us  [the longest x8 8.3 us: shards(): arrived = [lax.ppermute(f, 'dp', forth), lax.ppermute(b, 'dp', back)]]
    dot_general x8 -> x0, matrix products: 23.6 us -> none  [the longest x1 8.2 us: shards(): jnp.einsum('te,de->td', values_grad, lax.all_gather(weight, 'dp', axis=0,...]
    pallas_call x0 -> x15, Pallas kernels: none -> 18.1 us  [the longest x1 3.5 us: attention_back(): pl.pallas_call(back_kernel, grid=(HK,), in_specs=[pl.BlockSpec((1, tokens...]
    unnamed x21, local copies, waits for them, and re-layouts: 12.2 us -> 4.79 us
    convert_element_type x4 -> x1, other arithmetic: 5.44 us -> 0.01 us  [rope_tables(): angle = places.astype(F32)[:, None] * freq[None, :]]
  transfers between devices with their start and end apart: 3 -> 29, of which waited for: 3 -> 15; matrix products, arithmetic and copies ran while one was open for 14% -> 2% of each run, Pallas kernels for 0% -> 11%
where the time goes in v1:
time: 135 us
  waiting for transfers between devices  77.2 us (57%)
  starting transfers between devices  28.6 us (21%)
  Pallas kernels  18.1 us (13%)
  local copies, waits for them, and re-layouts  6.09 us (5%)
  between operations  3.61 us (3%)
    ppermute x8, waiting for transfers between devices, shards(): arrived = [lax.ppermute(f, 'dp', forth), lax.ppermute(b, 'dp', back)]  25.1 us
    ppermute x3, waiting for transfers between devices, shards(): b = lax.ppermute(b, 'dp', back)  24.3 us
    ppermute x4, waiting for transfers between devices, shards(): lax.ppermute(out_m, ('section', 'dp'), down)  17.8 us
    ppermute x4, waiting for transfers between devices, shards(): lax.ppermute(out_t, ('section', 'dp'), cross)  8.95 us
    ppermute x8, starting transfers between devices, shards(): arrived = [lax.ppermute(f, 'dp', forth), lax.ppermute(b, 'dp', back)]  8.3 us
    ppermute x3, starting transfers between devices, shards(): b = lax.ppermute(b, 'dp', back)  6.06 us
    ppermute x4, starting transfers between devices, shards(): lax.ppermute(out_m, ('section', 'dp'), down)  5.15 us
    ppermute x4, starting transfers between devices, shards(): lax.ppermute(out_t, ('section', 'dp'), cross)  5.15 us
  transfers between devices with their start and end apart: 29, of which 15 were waited for; matrix products, arithmetic and copies ran while one was open for 2% of the time, Pallas kernels for 11%

profile of v1, /device:TPU:0, one launch (start us, length us, event | category | flops | bytes accessed | tf_op | source)
XLA Modules:
  0.0 134.7 jit_solution(9221911302067488303)
XLA Ops:
  0.6 3.0 %collective-permute-start.5 = (bf16[512,512]{1,0:T(8,128)(2,1)}, bf16[512,512]{1,0:T(8,128)(2,1)S(1)}, u32[]{:S(2)}, u32[]{:S(2)}) collective-permute-start(bf16[512,512]{1,0:T(8,128)(2,1)} %bitcast.19), channel_id=1, source_target_pairs={{0,2},{1,3},{2,6},{3,7},{4,0},{5,1},{6,10},{7,11},{8,4},{9,5},{10,... | collective-permute-start | bytes 1572872 | tf_op jit(solution)/shard_map/ppermute | solution.py:414
  3.8 12.1 %collective-permute-done.5.refs_3_.refs_10_ = bf16[512,512]{1,0:T(8,128)(2,1)S(1)} collective-permute-done((bf16[512,512]{1,0:T(8,128)(2,1)}, bf16[512,512]{1,0:T(8,128)(2,1)S(1)}, u32[]{:S(2)}, u32[]{:S(2)}) %collective-permute-start.5) | collective-permute-done | bytes 524320 | tf_op jit(solution)/shard_map/ppermute | solution.py:414
  15.8 1.7 %collective-permute-start.6 = (bf16[512,512]{1,0:T(8,128)(2,1)S(1)}, bf16[512,512]{1,0:T(8,128)(2,1)S(1)}, u32[]{:S(2)}, u32[]{:S(2)}) collective-permute-start(bf16[512,512]{1,0:T(8,128)(2,1)S(1)} %collective-permute-done.5.refs_3_.refs_10_), channel_id=1, source_target_pairs={{0,2},{1,3},{2,6},{3,7},{4,0},{5,1},{6,10},{7,11},{8,4},{9,5},{10,... | collective-permute-start | bytes 1572872 | tf_op jit(solution)/shard_map/ppermute | solution.py:414
  18.5 1.2 dynamic_slice.6
  21.7 0.7 broadcast_add_fusion
  22.5 1.6 %copy-done.3 = bf16[1,128,8192]{2,1,0:T(8,128)(2,1)S(1)} copy-done((bf16[1,128,8192]{2,1,0:T(8,128)(2,1)S(1)}, bf16[1,128,8192]{2,1,0:T(8,128)(2,1)}, u32[]{:S(2)}) %copy-start.3) | copy-done | bytes 2097176
  24.1 0.9 copy-done.6
  25.1 2.3 %prep.1 = (bf16[8,128,512]{2,1,0:T(8,128)(2,1)S(1)}, bf16[8,128,512]{2,1,0:T(8,128)(2,1)S(1)}, f32[8,1,512]{2,1,0:T(1,128)S(1)}, f32[128,128]{1,0:T(8,128)S(1)}) custom-call(s32[17]{0:T(128)S(1)} %pad_add_fusion.where, bf16[128,8192]{1,0:T(8,128)(2,1)S(1)} %bitcast.15, bf16[128,8192]{1,0:T(8,128)(2,1)S(1)} %bitcast.16, bf16[10,8192]{1,0:T(8,128)(2,1)S(1)} %copy-done.6, ...), custom_call_target="tpu_custom_call" | custom-call | tf_op jit(solution)/shard_map/prep/pallas_call | solution.py:80
  27.5 1.4 %collective-permute-done.6.refs_4_.refs_9_ = bf16[512,512]{1,0:T(8,128)(2,1)S(1)} collective-permute-done((bf16[512,512]{1,0:T(8,128)(2,1)S(1)}, bf16[512,512]{1,0:T(8,128)(2,1)S(1)}, u32[]{:S(2)}, u32[]{:S(2)}) %collective-permute-start.6) | collective-permute-done | bytes 524320 | tf_op jit(solution)/shard_map/ppermute | solution.py:414
  29.0 1.4 %collective-permute-start.7 = (bf16[512,512]{1,0:T(8,128)(2,1)S(1)}, bf16[512,512]{1,0:T(8,128)(2,1)S(1)}, u32[]{:S(2)}, u32[]{:S(2)}) collective-permute-start(bf16[512,512]{1,0:T(8,128)(2,1)S(1)} %collective-permute-done.6.refs_4_.refs_9_), channel_id=1, source_target_pairs={{0,2},{1,3},{2,6},{3,7},{4,0},{5,1},{6,10},{7,11},{8,4},{9,5},{10,... | collective-permute-start | bytes 1572872 | tf_op jit(solution)/shard_map/ppermute | solution.py:414
  30.3 0.7 collective-permute-start.3
  31.0 10.9 %collective-permute-done.7.refs_5_.refs_10_ = bf16[512,512]{1,0:T(8,128)(2,1)S(1)} collective-permute-done((bf16[512,512]{1,0:T(8,128)(2,1)S(1)}, bf16[512,512]{1,0:T(8,128)(2,1)S(1)}, u32[]{:S(2)}, u32[]{:S(2)}) %collective-permute-start.7) | collective-permute-done | bytes 524320 | tf_op jit(solution)/shard_map/ppermute | solution.py:414
  41.9 1.7 %collective-permute-start.8 = (bf16[256,512]{1,0:T(8,128)(2,1)S(1)}, bf16[256,512]{1,0:T(8,128)(2,1)S(1)}, u32[]{:S(2)}, u32[]{:S(2)}) collective-permute-start(bf16[256,512]{1,0:T(8,128)(2,1)S(1)} %slice.9), channel_id=1, source_target_pairs={{0,2},{1,3},{2,6},{3,7},{4,0},{5,1},{6,10},{7,11},{8,4},{9,5},{10,... | collective-permute-start | bytes 786440 | tf_op jit(solution)/shard_map/ppermute | solution.py:418
  44.5 2.7 %probs.1 = (f32[4,128,1024]{2,1,0:T(8,128)S(1)}, bf16[4,1024,128]{2,1,0:T(8,128)(2,1)S(1)}, bf16[4,128,128]{2,1,0:T(8,128)(2,1)S(1)}, bf16[128,512]{1,0:T(8,128)(2,1)S(1)}) custom-call(bf16[128,4096]{1,0:T(8,128)(2,1)S(1)} %bitcast.23, bf16[128,512]{1,0:T(8,128)(2,1)S(1)} %bitcast.24, bf16[128,4096]{1,0:T(8,128)(2,1)S(1)} %bitcast.17, ...), custom_call_target="tpu_custom_call" | custom-call | tf_op jit(solution)/shard_map/probs/pallas_call | solution.py:144
  47.3 1.0 copy-done
  48.3 2.3 %values_some.1.refs_3_ = f32[256,512]{1,0:T(8,128)S(1)} custom-call(bf16[8,128,512]{2,1,0:T(8,128)(2,1)S(1)} %get-tuple-element.38.refs_0_, bf16[8,128,512]{2,1,0:T(8,128)(2,1)} %copy-done, bf16[512,512]{1,0:T(8,128)(2,1)S(1)} %bitcast.21, bf16[512,512]{1,0:T(8,128)(2,1)S(1)} %collective-permute-done.5.refs_3_.refs_10_, ...), custom_call_target="tpu_custom_call" | custom-call | tf_op jit(solution)/shard_map/values_some/pallas_call | solution.py:231
  50.8 1.2 copy-done.1
  52.7 1.8 %collective-permute-start.11 = (bf16[256,512]{1,0:T(8,128)(2,1)S(1)}, bf16[256,512]{1,0:T(8,128)(2,1)S(1)}, u32[]{:S(2)}, u32[]{:S(2)}) collective-permute-start(bf16[256,512]{1,0:T(8,128)(2,1)S(1)} %get-tuple-element.47), channel_id=1, source_target_pairs={{0,4},{1,5},{2,0},{3,1},{4,8},{5,9},{6,2},{7,3},{8,12},{9,13},{10,... | collective-permute-start | bytes 786440 | tf_op jit(solution)/shard_map/ppermute | solution.py:440
  54.8 6.7 %collective-permute-done.11.refs_4_ = bf16[256,512]{1,0:T(8,128)(2,1)S(1)} collective-permute-done((bf16[256,512]{1,0:T(8,128)(2,1)S(1)}, bf16[256,512]{1,0:T(8,128)(2,1)S(1)}, u32[]{:S(2)}, u32[]{:S(2)}) %collective-permute-start.11) | collective-permute-done | bytes 262176 | tf_op jit(solution)/shard_map/ppermute | solution.py:440
  61.4 1.5 %collective-permute-done.12.refs_5_ = bf16[256,512]{1,0:T(8,128)(2,1)S(1)} collective-permute-done((bf16[256,512]{1,0:T(8,128)(2,1)S(1)}, bf16[256,512]{1,0:T(8,128)(2,1)S(1)}, u32[]{:S(2)}, u32[]{:S(2)}) %collective-permute-start.12) | collective-permute-done | bytes 262176 | tf_op jit(solution)/shard_map/ppermute | solution.py:440
  63.4 1.6 %collective-permute-start.13 = (bf16[512,512]{1,0:T(8,128)(2,1)S(1)}, bf16[512,512]{1,0:T(8,128)(2,1)S(1)}, u32[]{:S(2)}, u32[]{:S(2)}) collective-permute-start(bf16[512,512]{1,0:T(8,128)(2,1)S(1)} %get-tuple-element.49), channel_id=1, source_target_pairs={{0,4},{1,5},{2,0},{3,1},{4,8},{5,9},{6,2},{7,3},{8,12},{9,13},{10,... | collective-permute-start | bytes 1572872 | tf_op jit(solution)/shard_map/ppermute | solution.py:440
  65.4 11.2 %collective-permute-done.13.refs_4_ = bf16[512,512]{1,0:T(8,128)(2,1)S(1)} collective-permute-done((bf16[512,512]{1,0:T(8,128)(2,1)S(1)}, bf16[512,512]{1,0:T(8,128)(2,1)S(1)}, u32[]{:S(2)}, u32[]{:S(2)}) %collective-permute-start.13) | collective-permute-done | bytes 524320 | tf_op jit(solution)/shard_map/ppermute | solution.py:440
  76.6 1.3 collective-permute-done.14.refs_5_
  78.4 1.6 %collective-permute-start.15 = (bf16[512,512]{1,0:T(8,128)(2,1)S(1)}, bf16[512,512]{1,0:T(8,128)(2,1)S(1)}, u32[]{:S(2)}, u32[]{:S(2)}) collective-permute-start(bf16[512,512]{1,0:T(8,128)(2,1)S(1)} %get-tuple-element.51), channel_id=1, source_target_pairs={{0,4},{1,5},{2,0},{3,1},{4,8},{5,9},{6,2},{7,3},{8,12},{9,13},{10,... | collective-permute-start | bytes 1572872 | tf_op jit(solution)/shard_map/ppermute | solution.py:440
  80.5 0.5 collective-permute-start.19
  81.0 0.9 collective-permute-done.19.refs_6_
  81.9 0.5 local_grad.7
  82.4 1.3 collective-permute-start.27
  83.7 1.3 collective-permute-start.28
  85.0 0.5 local_grad.6
  85.5 0.5 local_grad.5
  86.0 4.5 %collective-permute-done.15.refs_4_ = bf16[512,512]{1,0:T(8,128)(2,1)S(1)} collective-permute-done((bf16[512,512]{1,0:T(8,128)(2,1)S(1)}, bf16[512,512]{1,0:T(8,128)(2,1)S(1)}, u32[]{:S(2)}, u32[]{:S(2)}) %collective-permute-start.15) | collective-permute-done | bytes 524320 | tf_op jit(solution)/shard_map/ppermute | solution.py:440
  90.5 1.3 collective-permute-start.25
  91.8 1.3 collective-permute-start.26
  93.6 1.3 collective-permute-start.23
  94.9 1.6 %collective-permute-start.17 = (bf16[512,512]{1,0:T(8,128)(2,1)S(1)}, bf16[512,512]{1,0:T(8,128)(2,1)S(1)}, u32[]{:S(2)}, u32[]{:S(2)}) collective-permute-start(bf16[512,512]{1,0:T(8,128)(2,1)S(1)} %get-tuple-element.53), channel_id=1, source_target_pairs={{0,4},{1,5},{2,0},{3,1},{4,8},{5,9},{6,2},{7,3},{8,12},{9,13},{10,... | collective-permute-start | bytes 1572872 | tf_op jit(solution)/shard_map/ppermute | solution.py:440
  96.5 1.4 %collective-permute-done.28.refs_7_ = bf16[128,1024]{1,0:T(8,128)(2,1)S(1)} collective-permute-done((bf16[128,1024]{1,0:T(8,128)(2,1)S(1)}, bf16[128,1024]{1,0:T(8,128)(2,1)S(1)}, u32[]{:S(2)}, u32[]{:S(2)}) %collective-permute-start.28) | collective-permute-done | bytes 262176 | tf_op jit(solution)/shard_map/ppermute | solution.py:432
  98.8 5.9 %collective-permute-done.25.refs_4_ = bf16[128,1024]{1,0:T(8,128)(2,1)S(1)} collective-permute-done((bf16[128,1024]{1,0:T(8,128)(2,1)S(1)}, bf16[128,1024]{1,0:T(8,128)(2,1)S(1)}, u32[]{:S(2)}, u32[]{:S(2)}) %collective-permute-start.25) | collective-permute-done | bytes 262176 | tf_op jit(solution)/shard_map/ppermute | solution.py:432
  104.7 1.3 collective-permute-start.24
  106.0 3.1 %collective-permute-done.26.refs_5_ = bf16[128,1024]{1,0:T(8,128)(2,1)S(1)} collective-permute-done((bf16[128,1024]{1,0:T(8,128)(2,1)S(1)}, bf16[128,1024]{1,0:T(8,128)(2,1)S(1)}, u32[]{:S(2)}, u32[]{:S(2)}) %collective-permute-start.26) | collective-permute-done | bytes 262176 | tf_op jit(solution)/shard_map/ppermute | solution.py:432
  109.1 1.3 collective-permute-start.21
  110.4 5.5 %collective-permute-done.23.refs_2_ = bf16[128,1024]{1,0:T(8,128)(2,1)S(1)} collective-permute-done((bf16[128,1024]{1,0:T(8,128)(2,1)S(1)}, bf16[128,1024]{1,0:T(8,128)(2,1)S(1)}, u32[]{:S(2)}, u32[]{:S(2)}) %collective-permute-start.23) | collective-permute-done | bytes 262176 | tf_op jit(solution)/shard_map/ppermute | solution.py:432
  115.9 1.3 collective-permute-start.22
  117.2 3.5 %back.1 = (bf16[128,4096]{1,0:T(8,128)(2,1)}, bf16[128,512]{1,0:T(8,128)(2,1)}) custom-call(f32[4,128,1024]{2,1,0:T(8,128)S(1)} %get-tuple-element.35.probs, bf16[4,1024,128]{2,1,0:T(8,128)(2,1)S(1)} %get-tuple-element.36.q_rot, bf16[4,128,128]{2,1,0:T(8,128)(2,1)S(1)} %get-tuple-element.37.k_rot, bf16[128,4096]{1,0:T(8,128)(2,1)S(1)} %bitcast.18, ...), custom_call_target="tpu_custom_call" | custom-call | tf_op jit(solution)/shard_map/back/pallas_call | solution.py:185
  120.7 6.4 %collective-permute-done.21.refs_0_ = bf16[128,1024]{1,0:T(8,128)(2,1)S(1)} collective-permute-done((bf16[128,1024]{1,0:T(8,128)(2,1)S(1)}, bf16[128,1024]{1,0:T(8,128)(2,1)S(1)}, u32[]{:S(2)}, u32[]{:S(2)}) %collective-permute-start.21) | collective-permute-done | bytes 262176 | tf_op jit(solution)/shard_map/ppermute | solution.py:432
  127.1 4.4 %collective-permute-done.22.refs_1_ = bf16[128,1024]{1,0:T(8,128)(2,1)S(1)} collective-permute-done((bf16[128,1024]{1,0:T(8,128)(2,1)S(1)}, bf16[128,1024]{1,0:T(8,128)(2,1)S(1)}, u32[]{:S(2)}, u32[]{:S(2)}) %collective-permute-start.22) | collective-permute-done | bytes 262176 | tf_op jit(solution)/shard_map/ppermute | solution.py:432
  131.6 2.0 %join.1 = bf16[128,8192]{1,0:T(8,128)(2,1)} custom-call(s32[17]{0:T(128)S(1)} %pad_add_fusion.where, bf16[128,1024]{1,0:T(8,128)(2,1)S(1)} %collective-permute-done.21.refs_0_, bf16[128,1024]{1,0:T(8,128)(2,1)S(1)} %collective-permute-done.22.refs_1_, bf16[128,1024]{1,0:T(8,128)(2,1)S(1)} %collective-permute-done.23.refs_2_, ...), custom_call_target="tpu_custom_call" | custom-call | tf_op jit(solution)/shard_map/join/pallas_call | solution.py:352
  133.6 1.1 weight_step.9
  (56 shorter events, 5.9 us)
Async XLA Ops:
  0.6 15.2 %collective-permute-start.5 = (bf16[512,512]{1,0:T(8,128)(2,1)}, bf16[512,512]{1,0:T(8,128)(2,1)S(1)}, u32[]{:S(2)}, u32[]{:S(2)}) collective-permute-start(bf16[512,512]{1,0:T(8,128)(2,1)} %bitcast.19), channel_id=1, source_target_pairs={{0,2},{1,3},{2,6},{3,7},{4,0},{5,1},{6,10},{7,11},{8,4},{9,5},{10,... | collective-permute-start | bytes 1572872 | tf_op jit(solution)/shard_map/ppermute | solution.py:414
  3.6 13.9 %collective-permute-start.1 = (bf16[512,512]{1,0:T(8,128)(2,1)}, bf16[512,512]{1,0:T(8,128)(2,1)S(1)}, u32[]{:S(2)}, u32[]{:S(2)}) collective-permute-start(bf16[512,512]{1,0:T(8,128)(2,1)} %bitcast.20), channel_id=1, source_target_pairs={{0,4},{1,5},{2,0},{3,1},{4,8},{5,9},{6,2},{7,3},{8,12},{9,13},{10,... | collective-permute-start | bytes 1572872 | tf_op jit(solution)/shard_map/ppermute | solution.py:413
  15.8 13.1 %collective-permute-start.6 = (bf16[512,512]{1,0:T(8,128)(2,1)S(1)}, bf16[512,512]{1,0:T(8,128)(2,1)S(1)}, u32[]{:S(2)}, u32[]{:S(2)}) collective-permute-start(bf16[512,512]{1,0:T(8,128)(2,1)S(1)} %collective-permute-done.5.refs_3_.refs_10_), channel_id=1, source_target_pairs={{0,2},{1,3},{2,6},{3,7},{4,0},{5,1},{6,10},{7,11},{8,4},{9,5},{10,... | collective-permute-start | bytes 1572872 | tf_op jit(solution)/shard_map/ppermute | solution.py:414
  17.5 12.8 %collective-permute-start.2 = (bf16[512,512]{1,0:T(8,128)(2,1)S(1)}, bf16[512,512]{1,0:T(8,128)(2,1)S(1)}, u32[]{:S(2)}, u32[]{:S(2)}) collective-permute-start(bf16[512,512]{1,0:T(8,128)(2,1)S(1)} %collective-permute-done.1.refs_8_.refs_10_), channel_id=1, source_target_pairs={{0,4},{1,5},{2,0},{3,1},{4,8},{5,9},{6,2},{7,3},{8,12},{9,13},{10,... | collective-permute-start | bytes 1572872 | tf_op jit(solution)/shard_map/ppermute | solution.py:413
  22.5 1.6 %copy-start.3 = (bf16[1,128,8192]{2,1,0:T(8,128)(2,1)S(1)}, bf16[1,128,8192]{2,1,0:T(8,128)(2,1)}, u32[]{:S(2)}) copy-start(bf16[1,128,8192]{2,1,0:T(8,128)(2,1)} %param.10) | copy-start | bytes 6291460
  24.1 0.9 copy-start.6
  25.1 5.9 %copy-start.9 = (s32[1,128]{1,0:T(1,128)S(1)}, s32[1,128]{1,0:T(1,128)}, u32[]{:S(2)}) copy-start(s32[1,128]{1,0:T(1,128)} %param.13) | copy-start | bytes 1540
  25.1 19.4 %copy-start.4 = (bf16[1,128,4096]{2,1,0:T(8,128)(2,1)S(1)}, bf16[1,128,4096]{2,1,0:T(8,128)(2,1)}, u32[]{:S(2)}) copy-start(bf16[1,128,4096]{2,1,0:T(8,128)(2,1)} %param.17) | copy-start | bytes 3145732
  25.1 19.4 %copy-start.7 = (bf16[1,128,4096]{2,1,0:T(8,128)(2,1)S(1)}, bf16[1,128,4096]{2,1,0:T(8,128)(2,1)}, u32[]{:S(2)}) copy-start(bf16[1,128,4096]{2,1,0:T(8,128)(2,1)} %param.14) | copy-start | bytes 3145732
  25.1 19.4 %copy-start.8 = (bf16[1,128,512]{2,1,0:T(8,128)(2,1)S(1)}, bf16[1,128,512]{2,1,0:T(8,128)(2,1)}, u32[]{:S(2)}) copy-start(bf16[1,128,512]{2,1,0:T(8,128)(2,1)} %param.15) | copy-start | bytes 393220
  27.4 20.9 %copy-start.5 = (bf16[1,512,512]{2,1,0:T(8,128)(2,1)S(1)}, bf16[1,512,512]{2,1,0:T(8,128)(2,1)}, u32[]{:S(2)}) copy-start(bf16[1,512,512]{2,1,0:T(8,128)(2,1)} %param.16) | copy-start | bytes 1572868
  27.5 19.9 %collective-permute-start = (bf16[8,128,512]{2,1,0:T(8,128)(2,1)S(1)}, bf16[8,128,512]{2,1,0:T(8,128)(2,1)S(1)}, u32[]{:S(2)}, u32[]{:S(2)}) collective-permute-start(bf16[8,128,512]{2,1,0:T(8,128)(2,1)S(1)} %get-tuple-element.39), channel_id=1, source_target_pairs={{0,1},{1,0},{2,3},{3,2},{4,5},{5,4},{6,7},{7,6},{8,9},{9,8},{10,11... | collective-permute-start | bytes 3145736 | tf_op jit(solution)/shard_map/ppermute | solution.py:403
  29.0 12.9 %collective-permute-start.7 = (bf16[512,512]{1,0:T(8,128)(2,1)S(1)}, bf16[512,512]{1,0:T(8,128)(2,1)S(1)}, u32[]{:S(2)}, u32[]{:S(2)}) collective-permute-start(bf16[512,512]{1,0:T(8,128)(2,1)S(1)} %collective-permute-done.6.refs_4_.refs_9_), channel_id=1, source_target_pairs={{0,2},{1,3},{2,6},{3,7},{4,0},{5,1},{6,10},{7,11},{8,4},{9,5},{10,... | collective-permute-start | bytes 1572872 | tf_op jit(solution)/shard_map/ppermute | solution.py:414
  30.3 13.3 %collective-permute-start.3 = (bf16[512,512]{1,0:T(8,128)(2,1)S(1)}, bf16[512,512]{1,0:T(8,128)(2,1)S(1)}, u32[]{:S(2)}, u32[]{:S(2)}) collective-permute-start(bf16[512,512]{1,0:T(8,128)(2,1)S(1)} %collective-permute-done.2.refs_7_.refs_9_), channel_id=1, source_target_pairs={{0,4},{1,5},{2,0},{3,1},{4,8},{5,9},{6,2},{7,3},{8,12},{9,13},{10,... | collective-permute-start | bytes 1572872 | tf_op jit(solution)/shard_map/ppermute | solution.py:413
  41.9 8.8 %collective-permute-start.8 = (bf16[256,512]{1,0:T(8,128)(2,1)S(1)}, bf16[256,512]{1,0:T(8,128)(2,1)S(1)}, u32[]{:S(2)}, u32[]{:S(2)}) collective-permute-start(bf16[256,512]{1,0:T(8,128)(2,1)S(1)} %slice.9), channel_id=1, source_target_pairs={{0,2},{1,3},{2,6},{3,7},{4,0},{5,1},{6,10},{7,11},{8,4},{9,5},{10,... | collective-permute-start | bytes 786440 | tf_op jit(solution)/shard_map/ppermute | solution.py:418
  43.6 7.0 %collective-permute-start.4 = (bf16[256,512]{1,0:T(8,128)(2,1)S(1)}, bf16[256,512]{1,0:T(8,128)(2,1)S(1)}, u32[]{:S(2)}, u32[]{:S(2)}) collective-permute-start(bf16[256,512]{1,0:T(8,128)(2,1)S(1)} %slice.8), channel_id=1, source_target_pairs={{0,4},{1,5},{2,0},{3,1},{4,8},{5,9},{6,2},{7,3},{8,12},{9,13},{10,... | collective-permute-start | bytes 786440 | tf_op jit(solution)/shard_map/ppermute | solution.py:417
  47.2 3.5 %collective-permute-start.9 = (bf16[128,512]{1,0:T(8,128)(2,1)S(1)}, bf16[128,512]{1,0:T(8,128)(2,1)S(1)}, u32[]{:S(2)}, u32[]{:S(2)}) collective-permute-start(bf16[128,512]{1,0:T(8,128)(2,1)S(1)} %get-tuple-element.46.refs_4_.refs_2_), channel_id=1, source_target_pairs={{0,1},{1,0},{2,3},{3,2},{4,5},{5,4},{6,7},{7,6},{8,9},{9,8},{10,11... | collective-permute-start | bytes 393224 | tf_op jit(solution)/shard_map/ppermute | solution.py:407
  47.3 1.0 copy-start
  50.7 1.2 copy-start.1
  52.7 8.8 %collective-permute-start.11 = (bf16[256,512]{1,0:T(8,128)(2,1)S(1)}, bf16[256,512]{1,0:T(8,128)(2,1)S(1)}, u32[]{:S(2)}, u32[]{:S(2)}) collective-permute-start(bf16[256,512]{1,0:T(8,128)(2,1)S(1)} %get-tuple-element.47), channel_id=1, source_target_pairs={{0,4},{1,5},{2,0},{3,1},{4,8},{5,9},{6,2},{7,3},{8,12},{9,13},{10,... | collective-permute-start | bytes 786440 | tf_op jit(solution)/shard_map/ppermute | solution.py:440
  54.5 8.4 %collective-permute-start.12 = (bf16[256,512]{1,0:T(8,128)(2,1)S(1)}, bf16[256,512]{1,0:T(8,128)(2,1)S(1)}, u32[]{:S(2)}, u32[]{:S(2)}) collective-permute-start(bf16[256,512]{1,0:T(8,128)(2,1)S(1)} %get-tuple-element.48), channel_id=1, source_target_pairs={{0,2},{1,3},{2,6},{3,7},{4,0},{5,1},{6,10},{7,11},{8,4},{9,5},{10,... | collective-permute-start | bytes 786440 | tf_op jit(solution)/shard_map/ppermute | solution.py:440
  63.4 13.3 %collective-permute-start.13 = (bf16[512,512]{1,0:T(8,128)(2,1)S(1)}, bf16[512,512]{1,0:T(8,128)(2,1)S(1)}, u32[]{:S(2)}, u32[]{:S(2)}) collective-permute-start(bf16[512,512]{1,0:T(8,128)(2,1)S(1)} %get-tuple-element.49), channel_id=1, source_target_pairs={{0,4},{1,5},{2,0},{3,1},{4,8},{5,9},{6,2},{7,3},{8,12},{9,13},{10,... | collective-permute-start | bytes 1572872 | tf_op jit(solution)/shard_map/ppermute | solution.py:440
  65.0 12.9 %collective-permute-start.14 = (bf16[512,512]{1,0:T(8,128)(2,1)S(1)}, bf16[512,512]{1,0:T(8,128)(2,1)S(1)}, u32[]{:S(2)}, u32[]{:S(2)}) collective-permute-start(bf16[512,512]{1,0:T(8,128)(2,1)S(1)} %get-tuple-element.50), channel_id=1, source_target_pairs={{0,2},{1,3},{2,6},{3,7},{4,0},{5,1},{6,10},{7,11},{8,4},{9,5},{10,... | collective-permute-start | bytes 1572872 | tf_op jit(solution)/shard_map/ppermute | solution.py:440
  78.4 12.1 %collective-permute-start.15 = (bf16[512,512]{1,0:T(8,128)(2,1)S(1)}, bf16[512,512]{1,0:T(8,128)(2,1)S(1)}, u32[]{:S(2)}, u32[]{:S(2)}) collective-permute-start(bf16[512,512]{1,0:T(8,128)(2,1)S(1)} %get-tuple-element.51), channel_id=1, source_target_pairs={{0,4},{1,5},{2,0},{3,1},{4,8},{5,9},{6,2},{7,3},{8,12},{9,13},{10,... | collective-permute-start | bytes 1572872 | tf_op jit(solution)/shard_map/ppermute | solution.py:440
  80.0 11.7 %collective-permute-start.16 = (bf16[512,512]{1,0:T(8,128)(2,1)S(1)}, bf16[512,512]{1,0:T(8,128)(2,1)S(1)}, u32[]{:S(2)}, u32[]{:S(2)}) collective-permute-start(bf16[512,512]{1,0:T(8,128)(2,1)S(1)} %get-tuple-element.52), channel_id=1, source_target_pairs={{0,2},{1,3},{2,6},{3,7},{4,0},{5,1},{6,10},{7,11},{8,4},{9,5},{10,... | collective-permute-start | bytes 1572872 | tf_op jit(solution)/shard_map/ppermute | solution.py:440
  80.5 1.4 %collective-permute-start.20 = (f32[256,128]{1,0:T(8,128)S(1)}, f32[256,128]{1,0:T(8,128)S(1)}, u32[]{:S(2)}, u32[]{:S(2)}) collective-permute-start(f32[256,128]{1,0:T(8,128)S(1)} %get-tuple-element.45.refs_7_), channel_id=1, source_target_pairs={{0,1},{1,0},{2,3},{3,2},{4,5},{5,4},{6,7},{7,6},{8,9},{9,8},{10,11... | collective-permute-start | bytes 393224 | tf_op jit(solution)/shard_map/ppermute | solution.py:424
  80.5 1.4 %collective-permute-start.19 = (f32[128,128]{1,0:T(8,128)S(1)}, f32[128,128]{1,0:T(8,128)S(1)}, u32[]{:S(2)}, u32[]{:S(2)}) collective-permute-start(f32[128,128]{1,0:T(8,128)S(1)} %get-tuple-element.34.inverse.refs_5_), channel_id=1, source_target_pairs={{0,1},{1,0},{2,3},{3,2},{4,5},{5,4},{6,7},{7,6},{8,9},{9,8},{10,11... | collective-permute-start | bytes 196616 | tf_op jit(solution)/shard_map/ppermute | solution.py:404
  81.0 12.6 %collective-permute-start.10 = (f32[128,512]{1,0:T(8,128)S(1)}, f32[128,512]{1,0:T(8,128)S(1)}, u32[]{:S(2)}, u32[]{:S(2)}) collective-permute-start(f32[128,512]{1,0:T(8,128)S(1)} %get-tuple-element.42), channel_id=1, source_target_pairs={{0,1},{1,0},{2,3},{3,2},{4,5},{5,4},{6,7},{7,6},{8,9},{9,8},{10,11... | collective-permute-start | bytes 786440 | tf_op jit(solution)/shard_map/ppermute | solution.py:423
  82.4 12.4 %collective-permute-start.27 = (bf16[128,1024]{1,0:T(8,128)(2,1)S(1)}, bf16[128,1024]{1,0:T(8,128)(2,1)S(1)}, u32[]{:S(2)}, u32[]{:S(2)}) collective-permute-start(bf16[128,1024]{1,0:T(8,128)(2,1)S(1)} %get-tuple-element.62), channel_id=1, source_target_pairs={{16,0},{17,1},{18,2},{19,3},{20,4},{21,5},{22,6},{23,7},{24,8},{25... | collective-permute-start | bytes 786440 | tf_op jit(solution)/shard_map/ppermute | solution.py:432
  83.7 14.1 %collective-permute-start.28 = (bf16[128,1024]{1,0:T(8,128)(2,1)S(1)}, bf16[128,1024]{1,0:T(8,128)(2,1)S(1)}, u32[]{:S(2)}, u32[]{:S(2)}) collective-permute-start(bf16[128,1024]{1,0:T(8,128)(2,1)S(1)} %get-tuple-element.63), channel_id=1, source_target_pairs={{16,1},{17,0},{18,3},{19,2},{20,5},{21,4},{22,7},{23,6},{24,9},{25... | collective-permute-start | bytes 786440 | tf_op jit(solution)/shard_map/ppermute | solution.py:432
  90.5 14.2 %collective-permute-start.25 = (bf16[128,1024]{1,0:T(8,128)(2,1)S(1)}, bf16[128,1024]{1,0:T(8,128)(2,1)S(1)}, u32[]{:S(2)}, u32[]{:S(2)}) collective-permute-start(bf16[128,1024]{1,0:T(8,128)(2,1)S(1)} %get-tuple-element.60), channel_id=1, source_target_pairs={{16,0},{17,1},{18,2},{19,3},{20,4},{21,5},{22,6},{23,7},{24,8},{25... | collective-permute-start | bytes 786440 | tf_op jit(solution)/shard_map/ppermute | solution.py:432
  91.8 17.3 %collective-permute-start.26 = (bf16[128,1024]{1,0:T(8,128)(2,1)S(1)}, bf16[128,1024]{1,0:T(8,128)(2,1)S(1)}, u32[]{:S(2)}, u32[]{:S(2)}) collective-permute-start(bf16[128,1024]{1,0:T(8,128)(2,1)S(1)} %get-tuple-element.61), channel_id=1, source_target_pairs={{16,1},{17,0},{18,3},{19,2},{20,5},{21,4},{22,7},{23,6},{24,9},{25... | collective-permute-start | bytes 786440 | tf_op jit(solution)/shard_map/ppermute | solution.py:432
  93.6 22.4 %collective-permute-start.23 = (bf16[128,1024]{1,0:T(8,128)(2,1)S(1)}, bf16[128,1024]{1,0:T(8,128)(2,1)S(1)}, u32[]{:S(2)}, u32[]{:S(2)}) collective-permute-start(bf16[128,1024]{1,0:T(8,128)(2,1)S(1)} %get-tuple-element.58), channel_id=1, source_target_pairs={{16,0},{17,1},{18,2},{19,3},{20,4},{21,5},{22,6},{23,7},{24,8},{25... | collective-permute-start | bytes 786440 | tf_op jit(solution)/shard_map/ppermute | solution.py:432
  94.9 38.7 %collective-permute-start.17 = (bf16[512,512]{1,0:T(8,128)(2,1)S(1)}, bf16[512,512]{1,0:T(8,128)(2,1)S(1)}, u32[]{:S(2)}, u32[]{:S(2)}) collective-permute-start(bf16[512,512]{1,0:T(8,128)(2,1)S(1)} %get-tuple-element.53), channel_id=1, source_target_pairs={{0,4},{1,5},{2,0},{3,1},{4,8},{5,9},{6,2},{7,3},{8,12},{9,13},{10,... | collective-permute-start | bytes 1572872 | tf_op jit(solution)/shard_map/ppermute | solution.py:440
  97.9 35.7 %collective-permute-start.18 = (bf16[512,512]{1,0:T(8,128)(2,1)S(1)}, bf16[512,512]{1,0:T(8,128)(2,1)S(1)}, u32[]{:S(2)}, u32[]{:S(2)}) collective-permute-start(bf16[512,512]{1,0:T(8,128)(2,1)S(1)} %get-tuple-element.54), channel_id=1, source_target_pairs={{0,2},{1,3},{2,6},{3,7},{4,0},{5,1},{6,10},{7,11},{8,4},{9,5},{10,... | collective-permute-start | bytes 1572872 | tf_op jit(solution)/shard_map/ppermute | solution.py:440
  104.7 16.0 %collective-permute-start.24 = (bf16[128,1024]{1,0:T(8,128)(2,1)S(1)}, bf16[128,1024]{1,0:T(8,128)(2,1)S(1)}, u32[]{:S(2)}, u32[]{:S(2)}) collective-permute-start(bf16[128,1024]{1,0:T(8,128)(2,1)S(1)} %get-tuple-element.59), channel_id=1, source_target_pairs={{16,1},{17,0},{18,3},{19,2},{20,5},{21,4},{22,7},{23,6},{24,9},{25... | collective-permute-start | bytes 786440 | tf_op jit(solution)/shard_map/ppermute | solution.py:432
  109.1 18.0 %collective-permute-start.21 = (bf16[128,1024]{1,0:T(8,128)(2,1)S(1)}, bf16[128,1024]{1,0:T(8,128)(2,1)S(1)}, u32[]{:S(2)}, u32[]{:S(2)}) collective-permute-start(bf16[128,1024]{1,0:T(8,128)(2,1)S(1)} %get-tuple-element.56), channel_id=1, source_target_pairs={{16,0},{17,1},{18,2},{19,3},{20,4},{21,5},{22,6},{23,7},{24,8},{25... | collective-permute-start | bytes 786440 | tf_op jit(solution)/shard_map/ppermute | solution.py:432
  115.9 15.7 %collective-permute-start.22 = (bf16[128,1024]{1,0:T(8,128)(2,1)S(1)}, bf16[128,1024]{1,0:T(8,128)(2,1)S(1)}, u32[]{:S(2)}, u32[]{:S(2)}) collective-permute-start(bf16[128,1024]{1,0:T(8,128)(2,1)S(1)} %get-tuple-element.57), channel_id=1, source_target_pairs={{16,1},{17,0},{18,3},{19,2},{20,5},{21,4},{22,7},{23,6},{24,9},{25... | collective-permute-start | bytes 786440 | tf_op jit(solution)/shard_map/ppermute | solution.py:432
  120.7 12.9 %copy-start.2 = (bf16[8,128,512]{2,1,0:T(8,128)(2,1)S(1)}, bf16[8,128,512]{2,1,0:T(8,128)(2,1)}, u32[]{:S(2)}) copy-start(bf16[8,128,512]{2,1,0:T(8,128)(2,1)} %copy-done) | copy-start | bytes 3145732

commit v2 on v1

v2 whole, which is shorter than its diff:
```python
import functools
import math

import jax
import jax.numpy as jnp
from jax import lax
from jax.experimental import pallas as pl
from jax.experimental.pallas import tpu as pltpu
from jax.sharding import PartitionSpec as P

HQ = 32
HK = 4
HD = 128
SHARE = HQ // HK
EPS = 1e-05
F32 = jnp.float32
BF16 = jnp.bfloat16
VMEM_LIMIT = 48 * 1024 * 1024


def cost(us):
    return pl.CostEstimate(flops=int(us * 1e9) + 1, bytes_accessed=1024, transcendentals=0)


SMALL = cost(0.2)
STAGE = 3.0
SWAP = 12.0
PACKED = 6.0
RING = 6.0
LITTLE = 1.0


def params(**more):
    return pltpu.CompilerParams(vmem_limit_bytes=VMEM_LIMIT, **more)


def mm(a, b, contract):
    return lax.dot_general(a, b, ((contract[:1], contract[1:]), ((), ())), preferred_element_type=F32)


def sds(shape, dtype):
    return jax.ShapeDtypeStruct(shape, dtype)


def rope_tables(places):
    half = HD // 2
    steps = jnp.arange(half, dtype=F32)
    freq = jnp.exp(steps * (-2.0 * math.log(500000.0) / HD))
    angle = places.astype(F32)[:, None] * freq[None, :]
    cosine, sine = jnp.cos(angle), jnp.sin(angle)
    return jnp.concatenate([cosine, cosine], 1), jnp.concatenate([-sine, sine], 1)


def turn(x, cosine, sine):
    return x * cosine + pltpu.roll(x, HD // 2, 1) * sine


def turn_back(x, cosine, sine):
    return x * cosine - pltpu.roll(x, HD // 2, 1) * sine


def prep_kernel(
    where, mine_in, theirs_in, gain_m, gain_t, mine, theirs, gain_out, inverse, total, *, width
):
    step = pl.program_id(0)
    rows = lax.broadcasted_iota(jnp.int32, gain_m.shape, 0) == where[0]
    g_m = jnp.sum(jnp.where(rows, gain_m[...].astype(F32), 0.0), axis=0, keepdims=True)
    g_t = jnp.sum(jnp.where(rows, gain_t[...].astype(F32), 0.0), axis=0, keepdims=True)
    h_m = mine_in[...].astype(F32)
    h_t = theirs_in[...].astype(F32)
    mine[0] = (h_m * g_m).astype(BF16)
    theirs[0] = (h_t * g_t).astype(BF16)
    gain_out[0] = g_m
    part = jnp.sum(h_m * h_m + h_t * h_t, axis=1, keepdims=True)
    @pl.when(step == 0)
    def _():
        total[...] = jnp.broadcast_to(part, total.shape)

    @pl.when(step > 0)
    def _():
        total[...] += jnp.broadcast_to(part, total.shape)

    @pl.when(step == pl.num_programs(0) - 1)
    def _():
        inverse[...] = lax.rsqrt(total[...] / width + EPS)


def prep(where, hidden, gain_table, chips, rows):
    tokens, width = hidden.shape
    layers = gain_table.shape[0]
    mine = lambda r, where: (0, where[1 + r])
    theirs = lambda r, where: (0, where[1 + chips + r])
    return pl.pallas_call(
        functools.partial(prep_kernel, width=width),
        grid_spec=pltpu.PrefetchScalarGridSpec(
            num_scalar_prefetch=1,
            grid=(chips,),
            in_specs=[
                pl.BlockSpec((tokens, rows), mine),
                pl.BlockSpec((tokens, rows), theirs),
                pl.BlockSpec((layers, rows), mine),
                pl.BlockSpec((layers, rows), theirs),
            ],
            out_specs=[
                pl.BlockSpec((1, tokens, rows), lambda r, where: (r, 0, 0)),
                pl.BlockSpec((1, tokens, rows), lambda r, where: (r, 0, 0)),
                pl.BlockSpec((1, 1, rows), lambda r, where: (r, 0, 0)),
                pl.BlockSpec((tokens, HD), lambda r, where: (0, 0)),
            ],
            scratch_shapes=[pltpu.VMEM((tokens, HD), F32)],
        ),
        out_shape=[
            sds((chips, tokens, rows), BF16),
            sds((chips, tokens, rows), BF16),
            sds((chips, 1, rows), F32),
            sds((tokens, HD), F32),
        ],
        compiler_params=params(),
        cost_estimate=SMALL,
        name="prep",
    )(where, hidden, hidden, gain_table, gain_table)


def pick_kernel(where, hidden, out_m, out_t, sem, *, soon, chips):
    rows = out_m.shape[2]
    copies = []
    for side, out in enumerate((out_m, out_t)):
        for i, r in enumerate(soon):
            column = pl.multiple_of(where[1 + side * chips + r] * rows, rows)
            source = hidden.at[:, pl.ds(column, rows)]
            copies.append(pltpu.make_async_copy(source, out.at[i], sem.at[side, i]))
    for copy in copies:
        copy.start()
    for copy in copies:
        copy.wait()


def pick(where, hidden, soon, chips, rows):
    somewhere = pl.BlockSpec(memory_space=pl.ANY)
    return pl.pallas_call(
        functools.partial(pick_kernel, soon=soon, chips=chips),
        in_specs=[pl.BlockSpec(memory_space=pltpu.SMEM), somewhere],
        out_specs=[somewhere, somewhere],
        out_shape=[sds((len(soon), hidden.shape[0], rows), BF16)] * 2,
        scratch_shapes=[pltpu.SemaphoreType.DMA((2, len(soon)))],
        compiler_params=params(),
        cost_estimate=SMALL,
        name="pick",
    )(where, hidden)


def stacked(ref):
    return jnp.concatenate([ref[:, h * HD : (h + 1) * HD] for h in range(SHARE)], axis=0)


def probs_kernel(q_ref, k_ref, d_ref, cosine, sine, inverse, probs, q_out, k_out, vgs):
    cos, sin = cosine[...], sine[...]
    tokens = k_ref.shape[0]
    k_rot = turn(k_ref[...].astype(F32), cos, sin).astype(BF16)
    q_rot = jnp.concatenate(
        [turn(q_ref[:, h * HD : (h + 1) * HD].astype(F32), cos, sin).astype(BF16) for h in range(SHARE)],
        axis=0,
    )
    q_out[0] = q_rot
    k_out[0] = k_rot
    scores = mm(k_rot, q_rot, (1, 1)) * (HD**-0.5)
    key_at = lax.broadcasted_iota(jnp.int32, (tokens, tokens), 0)
    query_at = lax.broadcasted_iota(jnp.int32, (tokens, tokens), 1)
    seen = key_at <= query_at
    lows = []
    for h in range(SHARE):
        s = jnp.where(seen, scores[:, h * tokens : (h + 1) * tokens], -1e30)
        e = jnp.exp(s - jnp.max(s, axis=0, keepdims=True))
        p = e / jnp.sum(e, axis=0, keepdims=True)
        probs[0, :, h * tokens : (h + 1) * tokens] = p
        lows.append(p.astype(BF16))
    grad = mm(jnp.concatenate(lows, axis=1), stacked(d_ref), (1, 0))
    vgs[...] = (grad * inverse[...]).astype(BF16)


def attention_probs(queries, keys, out_grad, cosine, sine, inverse):
    tokens = queries.shape[0]
    group = pl.BlockSpec((tokens, SHARE * HD), lambda g: (0, g))
    head = pl.BlockSpec((tokens, HD), lambda g: (0, g))
    table = pl.BlockSpec((tokens, HD), lambda g: (0, 0))
    return pl.pallas_call(
        probs_kernel,
        grid=(HK,),
        in_specs=[group, head, group, table, table, table],
        out_specs=[
            pl.BlockSpec((1, tokens, SHARE * tokens), lambda g: (g, 0, 0)),
            pl.BlockSpec((1, SHARE * tokens, HD), lambda g: (g, 0, 0)),
            pl.BlockSpec((1, tokens, HD), lambda g: (g, 0, 0)),
            head,
        ],
        out_shape=[
            sds((HK, tokens, SHARE * tokens), F32),
            sds((HK, SHARE * tokens, HD), BF16),
            sds((HK, tokens, HD), BF16),
            sds((tokens, HK * HD), BF16),
        ],
        compiler_params=params(),
        cost_estimate=SMALL,
        name="probs",
    )(queries, keys, out_grad, cosine, sine, inverse)


def back_kernel(probs, q_rot, k_rot, d_ref, u_one, u_two, cosine, sine, inverse, dq, dk):
    cos, sin = cosine[...], sine[...]
    tokens = k_rot.shape[1]
    values = ((u_one[...] + u_two[...]) * inverse[...]).astype(BF16)
    d_probs = mm(values, stacked(d_ref), (1, 1))
    p = probs[0]
    delta = jnp.sum(p.astype(BF16).astype(F32) * d_probs, axis=0, keepdims=True)
    d_scores = (p * (d_probs - delta) * (HD**-0.5)).astype(BF16)
    dk[...] = turn_back(mm(d_scores, q_rot[0], (1, 0)), cos, sin).astype(BF16)
    key = k_rot[0]
    for h in range(SHARE):
        part = mm(d_scores[:, h * tokens : (h + 1) * tokens], key, (0, 0))
        dq[:, h * HD : (h + 1) * HD] = turn_back(part, cos, sin).astype(BF16)


def attention_back(probs, q_rot, k_rot, out_grad, u_one, u_two, cosine, sine, inverse):
    tokens = out_grad.shape[0]
    group = pl.BlockSpec((tokens, SHARE * HD), lambda g: (0, g))
    head = pl.BlockSpec((tokens, HD), lambda g: (0, g))
    table = pl.BlockSpec((tokens, HD), lambda g: (0, 0))
    return pl.pallas_call(
        back_kernel,
        grid=(HK,),
        in_specs=[
            pl.BlockSpec((1, tokens, SHARE * tokens), lambda g: (g, 0, 0)),
            pl.BlockSpec((1, SHARE * tokens, HD), lambda g: (g, 0, 0)),
            pl.BlockSpec((1, tokens, HD), lambda g: (g, 0, 0)),
            group,
            head,
            head,
            table,
            table,
            table,
        ],
        out_specs=[group, head],
        out_shape=[sds((tokens, HQ * HD), BF16), sds((tokens, HK * HD), BF16)],
        compiler_params=params(),
        cost_estimate=SMALL,
        name="back",
    )(probs, q_rot, k_rot, out_grad, u_one, u_two, cosine, sine, inverse)


def span(part, rows):
    side = part[1]
    return slice(0, rows) if side is None else slice(side * rows // 2, (side + 1) * rows // 2)


def features(ref, part):
    return ref[part[0]][:, span(part, ref.shape[2])]


def both_vgs(vgs, vgs_t):
    return jnp.concatenate([vgs[...], vgs_t[...]], axis=0)


def pair(mine, theirs, part):
    return jnp.concatenate([features(mine, part), features(theirs, part)], axis=0)


def values_kernel(*refs, parts, first, last):
    mine, theirs = refs[0], refs[1]
    weights, rest = refs[2 : 2 + len(parts)], refs[2 + len(parts) :]
    tokens = mine.shape[1]
    acc = None
    if not first:
        acc, rest = rest[0][...], rest[1:]
    for part, w in zip(parts, weights, strict=True):
        product = mm(pair(mine, theirs, part), w[...], (1, 0))
        acc = product if acc is None else acc + product
    if not last:
        rest[0][...] = acc
        return
    vgs, vgs_t, inverse, u_mine, packed = rest
    vgs = both_vgs(vgs, vgs_t).astype(F32)
    wide = acc.shape[1]
    u_mine[...] = acc[:tokens]
    packed[:, :wide] = acc[tokens:]
    dot_m = jnp.sum(acc[:tokens] * vgs[:tokens], axis=1, keepdims=True)
    dot_t = jnp.sum(acc[tokens:] * vgs[tokens:], axis=1, keepdims=True)
    packed[:, wide : wide + HD] = jnp.broadcast_to(dot_m, (tokens, HD))
    packed[:, wide + HD : wide + 2 * HD] = jnp.broadcast_to(dot_t, (tokens, HD))
    packed[:, wide + 2 * HD :] = inverse[...]


def values_sum(mine, theirs, parts, weights, before=(), final=()):
    tokens, wide = mine.shape[1], weights[0].shape[1]
    if final:
        out = [sds((tokens, wide), F32), sds((tokens, wide + 3 * HD), F32)]
    else:
        out = sds((2 * tokens, wide), F32)
    return pl.pallas_call(
        functools.partial(values_kernel, parts=parts, first=not before, last=bool(final)),
        out_shape=out,
        compiler_params=params(),
        cost_estimate=SMALL,
        name="values",
    )(mine, theirs, *weights, *before, *final)


def first_kernel(*refs, count):
    vgs, vgs_t, gain = refs[:3]
    weights, (out_m, out_t) = refs[3 : 3 + count], refs[3 + count :]
    tokens = vgs.shape[0]
    left = both_vgs(vgs, vgs_t)
    for i in range(count):
        part = mm(left, weights[i][...], (1, 1)) * gain[i]
        out_m[i] = part[:tokens].astype(BF16)
        out_t[i] = part[tokens:].astype(BF16)


def first_terms(vgs, vgs_t, gain, weights):
    count = len(weights)
    out = sds((count, vgs.shape[0], weights[0].shape[0]), BF16)
    return pl.pallas_call(
        functools.partial(first_kernel, count=count),
        out_shape=[out, out],
        compiler_params=params(),
        cost_estimate=SMALL,
        name="first_terms",
    )(vgs, vgs_t, gain, *weights)


def local_kernel(*refs, parts, shares, width):
    mine, theirs, vgs, vgs_t, gain, inverse, own, got = refs[:8]
    weights, outs = refs[8 : 8 + len(parts)], refs[8 + len(parts) :]
    blocks = sum(shares, [])
    rows = mine.shape[2]
    tokens, wide = vgs.shape
    one, two, three = (slice(wide + i * HD, wide + (i + 1) * HD) for i in range(3))
    inv_m, inv_t = inverse[...], got[:, three]
    c_m = inv_m * inv_m * (own[:, one] + got[:, two]) / width
    c_t = inv_t * inv_t * (own[:, two] + got[:, one]) / width
    coarse = c_m.astype(BF16)
    fine = (c_m - coarse.astype(F32)).astype(BF16)
    lane = lax.broadcasted_iota(jnp.int32, c_m.shape, 1)
    outs[0][:, len(blocks) * rows :] = jnp.where(lane < HD // 2, coarse.astype(F32), fine.astype(F32)).astype(BF16)
    c_m = jnp.concatenate([c_m] * (rows // HD), axis=1)
    c_t = jnp.concatenate([c_t] * (rows // HD), axis=1)
    left = both_vgs(vgs, vgs_t)
    for part, w in zip(parts, weights, strict=True):
        r, at = part[0], span(part, rows)
        n = blocks.index(r)
        share, i = (0, n) if n < len(shares[0]) else (1, n - len(shares[0]))
        at_m = slice(n * rows + at.start, n * rows + at.stop)
        at_t = slice(i * rows + at.start, i * rows + at.stop)
        g = gain[r][:, at]
        over = 1.0 / g
        product = mm(left, w[...], (1, 1))
        h_m, h_t = features(mine, part).astype(F32), features(theirs, part).astype(F32)
        outs[0][:, at_m] = (product[:tokens] * g - h_m * over * c_m[:, at]).astype(BF16)
        outs[1 + share][:, at_t] = (product[tokens:] * g - h_t * over * c_t[:, at]).astype(BF16)


def local_grads(mine, theirs, vgs, vgs_t, gain, inverse, own, got, shares, parts, weights, width):
    tokens, rows = mine.shape[1:]
    wide = [len(share) * rows for share in shares]
    out = [sds((tokens, w), BF16) for w in (sum(wide) + HD, *wide)]
    return pl.pallas_call(
        functools.partial(local_kernel, parts=parts, shares=shares, width=width),
        out_shape=out,
        compiler_params=params(),
        cost_estimate=SMALL,
        name="local_grad",
    )(mine, theirs, vgs, vgs_t, gain, inverse, own, got, *weights)


def weight_kernel(*refs, part):
    mine, theirs, vgs, vgs_t = refs[:4]
    right = both_vgs(vgs, vgs_t)
    total = mm(pair(mine, theirs, part), right, (0, 0))
    for arrived in refs[4:-1]:
        total = total + arrived[...].astype(F32)
    refs[-1][...] = total.astype(BF16)


def weight_step(mine, theirs, vgs, vgs_t, part, arrived):
    return pl.pallas_call(
        functools.partial(weight_kernel, part=part),
        out_shape=sds((mine.shape[2] // 2, vgs.shape[1]), BF16),
        compiler_params=params(),
        cost_estimate=SMALL,
        name="weight_step",
    )(mine, theirs, vgs, vgs_t, *arrived)


def weight_last_kernel(mine, theirs, vgs, vgs_t, low_f, low_b, high_f, high_b, pin, out):
    right = both_vgs(vgs, vgs_t)
    half = low_f.shape[0]
    for side, (one, two) in enumerate(((low_f, low_b), (high_f, high_b))):
        total = mm(pair(mine, theirs, (0, side)), right, (0, 0))
        total = total + one[...].astype(F32) + two[...].astype(F32)
        out[side * half : (side + 1) * half, :] = total.astype(BF16)


def weight_last(mine, theirs, vgs, vgs_t, arrived, pin):
    return pl.pallas_call(
        weight_last_kernel,
        out_shape=sds((mine.shape[2], vgs.shape[1]), BF16),
        compiler_params=params(),
        cost_estimate=SMALL,
        name="weight_last",
    )(mine, theirs, vgs, vgs_t, *arrived, pin)


def copies_of(pieces, shares, where, out, sem, first, rows):
    copies = []
    for piece, blocks in zip(pieces, shares, strict=True):
        for j, r in enumerate(blocks):
            column = pl.multiple_of(where[first + r] * rows, rows)
            source, target = piece.at[:, j * rows : (j + 1) * rows], out.at[:, pl.ds(column, rows)]
            copies.append(pltpu.make_async_copy(source, target, sem.at[len(copies)]))
    return copies


def early_kernel(where, ones, twos, raw_m, raw_t, second, *refs, soon, shares, chips, rows):
    pieces, (out, done, sem, sems) = refs[:-4], refs[-4:]
    copies = copies_of(pieces, shares, where, out, sem, 1, rows)
    for copy in copies:
        copy.start()
    c = second[...].astype(F32)
    c = c + pltpu.roll(c, HD // 2, 1)
    c = jnp.concatenate([c] * (rows // HD), axis=1)
    for side, (terms, raw) in enumerate(((ones, raw_m), (twos, raw_t))):
        for i, r in enumerate(soon):
            done[side, i] = (terms[i].astype(F32) - raw[i].astype(F32) * c).astype(BF16)
            column = pl.multiple_of(where[1 + side * chips + r] * rows, rows)
            copies.append(pltpu.make_async_copy(done.at[side, i], out.at[:, pl.ds(column, rows)], sems.at[side, i]))
            copies[-1].start()
    for copy in copies:
        copy.wait()


def early_blocks(where, ones, twos, raw_m, raw_t, pieces, soon, shares, chips, width):
    _, tokens, rows = ones.shape
    somewhere = pl.BlockSpec(memory_space=pl.ANY)
    return pl.pallas_call(
        functools.partial(early_kernel, soon=soon, shares=shares, chips=chips, rows=rows),
        grid=(1,),
        in_specs=[
            pl.BlockSpec(memory_space=pltpu.SMEM),
            pl.BlockSpec(ones.shape, lambda i: (0, 0, 0)),
            pl.BlockSpec(twos.shape, lambda i: (0, 0, 0)),
            pl.BlockSpec(ones.shape, lambda i: (0, 0, 0)),
            pl.BlockSpec(ones.shape, lambda i: (0, 0, 0)),
            pl.BlockSpec((tokens, HD), lambda i: (0, len(shares[0]) * rows // HD)),
        ]
        + [somewhere] * len(pieces),
        out_specs=somewhere,
        out_shape=sds((tokens, width), BF16),
        scratch_shapes=[
            pltpu.VMEM((2, *ones.shape), BF16),
            pltpu.SemaphoreType.DMA((sum(len(x) for x in shares),)),
            pltpu.SemaphoreType.DMA((2, len(soon))),
        ],
        compiler_params=params(),
        cost_estimate=SMALL,
        name="early_blocks",
    )(where, ones, twos, raw_m, raw_t, pieces[0], *pieces)


def join_kernel(where, base, *refs, shares, chips, rows):
    pieces, (out, sem) = refs[:-2], refs[-2:]
    copies = copies_of(pieces, shares, where, out, sem, 1 + chips, rows)
    for copy in copies:
        copy.start()
    for copy in copies:
        copy.wait()


def join(where, base, pieces, shares, chips, rows):
    somewhere = pl.BlockSpec(memory_space=pl.ANY)
    return pl.pallas_call(
        functools.partial(join_kernel, shares=shares, chips=chips, rows=rows),
        in_specs=[pl.BlockSpec(memory_space=pltpu.SMEM)] + [somewhere] * (1 + len(pieces)),
        out_specs=somewhere,
        out_shape=sds(base.shape, BF16),
        input_output_aliases={1: 0},
        scratch_shapes=[pltpu.SemaphoreType.DMA((sum(len(x) for x in shares),))],
        compiler_params=params(),
        cost_estimate=SMALL,
        name="join",
    )(where, base, *pieces)


def fence_kernel(x, out):
    out[...] = x[...]


def fence(x, us):
    return pl.pallas_call(
        fence_kernel,
        out_shape=sds(x.shape, x.dtype),
        compiler_params=params(),
        cost_estimate=cost(us),
        name="fence",
    )(x)


def last_layer(layer_counts, layers):
    sections, mine = lax.axis_size("section"), lax.axis_index("section")
    own = layer_counts[0]
    total = own
    if sections > 2:
        reach = 1
        while reach < sections:
            route = [(i, i + reach) for i in range(sections - reach)]
            total = total + lax.ppermute(total, "section", route)
            reach *= 2
    return jnp.where(mine == sections - 1, layers, total) - 1


def shards(hidden, gain_table, layer_counts, positions, queries, keys, value_weight, out_grad):
    tokens_in, weight = hidden[0], value_weight[0]
    tokens, width = tokens_in.shape
    rows = weight.shape[0]
    sections = lax.axis_size("section")
    devices = lax.axis_size("dp")
    chips = devices // 2
    ring = list(range(0, chips, 2)) + list(range(1, chips, 2))[::-1]
    place_of = [ring.index(c) for c in range(chips)]
    me = lax.axis_index("dp")
    chip, core = me // 2, me % 2
    place = jnp.where(chip % 2 == 0, chip // 2, chips - 1 - chip // 2)
    spots = (place + jnp.arange(chips, dtype=jnp.int32)) % chips
    order = 2 * jnp.where(spots < (chips + 1) // 2, 2 * spots, 2 * (chips - 1 - spots) + 1)

    def hop(d, by):
        return 2 * ring[(place_of[d // 2] + by) % chips] + d % 2

    forth = [(d, hop(d, 1)) for d in range(devices)]
    back = [(d, hop(d, -1)) for d in range(devices)]
    swap = [(d, d ^ 1) for d in range(devices)]
    down = [(s * devices + d, (s - 1) * devices + d) for s in range(1, sections) for d in range(devices)]
    cross = [(s * devices + d, (s - 1) * devices + (d ^ 1)) for s in range(1, sections) for d in range(devices)]

    half = chips // 2
    low, high = slice(0, rows // 2), slice(rows // 2, rows)
    soon = [0, 1, chips - 1]
    later = [[2, chips - 2, 3], list(range(4, chips - 2))]

    def ahead(x):
        return lax.ppermute(x, "dp", forth)

    def behind(x):
        return lax.ppermute(x, "dp", back)

    def swapped(x):
        return lax.ppermute(x, "dp", swap)

    def sent_down(x):
        return lax.ppermute(x, ("section", "dp"), down)

    def sent_across(x):
        return lax.ppermute(x, ("section", "dp"), cross)

    token = []

    def after(x):
        x = lax.optimization_barrier((x, *token))[0] if token else x
        token[:] = [x]
        return x

    def then(*results):
        token[:] = [results[0]]
        return results if len(results) > 1 else results[0]

    pin = [jnp.zeros((8, HD), F32)]

    def hold(us=STAGE):
        pin[0] = then(fence(after(pin[0]), us))

    def parts_of(some):
        return [part for part in held if part[0] in some]

    def weights(parts):
        return [held[part] for part in parts]

    held = {(0, None): weight}
    moving = {}

    def gather_step(step):
        if step > 1:
            for r in (chips - step + 1, step - 1):
                held[r, None] = after(moving.pop(r))
        f, b = held[(chips - step + 1) % chips, None], held[step - 1, None]
        if step < half:
            moving[chips - step], moving[step] = ahead(f), behind(b)
        else:
            moving[0], moving[1] = ahead(f[low]), behind(b[high])

    gather_step(1)

    last = last_layer(layer_counts, gain_table.shape[0])
    where = jnp.concatenate([last[None], order + core, order + 1 - core]).astype(jnp.int32)
    cosine, sine = rope_tables(positions[0])
    raw_m, raw_t = then(*pick(where, tokens_in, soon, chips, rows))
    raw_m = sent_down(raw_m)
    mine, send, gain, inverse = then(*prep(after(where), tokens_in, gain_table, chips, rows))
    theirs = swapped(send)
    probs, q_rot, k_rot, vgs = then(
        *attention_probs(queries[0], keys[0], out_grad[0], cosine, sine, after(inverse))
    )
    vgs_t = swapped(vgs)
    hold(SWAP)
    gather_step(2)
    theirs, vgs_t = after(theirs), after(vgs_t)
    soon_gain = jnp.concatenate([gain[r : r + 1] for r in soon], axis=0)
    parts = parts_of(soon)
    one, two = then(*first_terms(after(vgs), vgs_t, soon_gain, [held[r, None] for r in soon]))
    raw_m = after(raw_m)
    one = sent_down(after(one))
    total = then(values_sum(after(mine), theirs, parts, weights(parts)))
    hold(RING)
    for step in range(3, half + 1):
        gather_step(step)
        if step == 3:
            one = after(one)
            two = sent_across(after(two))
        if step < half:
            parts = parts_of([step - 1, chips - step + 1])
            total = then(values_sum(after(mine), theirs, parts, weights(parts), (total,)))
            hold(RING)

    chains = [
        (0, ahead, list(range(half, 0, -1))),
        (1, behind, list(range(half, chips))),
        (1, ahead, list(range(half - 1, 0, -1))),
        (0, behind, list(range(half + 1, chips))),
    ]
    arrived = [()] * 4
    at = [0] * 4

    def weight_turn(*which):
        for i in which:
            side, move, route = chains[i]
            got = tuple(after(x) for x in arrived[i])
            part = (route[at[i]], side)
            total = then(weight_step(after(mine), theirs, vgs, vgs_t, part, got))
            arrived[i] = (move(total),)
            at[i] += 1

    hold(RING)
    two = after(two)
    raw_t = sent_down(after(raw_t))
    weight_turn(0, 1)
    parts = parts_of([half - 1, half + 1])
    total = then(values_sum(after(mine), theirs, parts, weights(parts), (total,)))
    hold(LITTLE)
    held[half, 0], held[half, 1] = after(moving[0]), after(moving[1])
    parts = parts_of([half])
    u_mine, packed = values_sum(after(mine), theirs, parts, weights(parts), (total,), (vgs, vgs_t, inverse))
    then(packed)
    got = swapped(packed)
    weight_turn(2)
    hold(PACKED)
    got = after(got)
    weight_turn(3)
    parts = parts_of(sum(later, []))
    m, t1, t2 = then(
        *local_grads(
            mine, theirs, after(vgs), vgs_t, gain, inverse, packed, got, later, parts, weights(parts), width
        )
    )
    raw_t = after(raw_t)
    m = sent_down(after(m))
    hold()
    weight_turn(0, 1)
    hold()
    weight_turn(2, 3)
    query_grad, key_grad = then(
        *attention_back(probs, q_rot, k_rot, out_grad[0], after(u_mine), got, cosine, sine, inverse)
    )
    for turn in range(2, half - 1):
        hold()
        weight_turn(0, 1)
        hold()
        weight_turn(2, 3)
        if turn == 2:
            m = after(m)
            t1 = sent_across(after(t1))
    hold()
    weight_turn(0, 1)
    last_low, last_high = after(arrived[3][0]), after(arrived[2][0])
    t2 = sent_across(after(t2))
    hold()
    upstream = then(early_blocks(where, one, two, raw_m, raw_t, [after(m)], soon, [sum(later, [])], chips, width))
    arrived = [after(arrived[0][0]), last_low, after(arrived[1][0]), last_high]
    weight_grad = then(weight_last(mine, theirs, after(vgs), vgs_t, arrived, pin[0]))
    t1, t2 = after(t1), after(t2)
    upstream = then(join(where, after(upstream), [t1, t2], later, chips, rows))
    return (query_grad[None], key_grad[None], weight_grad[None], upstream[None])


def solution(mesh):
    split = P("section", "dp", None)
    in_specs = (split, P(), P("section"), P("section", "dp"), split, split, split, split)
    out_specs = (split,) * 4
    return jax.shard_map(shards, mesh=mesh, in_specs=in_specs, out_specs=out_specs, check_vma=False)
```

time: 135 us -> 115 us (0.85)
  waiting for transfers between devices: 77.2 us -> 52.7 us
  starting transfers between devices: 28.6 us -> 33.6 us
  Pallas kernels: 18.1 us -> 22.7 us
  local copies, waits for them, and re-layouts: 6.09 us -> 3.21 us
  between operations: 3.61 us -> 1.81 us
    ppermute x29 -> x32, waiting for transfers between devices: 77.2 us -> 52.7 us  [the longest x11 20 us: ahead(): return lax.ppermute(x, 'dp', forth)]
    ppermute x29 -> x32, starting transfers between devices: 28.6 us -> 33.6 us  [the longest x11 19.5 us: ahead(): return lax.ppermute(x, 'dp', forth)]
    pallas_call x12 -> x36, Pallas kernels: 9.49 us -> 14.1 us  [the longest x14 3.46 us: weight_step(): pl.pallas_call(functools.partial(weight_kernel, part=part), out_shape=sds...]
    unnamed x21 -> x22, local copies, waits for them, and re-layouts: 4.79 us -> 3.17 us
  transfers between devices with their start and end apart: 29 -> 32, of which waited for: 15 -> 16; matrix products, arithmetic and copies ran while one was open for 2% -> 0% of each run, Pallas kernels for 11% -> 18%
where the time goes in v2:
time: 115 us
  waiting for transfers between devices  52.7 us (46%)
  starting transfers between devices  33.6 us (29%)
  Pallas kernels  22.7 us (20%)
  local copies, waits for them, and re-layouts  3.21 us (3%)
  between operations  1.81 us (2%)
    ppermute x11, waiting for transfers between devices, ahead(): return lax.ppermute(x, 'dp', forth)  20 us
    ppermute x11, starting transfers between devices, ahead(): return lax.ppermute(x, 'dp', forth)  19.5 us
    ppermute x11, waiting for transfers between devices, behind(): return lax.ppermute(x, 'dp', back)  17.8 us
    ppermute x3, waiting for transfers between devices, sent_across(): return lax.ppermute(x, ('section', 'dp'), cross)  6.91 us
    ppermute x4, waiting for transfers between devices, sent_down(): return lax.ppermute(x, ('section', 'dp'), down)  6.24 us
    ppermute x4, starting transfers between devices, sent_down(): return lax.ppermute(x, ('section', 'dp'), down)  5.26 us
    ppermute x11, starting transfers between devices, behind(): return lax.ppermute(x, 'dp', back)  4.28 us
    ppermute x3, starting transfers between devices, sent_across(): return lax.ppermute(x, ('section', 'dp'), cross)  3.84 us
  transfers between devices with their start and end apart: 32, of which 16 were waited for; matrix products, arithmetic and copies ran while one was open for 0% of the time, Pallas kernels for 18%

profile of v2, /device:TPU:0, one launch (start us, length us, event | category | flops | bytes accessed | tf_op | source)
XLA Modules:
  0.0 114.5 jit_solution(15171830317630974284)
XLA Ops:
  0.6 3.1 %collective-permute-start.1 = (bf16[512,512]{1,0:T(8,128)(2,1)}, bf16[512,512]{1,0:T(8,128)(2,1)S(1)}, u32[]{:S(2)}, u32[]{:S(2)}) collective-permute-start(bf16[512,512]{1,0:T(8,128)(2,1)} %bitcast.19), channel_id=1, source_target_pairs={{0,4},{1,5},{2,0},{3,1},{4,8},{5,9},{6,2},{7,3},{8,12},{9,13},{10,... | collective-permute-start | bytes 1572872 | tf_op jit(solution)/shard_map/ppermute | solution.py:549
  4.5 1.6 %copy-done.4 = bf16[1,128,8192]{2,1,0:T(8,128)(2,1)S(1)} copy-done((bf16[1,128,8192]{2,1,0:T(8,128)(2,1)S(1)}, bf16[1,128,8192]{2,1,0:T(8,128)(2,1)}, u32[]{:S(2)}) %copy-start.4) | copy-done | bytes 2097176
  6.1 1.4 %pick.1 = (bf16[3,128,512]{2,1,0:T(8,128)(2,1)S(1)}, bf16[3,128,512]{2,1,0:T(8,128)(2,1)}) custom-call(s32[17]{0:T(128)S(1)} %pad_add_fusion.where, bf16[128,8192]{1,0:T(8,128)(2,1)S(1)} %bitcast.14), custom_call_target="tpu_custom_call" | custom-call | flops 200000000 | bytes 1024 | tf_op jit(solution)/shard_map/pick/pallas_call | solution.py:140
  7.5 1.4 %collective-permute-start.6 = (bf16[3,128,512]{2,1,0:T(8,128)(2,1)S(1)}, bf16[3,128,512]{2,1,0:T(8,128)(2,1)S(1)}, u32[]{:S(2)}, u32[]{:S(2)}) collective-permute-start(bf16[3,128,512]{2,1,0:T(8,128)(2,1)S(1)} %get-tuple-element.99), channel_id=1, source_target_pairs={{16,0},{17,1},{18,2},{19,3},{20,4},{21,5},{22,6},{23,7},{24,8},{25... | collective-permute-start | bytes 1179656 | tf_op jit(solution)/shard_map/ppermute | solution.py:558
  9.0 2.3 %prep.1 = (bf16[8,128,512]{2,1,0:T(8,128)(2,1)S(1)}, bf16[8,128,512]{2,1,0:T(8,128)(2,1)S(1)}, f32[8,1,512]{2,1,0:T(1,128)S(1)}, f32[128,128]{1,0:T(8,128)S(1)}) custom-call(s32[17]{0:T(128)S(1)} %pad_add_fusion.where, bf16[128,8192]{1,0:T(8,128)(2,1)S(1)} %bitcast.15, bf16[128,8192]{1,0:T(8,128)(2,1)S(1)} %bitcast.16, bf16[10,8192]{1,0:T(8,128)(2,1)S(1)} %copy-done.7, ...), custom_call_target="tpu_custom_call" | custom-call | flops 200000000 | bytes 1024 | tf_op jit(solution)/shard_map/prep/pallas_call | solution.py:93
  11.9 2.7 %probs.1 = (f32[4,128,1024]{2,1,0:T(8,128)S(1)}, bf16[4,1024,128]{2,1,0:T(8,128)(2,1)S(1)}, bf16[4,128,128]{2,1,0:T(8,128)(2,1)S(1)}, bf16[128,512]{1,0:T(8,128)(2,1)S(1)}) custom-call(bf16[128,4096]{1,0:T(8,128)(2,1)S(1)} %bitcast.23, bf16[128,512]{1,0:T(8,128)(2,1)S(1)} %bitcast.24, bf16[128,4096]{1,0:T(8,128)(2,1)S(1)} %bitcast.17, ...), custom_call_target="tpu_custom_call" | custom-call | flops 200000000 | bytes 1024 | tf_op jit(solution)/shard_map/probs/pallas_call | solution.py:186
  14.6 0.5 collective-permute-start.4
  15.2 0.6 collective-permute-done.1.refs_5_.refs_3_
  15.8 1.8 %collective-permute-start.3 = (bf16[512,512]{1,0:T(8,128)(2,1)S(1)}, bf16[512,512]{1,0:T(8,128)(2,1)S(1)}, u32[]{:S(2)}, u32[]{:S(2)}) collective-permute-start(bf16[512,512]{1,0:T(8,128)(2,1)S(1)} %collective-permute-done.1.refs_5_.refs_3_), channel_id=1, source_target_pairs={{0,4},{1,5},{2,0},{3,1},{4,8},{5,9},{6,2},{7,3},{8,12},{9,13},{10,... | collective-permute-start | bytes 1572872 | tf_op jit(solution)/shard_map/ppermute | solution.py:549
  17.8 0.6 first_terms.1
  18.5 1.7 %collective-permute-done.6.raw_m = bf16[3,128,512]{2,1,0:T(8,128)(2,1)S(1)} collective-permute-done((bf16[3,128,512]{2,1,0:T(8,128)(2,1)S(1)}, bf16[3,128,512]{2,1,0:T(8,128)(2,1)S(1)}, u32[]{:S(2)}, u32[]{:S(2)}) %collective-permute-start.6) | collective-permute-done | bytes 393248 | tf_op jit(solution)/shard_map/ppermute | solution.py:558
  20.1 1.3 %collective-permute-start.9 = (bf16[3,128,512]{2,1,0:T(8,128)(2,1)S(1)}, bf16[3,128,512]{2,1,0:T(8,128)(2,1)S(1)}, u32[]{:S(2)}, u32[]{:S(2)}) collective-permute-start(bf16[3,128,512]{2,1,0:T(8,128)(2,1)S(1)} %get-tuple-element.118), channel_id=1, source_target_pairs={{16,0},{17,1},{18,2},{19,3},{20,4},{21,5},{22,6},{23,7},{24,8},{25... | collective-permute-start | bytes 1179656 | tf_op jit(solution)/shard_map/ppermute | solution.py:558
  21.4 0.6 values.4.refs_4_
  22.0 7.4 %collective-permute-done.3.refs_2_.refs_8_ = bf16[512,512]{1,0:T(8,128)(2,1)S(1)} collective-permute-done((bf16[512,512]{1,0:T(8,128)(2,1)S(1)}, bf16[512,512]{1,0:T(8,128)(2,1)S(1)}, u32[]{:S(2)}, u32[]{:S(2)}) %collective-permute-start.3) | collective-permute-done | bytes 524320 | tf_op jit(solution)/shard_map/ppermute | solution.py:549
  29.4 1.8 %collective-permute-start.8 = (bf16[512,512]{1,0:T(8,128)(2,1)S(1)}, bf16[512,512]{1,0:T(8,128)(2,1)S(1)}, u32[]{:S(2)}, u32[]{:S(2)}) collective-permute-start(bf16[512,512]{1,0:T(8,128)(2,1)S(1)} %collective-permute-done.3.refs_2_.refs_8_), channel_id=1, source_target_pairs={{0,4},{1,5},{2,0},{3,1},{4,8},{5,9},{6,2},{7,3},{8,12},{9,13},{10,... | collective-permute-start | bytes 1572872 | tf_op jit(solution)/shard_map/ppermute | solution.py:549
  31.7 1.3 %collective-permute-start.12 = (bf16[3,128,512]{2,1,0:T(8,128)(2,1)S(1)}, bf16[3,128,512]{2,1,0:T(8,128)(2,1)S(1)}, u32[]{:S(2)}, u32[]{:S(2)}) collective-permute-start(bf16[3,128,512]{2,1,0:T(8,128)(2,1)S(1)} %get-tuple-element.125), channel_id=1, source_target_pairs={{16,1},{17,0},{18,3},{19,2},{20,5},{21,4},{22,7},{23,6},{24,9},{25... | collective-permute-start | bytes 1179656 | tf_op jit(solution)/shard_map/ppermute | solution.py:561
  33.4 8.7 %collective-permute-done.8.refs_2_.refs_10_ = bf16[512,512]{1,0:T(8,128)(2,1)S(1)} collective-permute-done((bf16[512,512]{1,0:T(8,128)(2,1)S(1)}, bf16[512,512]{1,0:T(8,128)(2,1)S(1)}, u32[]{:S(2)}, u32[]{:S(2)}) %collective-permute-start.8) | collective-permute-done | bytes 524320 | tf_op jit(solution)/shard_map/ppermute | solution.py:549
  42.1 1.5 %collective-permute-done.7.refs_3_.refs_11_ = bf16[512,512]{1,0:T(8,128)(2,1)S(1)} collective-permute-done((bf16[512,512]{1,0:T(8,128)(2,1)S(1)}, bf16[512,512]{1,0:T(8,128)(2,1)S(1)}, u32[]{:S(2)}, u32[]{:S(2)}) %collective-permute-start.7) | collective-permute-done | bytes 524320 | tf_op jit(solution)/shard_map/ppermute | solution.py:552
  43.6 1.6 %collective-permute-start.11 = (bf16[256,512]{1,0:T(8,128)(2,1)S(1)}, bf16[256,512]{1,0:T(8,128)(2,1)S(1)}, u32[]{:S(2)}, u32[]{:S(2)}) collective-permute-start(bf16[256,512]{1,0:T(8,128)(2,1)S(1)} %slice.17), channel_id=1, source_target_pairs={{0,4},{1,5},{2,0},{3,1},{4,8},{5,9},{6,2},{7,3},{8,12},{9,13},{10,... | collective-permute-start | bytes 786440 | tf_op jit(solution)/shard_map/ppermute | solution.py:549
  46.7 3.4 %collective-permute-done.11.refs_2_.refs_12_ = bf16[256,512]{1,0:T(8,128)(2,1)S(1)} collective-permute-done((bf16[256,512]{1,0:T(8,128)(2,1)S(1)}, bf16[256,512]{1,0:T(8,128)(2,1)S(1)}, u32[]{:S(2)}, u32[]{:S(2)}) %collective-permute-start.11) | collective-permute-done | bytes 262176 | tf_op jit(solution)/shard_map/ppermute | solution.py:549
  50.1 1.6 %collective-permute-done.10.refs_3_.refs_13_ = bf16[256,512]{1,0:T(8,128)(2,1)S(1)} collective-permute-done((bf16[256,512]{1,0:T(8,128)(2,1)S(1)}, bf16[256,512]{1,0:T(8,128)(2,1)S(1)}, u32[]{:S(2)}, u32[]{:S(2)}) %collective-permute-start.10) | collective-permute-done | bytes 262176 | tf_op jit(solution)/shard_map/ppermute | solution.py:552
  52.3 1.6 %collective-permute-start.15 = (bf16[256,512]{1,0:T(8,128)(2,1)S(1)}, bf16[256,512]{1,0:T(8,128)(2,1)S(1)}, u32[]{:S(2)}, u32[]{:S(2)}) collective-permute-start(bf16[256,512]{1,0:T(8,128)(2,1)S(1)} %weight_step.16), channel_id=1, source_target_pairs={{0,4},{1,5},{2,0},{3,1},{4,8},{5,9},{6,2},{7,3},{8,12},{9,13},{10,... | collective-permute-start | bytes 786440 | tf_op jit(solution)/shard_map/ppermute | solution.py:549
  54.4 1.6 %collective-permute-start.18 = (bf16[256,512]{1,0:T(8,128)(2,1)S(1)}, bf16[256,512]{1,0:T(8,128)(2,1)S(1)}, u32[]{:S(2)}, u32[]{:S(2)}) collective-permute-start(bf16[256,512]{1,0:T(8,128)(2,1)S(1)} %weight_step.14), channel_id=1, source_target_pairs={{0,4},{1,5},{2,0},{3,1},{4,8},{5,9},{6,2},{7,3},{8,12},{9,13},{10,... | collective-permute-start | bytes 786440 | tf_op jit(solution)/shard_map/ppermute | solution.py:549
  55.9 1.3 %collective-permute-start.16 = (bf16[3,128,512]{2,1,0:T(8,128)(2,1)}, bf16[3,128,512]{2,1,0:T(8,128)(2,1)S(1)}, u32[]{:S(2)}, u32[]{:S(2)}) collective-permute-start(bf16[3,128,512]{2,1,0:T(8,128)(2,1)} %get-tuple-element.133), channel_id=1, source_target_pairs={{16,0},{17,1},{18,2},{19,3},{20,4},{21,5},{22,6},{23,7},{24,8},{25... | collective-permute-start | bytes 1179656 | tf_op jit(solution)/shard_map/ppermute | solution.py:558
  57.3 1.8 %collective-permute-done.13.refs_7_.u_two = f32[128,896]{1,0:T(8,128)S(1)} collective-permute-done((f32[128,896]{1,0:T(8,128)S(1)}, f32[128,896]{1,0:T(8,128)S(1)}, u32[]{:S(2)}, u32[]{:S(2)}) %collective-permute-start.13) | collective-permute-done | bytes 458784 | tf_op jit(solution)/shard_map/ppermute | solution.py:555
  59.4 2.5 %local_grad.1 = (bf16[128,2688]{1,0:T(8,128)(2,1)S(1)}, bf16[128,1536]{1,0:T(8,128)(2,1)S(1)}, bf16[128,1024]{1,0:T(8,128)(2,1)S(1)}) custom-call(bf16[8,128,512]{2,1,0:T(8,128)(2,1)} %copy-done, bf16[8,128,512]{2,1,0:T(8,128)(2,1)} %copy-done.2, bf16[128,512]{1,0:T(8,128)(2,1)S(1)} %get-tuple-element.190.refs_0_.refs_2_.refs_5_.vgs, ...), custom_call_target="tpu_custom_call" | custom-call | flops 200000000 | bytes 1024 | tf_op jit(solution)/shard_map/local_grad/pallas_call | solution.py:365
  61.9 4.3 %collective-permute-done.16.raw_t = bf16[3,128,512]{2,1,0:T(8,128)(2,1)S(1)} collective-permute-done((bf16[3,128,512]{2,1,0:T(8,128)(2,1)}, bf16[3,128,512]{2,1,0:T(8,128)(2,1)S(1)}, u32[]{:S(2)}, u32[]{:S(2)}) %collective-permute-start.16) | collective-permute-done | bytes 393248 | tf_op jit(solution)/shard_map/ppermute | solution.py:558
  66.2 1.2 %copy-done.1 = bf16[8,128,512]{2,1,0:T(8,128)(2,1)S(1)} copy-done((bf16[8,128,512]{2,1,0:T(8,128)(2,1)S(1)}, bf16[8,128,512]{2,1,0:T(8,128)(2,1)}, u32[]{:S(2)}) %copy-start.1) | copy-done | bytes 1048600
  68.2 0.5 collective-permute-start.19
  68.7 1.6 %collective-permute-start.20 = (bf16[256,512]{1,0:T(8,128)(2,1)S(1)}, bf16[256,512]{1,0:T(8,128)(2,1)S(1)}, u32[]{:S(2)}, u32[]{:S(2)}) collective-permute-start(bf16[256,512]{1,0:T(8,128)(2,1)S(1)} %weight_step.18), channel_id=1, source_target_pairs={{0,4},{1,5},{2,0},{3,1},{4,8},{5,9},{6,2},{7,3},{8,12},{9,13},{10,... | collective-permute-start | bytes 786440 | tf_op jit(solution)/shard_map/ppermute | solution.py:549
  70.7 1.3 %collective-permute-start.23 = (bf16[128,2688]{1,0:T(8,128)(2,1)S(1)}, bf16[128,2688]{1,0:T(8,128)(2,1)S(1)}, u32[]{:S(2)}, u32[]{:S(2)}) collective-permute-start(bf16[128,2688]{1,0:T(8,128)(2,1)S(1)} %get-tuple-element.150), channel_id=1, source_target_pairs={{16,0},{17,1},{18,2},{19,3},{20,4},{21,5},{22,6},{23,7},{24,8},{25... | collective-permute-start | bytes 2064392 | tf_op jit(solution)/shard_map/ppermute | solution.py:558
  72.3 1.6 %collective-permute-start.25 = (bf16[256,512]{1,0:T(8,128)(2,1)S(1)}, bf16[256,512]{1,0:T(8,128)(2,1)S(1)}, u32[]{:S(2)}, u32[]{:S(2)}) collective-permute-start(bf16[256,512]{1,0:T(8,128)(2,1)S(1)} %weight_step.20), channel_id=1, source_target_pairs={{0,4},{1,5},{2,0},{3,1},{4,8},{5,9},{6,2},{7,3},{8,12},{9,13},{10,... | collective-permute-start | bytes 786440 | tf_op jit(solution)/shard_map/ppermute | solution.py:549
  73.9 4.0 %collective-permute-done.14.refs_4_ = bf16[256,512]{1,0:T(8,128)(2,1)S(1)} collective-permute-done((bf16[256,512]{1,0:T(8,128)(2,1)S(1)}, bf16[256,512]{1,0:T(8,128)(2,1)S(1)}, u32[]{:S(2)}, u32[]{:S(2)}) %collective-permute-start.14) | collective-permute-done | bytes 262176 | tf_op jit(solution)/shard_map/ppermute | solution.py:552
  78.2 3.5 %back.1 = (bf16[128,4096]{1,0:T(8,128)(2,1)}, bf16[128,512]{1,0:T(8,128)(2,1)}) custom-call(f32[4,128,1024]{2,1,0:T(8,128)S(1)} %get-tuple-element.104.probs, bf16[4,1024,128]{2,1,0:T(8,128)(2,1)S(1)} %get-tuple-element.105.q_rot, bf16[4,128,128]{2,1,0:T(8,128)(2,1)S(1)} %get-tuple-element.106.k_rot, bf16[128,4096]{1,0:T(8,128)(2,1)S(1)} %bitcast.18, ...), custom_call_target="tpu_custom_call" | custom-call | flops 200000000 | bytes 1024 | tf_op jit(solution)/shard_map/back/pallas_call | solution.py:228
  82.2 0.5 collective-permute-start.21
  82.7 1.6 %collective-permute-start.22 = (bf16[256,512]{1,0:T(8,128)(2,1)S(1)}, bf16[256,512]{1,0:T(8,128)(2,1)S(1)}, u32[]{:S(2)}, u32[]{:S(2)}) collective-permute-start(bf16[256,512]{1,0:T(8,128)(2,1)S(1)} %weight_step.22), channel_id=1, source_target_pairs={{0,4},{1,5},{2,0},{3,1},{4,8},{5,9},{6,2},{7,3},{8,12},{9,13},{10,... | collective-permute-start | bytes 786440 | tf_op jit(solution)/shard_map/ppermute | solution.py:549
  85.0 1.6 %collective-permute-start.28 = (bf16[256,512]{1,0:T(8,128)(2,1)S(1)}, bf16[256,512]{1,0:T(8,128)(2,1)S(1)}, u32[]{:S(2)}, u32[]{:S(2)}) collective-permute-start(bf16[256,512]{1,0:T(8,128)(2,1)S(1)} %weight_step.24), channel_id=1, source_target_pairs={{0,4},{1,5},{2,0},{3,1},{4,8},{5,9},{6,2},{7,3},{8,12},{9,13},{10,... | collective-permute-start | bytes 786440 | tf_op jit(solution)/shard_map/ppermute | solution.py:549
  86.6 7.8 %collective-permute-done.24.refs_4_ = bf16[256,512]{1,0:T(8,128)(2,1)S(1)} collective-permute-done((bf16[256,512]{1,0:T(8,128)(2,1)S(1)}, bf16[256,512]{1,0:T(8,128)(2,1)S(1)}, u32[]{:S(2)}, u32[]{:S(2)}) %collective-permute-start.24) | collective-permute-done | bytes 262176 | tf_op jit(solution)/shard_map/ppermute | solution.py:552
  95.2 1.3 %collective-permute-start.31 = (bf16[128,1536]{1,0:T(8,128)(2,1)S(1)}, bf16[128,1536]{1,0:T(8,128)(2,1)S(1)}, u32[]{:S(2)}, u32[]{:S(2)}) collective-permute-start(bf16[128,1536]{1,0:T(8,128)(2,1)S(1)} %get-tuple-element.176), channel_id=1, source_target_pairs={{16,1},{17,0},{18,3},{19,2},{20,5},{21,4},{22,7},{23,6},{24,9},{25... | collective-permute-start | bytes 1179656 | tf_op jit(solution)/shard_map/ppermute | solution.py:561
  96.7 1.6 %collective-permute-start.27 = (bf16[256,512]{1,0:T(8,128)(2,1)S(1)}, bf16[256,512]{1,0:T(8,128)(2,1)S(1)}, u32[]{:S(2)}, u32[]{:S(2)}) collective-permute-start(bf16[256,512]{1,0:T(8,128)(2,1)S(1)} %weight_step.26), channel_id=1, source_target_pairs={{0,4},{1,5},{2,0},{3,1},{4,8},{5,9},{6,2},{7,3},{8,12},{9,13},{10,... | collective-permute-start | bytes 786440 | tf_op jit(solution)/shard_map/ppermute | solution.py:549
  99.1 2.0 %collective-permute-done.29.low_b = bf16[256,512]{1,0:T(8,128)(2,1)S(1)} collective-permute-done((bf16[256,512]{1,0:T(8,128)(2,1)S(1)}, bf16[256,512]{1,0:T(8,128)(2,1)S(1)}, u32[]{:S(2)}, u32[]{:S(2)}) %collective-permute-start.29) | collective-permute-done | bytes 262176 | tf_op jit(solution)/shard_map/ppermute | solution.py:552
  101.1 1.3 %collective-permute-start.30 = (bf16[128,1024]{1,0:T(8,128)(2,1)S(1)}, bf16[128,1024]{1,0:T(8,128)(2,1)S(1)}, u32[]{:S(2)}, u32[]{:S(2)}) collective-permute-start(bf16[128,1024]{1,0:T(8,128)(2,1)S(1)} %get-tuple-element.185), channel_id=1, source_target_pairs={{16,1},{17,0},{18,3},{19,2},{20,5},{21,4},{22,7},{23,6},{24,9},{25... | collective-permute-start | bytes 786440 | tf_op jit(solution)/shard_map/ppermute | solution.py:561
  102.4 1.7 %early_blocks.1.base = bf16[128,8192]{1,0:T(8,128)(2,1)} custom-call(s32[17]{0:T(128)S(1)} %pad_add_fusion.where, bf16[3,128,512]{2,1,0:T(8,128)(2,1)S(1)} %collective-permute-done.9.ones, bf16[3,128,512]{2,1,0:T(8,128)(2,1)S(1)} %collective-permute-done.12.twos, bf16[3,128,512]{2,1,0:T(8,128)(2,1)S(1)} %collective-permute-done.6.raw_m, ...), custom_call_target="tpu_custom_call" | custom-call | flops 200000000 | bytes 1024 | tf_op jit(solution)/shard_map/early_blocks/pallas_call | solution.py:443
  104.1 0.9 collective-permute-done.26.high_f
  105.1 1.2 %weight_last.1 = bf16[512,512]{1,0:T(8,128)(2,1)} custom-call(bf16[8,128,512]{2,1,0:T(8,128)(2,1)S(1)} %copy-done.1, bf16[8,128,512]{2,1,0:T(8,128)(2,1)S(1)} %copy-done.3, bf16[128,512]{1,0:T(8,128)(2,1)S(1)} %get-tuple-element.190.refs_0_.refs_2_.refs_5_.vgs, bf16[128,512]{1,0:T(8,128)(2,1)S(1)} %collective-permute-done.4.refs_1_.refs_3_.refs_6_.vgs_t, ...), custom_call_target="tpu_custom_call" | custom-call | flops 200000000 | bytes 1024 | tf_op jit(solution)/shard_map/weight_last/pallas_call | solution.py:403
  106.2 1.3 %collective-permute-done.31.refs_0_ = bf16[128,1536]{1,0:T(8,128)(2,1)S(1)} collective-permute-done((bf16[128,1536]{1,0:T(8,128)(2,1)S(1)}, bf16[128,1536]{1,0:T(8,128)(2,1)S(1)}, u32[]{:S(2)}, u32[]{:S(2)}) %collective-permute-start.31) | collective-permute-done | bytes 393248 | tf_op jit(solution)/shard_map/ppermute | solution.py:561
  107.5 5.6 %collective-permute-done.30.refs_1_ = bf16[128,1024]{1,0:T(8,128)(2,1)S(1)} collective-permute-done((bf16[128,1024]{1,0:T(8,128)(2,1)S(1)}, bf16[128,1024]{1,0:T(8,128)(2,1)S(1)}, u32[]{:S(2)}, u32[]{:S(2)}) %collective-permute-start.30) | collective-permute-done | bytes 262176 | tf_op jit(solution)/shard_map/ppermute | solution.py:561
  113.1 1.4 %join.1 = bf16[128,8192]{1,0:T(8,128)(2,1)} custom-call(s32[17]{0:T(128)S(1)} %pad_add_fusion.where, bf16[128,8192]{1,0:T(8,128)(2,1)} %early_blocks.1.base, bf16[128,1536]{1,0:T(8,128)(2,1)S(1)} %collective-permute-done.31.refs_0_, bf16[128,1024]{1,0:T(8,128)(2,1)S(1)} %collective-permute-done.30.refs_1_), custom_call_target="tpu_custom_call", output_to_operand_aliasing={{}: (1, {})} | custom-call | flops 200000000 | bytes 1024 | tf_op jit(solution)/shard_map/join/pallas_call | solution.py:479
  (89 shorter events, 9.4 us)
Async XLA Ops:
  0.6 15.2 %collective-permute-start.1 = (bf16[512,512]{1,0:T(8,128)(2,1)}, bf16[512,512]{1,0:T(8,128)(2,1)S(1)}, u32[]{:S(2)}, u32[]{:S(2)}) collective-permute-start(bf16[512,512]{1,0:T(8,128)(2,1)} %bitcast.19), channel_id=1, source_target_pairs={{0,4},{1,5},{2,0},{3,1},{4,8},{5,9},{6,2},{7,3},{8,12},{9,13},{10,... | collective-permute-start | bytes 1572872 | tf_op jit(solution)/shard_map/ppermute | solution.py:549
  3.7 13.9 %collective-permute-start = (bf16[512,512]{1,0:T(8,128)(2,1)}, bf16[512,512]{1,0:T(8,128)(2,1)S(1)}, u32[]{:S(2)}, u32[]{:S(2)}) collective-permute-start(bf16[512,512]{1,0:T(8,128)(2,1)} %bitcast.20), channel_id=1, source_target_pairs={{0,2},{1,3},{2,6},{3,7},{4,0},{5,1},{6,10},{7,11},{8,4},{9,5},{10,... | collective-permute-start | bytes 1572872 | tf_op jit(solution)/shard_map/ppermute | solution.py:552
  4.5 1.6 %copy-start.4 = (bf16[1,128,8192]{2,1,0:T(8,128)(2,1)S(1)}, bf16[1,128,8192]{2,1,0:T(8,128)(2,1)}, u32[]{:S(2)}) copy-start(bf16[1,128,8192]{2,1,0:T(8,128)(2,1)} %param.8) | copy-start | bytes 6291460
  6.1 2.9 %copy-start.7 = (bf16[10,8192]{1,0:T(8,128)(2,1)S(1)}, bf16[10,8192]{1,0:T(8,128)(2,1)}, u32[]{:S(2)}) copy-start(bf16[10,8192]{1,0:T(8,128)(2,1)} %gain_t.1) | copy-start | bytes 491524
  7.5 3.9 %copy-start.10 = (s32[1,128]{1,0:T(1,128)S(1)}, s32[1,128]{1,0:T(1,128)}, u32[]{:S(2)}) copy-start(s32[1,128]{1,0:T(1,128)} %param.11) | copy-start | bytes 1540
  7.5 4.4 %copy-start.5 = (bf16[1,128,4096]{2,1,0:T(8,128)(2,1)S(1)}, bf16[1,128,4096]{2,1,0:T(8,128)(2,1)}, u32[]{:S(2)}) copy-start(bf16[1,128,4096]{2,1,0:T(8,128)(2,1)} %param.15) | copy-start | bytes 3145732
  7.5 4.4 %copy-start.8 = (bf16[1,128,4096]{2,1,0:T(8,128)(2,1)S(1)}, bf16[1,128,4096]{2,1,0:T(8,128)(2,1)}, u32[]{:S(2)}) copy-start(bf16[1,128,4096]{2,1,0:T(8,128)(2,1)} %param.12) | copy-start | bytes 3145732
  7.5 4.4 %copy-start.9 = (bf16[1,128,512]{2,1,0:T(8,128)(2,1)S(1)}, bf16[1,128,512]{2,1,0:T(8,128)(2,1)}, u32[]{:S(2)}) copy-start(bf16[1,128,512]{2,1,0:T(8,128)(2,1)} %param.13) | copy-start | bytes 393220
  7.5 12.6 %collective-permute-start.6 = (bf16[3,128,512]{2,1,0:T(8,128)(2,1)S(1)}, bf16[3,128,512]{2,1,0:T(8,128)(2,1)S(1)}, u32[]{:S(2)}, u32[]{:S(2)}) collective-permute-start(bf16[3,128,512]{2,1,0:T(8,128)(2,1)S(1)} %get-tuple-element.99), channel_id=1, source_target_pairs={{16,0},{17,1},{18,2},{19,3},{20,4},{21,5},{22,6},{23,7},{24,8},{25... | collective-permute-start | bytes 1179656 | tf_op jit(solution)/shard_map/ppermute | solution.py:558
  11.3 47.8 %copy-start = (bf16[8,128,512]{2,1,0:T(8,128)(2,1)}, bf16[8,128,512]{2,1,0:T(8,128)(2,1)S(1)}, u32[]{:S(2)}) copy-start(bf16[8,128,512]{2,1,0:T(8,128)(2,1)S(1)} %get-tuple-element.181.refs_0_.mine) | copy-start | bytes 3145732
  11.3 6.5 %collective-permute-start.5 = (bf16[8,128,512]{2,1,0:T(8,128)(2,1)S(1)}, bf16[8,128,512]{2,1,0:T(8,128)(2,1)S(1)}, u32[]{:S(2)}, u32[]{:S(2)}) collective-permute-start(bf16[8,128,512]{2,1,0:T(8,128)(2,1)S(1)} %get-tuple-element.111), channel_id=1, source_target_pairs={{0,1},{1,0},{2,3},{3,2},{4,5},{5,4},{6,7},{7,6},{8,9},{9,8},{10,11... | collective-permute-start | bytes 3145736 | tf_op jit(solution)/shard_map/ppermute | solution.py:555
  14.6 3.2 %collective-permute-start.4 = (bf16[128,512]{1,0:T(8,128)(2,1)S(1)}, bf16[128,512]{1,0:T(8,128)(2,1)S(1)}, u32[]{:S(2)}, u32[]{:S(2)}) collective-permute-start(bf16[128,512]{1,0:T(8,128)(2,1)S(1)} %get-tuple-element.190.refs_0_.refs_2_.refs_5_.vgs), channel_id=1, source_target_pairs={{0,1},{1,0},{2,3},{3,2},{4,5},{5,4},{6,7},{7,6},{8,9},{9,8},{10,11... | collective-permute-start | bytes 393224 | tf_op jit(solution)/shard_map/ppermute | solution.py:555
  15.2 2.6 %copy-start.6 = (bf16[1,512,512]{2,1,0:T(8,128)(2,1)S(1)}, bf16[1,512,512]{2,1,0:T(8,128)(2,1)}, u32[]{:S(2)}) copy-start(bf16[1,512,512]{2,1,0:T(8,128)(2,1)} %param.14) | copy-start | bytes 1572868
  15.8 13.6 %collective-permute-start.3 = (bf16[512,512]{1,0:T(8,128)(2,1)S(1)}, bf16[512,512]{1,0:T(8,128)(2,1)S(1)}, u32[]{:S(2)}, u32[]{:S(2)}) collective-permute-start(bf16[512,512]{1,0:T(8,128)(2,1)S(1)} %collective-permute-done.1.refs_5_.refs_3_), channel_id=1, source_target_pairs={{0,4},{1,5},{2,0},{3,1},{4,8},{5,9},{6,2},{7,3},{8,12},{9,13},{10,... | collective-permute-start | bytes 1572872 | tf_op jit(solution)/shard_map/ppermute | solution.py:549
  17.6 13.6 %collective-permute-start.2 = (bf16[512,512]{1,0:T(8,128)(2,1)S(1)}, bf16[512,512]{1,0:T(8,128)(2,1)S(1)}, u32[]{:S(2)}, u32[]{:S(2)}) collective-permute-start(bf16[512,512]{1,0:T(8,128)(2,1)S(1)} %collective-permute-done.refs_4_), channel_id=1, source_target_pairs={{0,2},{1,3},{2,6},{3,7},{4,0},{5,1},{6,10},{7,11},{8,4},{9,5},{10,... | collective-permute-start | bytes 1572872 | tf_op jit(solution)/shard_map/ppermute | solution.py:552
  17.8 41.3 %copy-start.2 = (bf16[8,128,512]{2,1,0:T(8,128)(2,1)}, bf16[8,128,512]{2,1,0:T(8,128)(2,1)S(1)}, u32[]{:S(2)}) copy-start(bf16[8,128,512]{2,1,0:T(8,128)(2,1)S(1)} %collective-permute-done.5.refs_1_.theirs) | copy-start | bytes 3145732
  20.1 11.5 %collective-permute-start.9 = (bf16[3,128,512]{2,1,0:T(8,128)(2,1)S(1)}, bf16[3,128,512]{2,1,0:T(8,128)(2,1)S(1)}, u32[]{:S(2)}, u32[]{:S(2)}) collective-permute-start(bf16[3,128,512]{2,1,0:T(8,128)(2,1)S(1)} %get-tuple-element.118), channel_id=1, source_target_pairs={{16,0},{17,1},{18,2},{19,3},{20,4},{21,5},{22,6},{23,7},{24,8},{25... | collective-permute-start | bytes 1179656 | tf_op jit(solution)/shard_map/ppermute | solution.py:558
  29.4 12.7 %collective-permute-start.8 = (bf16[512,512]{1,0:T(8,128)(2,1)S(1)}, bf16[512,512]{1,0:T(8,128)(2,1)S(1)}, u32[]{:S(2)}, u32[]{:S(2)}) collective-permute-start(bf16[512,512]{1,0:T(8,128)(2,1)S(1)} %collective-permute-done.3.refs_2_.refs_8_), channel_id=1, source_target_pairs={{0,4},{1,5},{2,0},{3,1},{4,8},{5,9},{6,2},{7,3},{8,12},{9,13},{10,... | collective-permute-start | bytes 1572872 | tf_op jit(solution)/shard_map/ppermute | solution.py:549
  31.2 12.4 %collective-permute-start.7 = (bf16[512,512]{1,0:T(8,128)(2,1)S(1)}, bf16[512,512]{1,0:T(8,128)(2,1)S(1)}, u32[]{:S(2)}, u32[]{:S(2)}) collective-permute-start(bf16[512,512]{1,0:T(8,128)(2,1)S(1)} %collective-permute-done.2.refs_3_.refs_9_), channel_id=1, source_target_pairs={{0,2},{1,3},{2,6},{3,7},{4,0},{5,1},{6,10},{7,11},{8,4},{9,5},{10,... | collective-permute-start | bytes 1572872 | tf_op jit(solution)/shard_map/ppermute | solution.py:552
  31.7 14.1 %collective-permute-start.12 = (bf16[3,128,512]{2,1,0:T(8,128)(2,1)S(1)}, bf16[3,128,512]{2,1,0:T(8,128)(2,1)S(1)}, u32[]{:S(2)}, u32[]{:S(2)}) collective-permute-start(bf16[3,128,512]{2,1,0:T(8,128)(2,1)S(1)} %get-tuple-element.125), channel_id=1, source_target_pairs={{16,1},{17,0},{18,3},{19,2},{20,5},{21,4},{22,7},{23,6},{24,9},{25... | collective-permute-start | bytes 1179656 | tf_op jit(solution)/shard_map/ppermute | solution.py:561
  43.6 6.4 %collective-permute-start.11 = (bf16[256,512]{1,0:T(8,128)(2,1)S(1)}, bf16[256,512]{1,0:T(8,128)(2,1)S(1)}, u32[]{:S(2)}, u32[]{:S(2)}) collective-permute-start(bf16[256,512]{1,0:T(8,128)(2,1)S(1)} %slice.17), channel_id=1, source_target_pairs={{0,4},{1,5},{2,0},{3,1},{4,8},{5,9},{6,2},{7,3},{8,12},{9,13},{10,... | collective-permute-start | bytes 786440 | tf_op jit(solution)/shard_map/ppermute | solution.py:549
  45.3 6.4 %collective-permute-start.10 = (bf16[256,512]{1,0:T(8,128)(2,1)S(1)}, bf16[256,512]{1,0:T(8,128)(2,1)S(1)}, u32[]{:S(2)}, u32[]{:S(2)}) collective-permute-start(bf16[256,512]{1,0:T(8,128)(2,1)S(1)} %slice.16), channel_id=1, source_target_pairs={{0,2},{1,3},{2,6},{3,7},{4,0},{5,1},{6,10},{7,11},{8,4},{9,5},{10,... | collective-permute-start | bytes 786440 | tf_op jit(solution)/shard_map/ppermute | solution.py:552
  52.3 19.8 %collective-permute-start.15 = (bf16[256,512]{1,0:T(8,128)(2,1)S(1)}, bf16[256,512]{1,0:T(8,128)(2,1)S(1)}, u32[]{:S(2)}, u32[]{:S(2)}) collective-permute-start(bf16[256,512]{1,0:T(8,128)(2,1)S(1)} %weight_step.16), channel_id=1, source_target_pairs={{0,4},{1,5},{2,0},{3,1},{4,8},{5,9},{6,2},{7,3},{8,12},{9,13},{10,... | collective-permute-start | bytes 786440 | tf_op jit(solution)/shard_map/ppermute | solution.py:549
  53.9 14.0 %collective-permute-start.17 = (bf16[256,512]{1,0:T(8,128)(2,1)S(1)}, bf16[256,512]{1,0:T(8,128)(2,1)S(1)}, u32[]{:S(2)}, u32[]{:S(2)}) collective-permute-start(bf16[256,512]{1,0:T(8,128)(2,1)S(1)} %weight_step.15), channel_id=1, source_target_pairs={{0,2},{1,3},{2,6},{3,7},{4,0},{5,1},{6,10},{7,11},{8,4},{9,5},{10,... | collective-permute-start | bytes 786440 | tf_op jit(solution)/shard_map/ppermute | solution.py:552
  54.4 11.8 %collective-permute-start.18 = (bf16[256,512]{1,0:T(8,128)(2,1)S(1)}, bf16[256,512]{1,0:T(8,128)(2,1)S(1)}, u32[]{:S(2)}, u32[]{:S(2)}) collective-permute-start(bf16[256,512]{1,0:T(8,128)(2,1)S(1)} %weight_step.14), channel_id=1, source_target_pairs={{0,4},{1,5},{2,0},{3,1},{4,8},{5,9},{6,2},{7,3},{8,12},{9,13},{10,... | collective-permute-start | bytes 786440 | tf_op jit(solution)/shard_map/ppermute | solution.py:549
  55.9 10.2 %collective-permute-start.16 = (bf16[3,128,512]{2,1,0:T(8,128)(2,1)}, bf16[3,128,512]{2,1,0:T(8,128)(2,1)S(1)}, u32[]{:S(2)}, u32[]{:S(2)}) collective-permute-start(bf16[3,128,512]{2,1,0:T(8,128)(2,1)} %get-tuple-element.133), channel_id=1, source_target_pairs={{16,0},{17,1},{18,2},{19,3},{20,4},{21,5},{22,6},{23,7},{24,8},{25... | collective-permute-start | bytes 1179656 | tf_op jit(solution)/shard_map/ppermute | solution.py:558
  57.2 1.9 %collective-permute-start.13 = (f32[128,896]{1,0:T(8,128)S(1)}, f32[128,896]{1,0:T(8,128)S(1)}, u32[]{:S(2)}, u32[]{:S(2)}) collective-permute-start(f32[128,896]{1,0:T(8,128)S(1)} %get-tuple-element.142.refs_6_), channel_id=1, source_target_pairs={{0,1},{1,0},{2,3},{3,2},{4,5},{5,4},{6,7},{7,6},{8,9},{9,8},{10,11... | collective-permute-start | bytes 1376264 | tf_op jit(solution)/shard_map/ppermute | solution.py:555
  66.2 1.2 %copy-start.1 = (bf16[8,128,512]{2,1,0:T(8,128)(2,1)S(1)}, bf16[8,128,512]{2,1,0:T(8,128)(2,1)}, u32[]{:S(2)}) copy-start(bf16[8,128,512]{2,1,0:T(8,128)(2,1)} %copy-done) | copy-start | bytes 3145732
  66.2 1.5 %copy-start.3 = (bf16[8,128,512]{2,1,0:T(8,128)(2,1)S(1)}, bf16[8,128,512]{2,1,0:T(8,128)(2,1)}, u32[]{:S(2)}) copy-start(bf16[8,128,512]{2,1,0:T(8,128)(2,1)} %copy-done.2) | copy-start | bytes 3145732
  68.2 13.7 %collective-permute-start.19 = (bf16[256,512]{1,0:T(8,128)(2,1)S(1)}, bf16[256,512]{1,0:T(8,128)(2,1)S(1)}, u32[]{:S(2)}, u32[]{:S(2)}) collective-permute-start(bf16[256,512]{1,0:T(8,128)(2,1)S(1)} %weight_step.19), channel_id=1, source_target_pairs={{0,2},{1,3},{2,6},{3,7},{4,0},{5,1},{6,10},{7,11},{8,4},{9,5},{10,... | collective-permute-start | bytes 786440 | tf_op jit(solution)/shard_map/ppermute | solution.py:552
  68.7 13.0 %collective-permute-start.20 = (bf16[256,512]{1,0:T(8,128)(2,1)S(1)}, bf16[256,512]{1,0:T(8,128)(2,1)S(1)}, u32[]{:S(2)}, u32[]{:S(2)}) collective-permute-start(bf16[256,512]{1,0:T(8,128)(2,1)S(1)} %weight_step.18), channel_id=1, source_target_pairs={{0,4},{1,5},{2,0},{3,1},{4,8},{5,9},{6,2},{7,3},{8,12},{9,13},{10,... | collective-permute-start | bytes 786440 | tf_op jit(solution)/shard_map/ppermute | solution.py:549
  70.3 7.7 %collective-permute-start.14 = (bf16[256,512]{1,0:T(8,128)(2,1)S(1)}, bf16[256,512]{1,0:T(8,128)(2,1)S(1)}, u32[]{:S(2)}, u32[]{:S(2)}) collective-permute-start(bf16[256,512]{1,0:T(8,128)(2,1)S(1)} %weight_step.17), channel_id=1, source_target_pairs={{0,2},{1,3},{2,6},{3,7},{4,0},{5,1},{6,10},{7,11},{8,4},{9,5},{10,... | collective-permute-start | bytes 786440 | tf_op jit(solution)/shard_map/ppermute | solution.py:552
  70.7 24.4 %collective-permute-start.23 = (bf16[128,2688]{1,0:T(8,128)(2,1)S(1)}, bf16[128,2688]{1,0:T(8,128)(2,1)S(1)}, u32[]{:S(2)}, u32[]{:S(2)}) collective-permute-start(bf16[128,2688]{1,0:T(8,128)(2,1)S(1)} %get-tuple-element.150), channel_id=1, source_target_pairs={{16,0},{17,1},{18,2},{19,3},{20,4},{21,5},{22,6},{23,7},{24,8},{25... | collective-permute-start | bytes 2064392 | tf_op jit(solution)/shard_map/ppermute | solution.py:558
  72.3 12.5 %collective-permute-start.25 = (bf16[256,512]{1,0:T(8,128)(2,1)S(1)}, bf16[256,512]{1,0:T(8,128)(2,1)S(1)}, u32[]{:S(2)}, u32[]{:S(2)}) collective-permute-start(bf16[256,512]{1,0:T(8,128)(2,1)S(1)} %weight_step.20), channel_id=1, source_target_pairs={{0,4},{1,5},{2,0},{3,1},{4,8},{5,9},{6,2},{7,3},{8,12},{9,13},{10,... | collective-permute-start | bytes 786440 | tf_op jit(solution)/shard_map/ppermute | solution.py:549
  82.2 16.1 %collective-permute-start.21 = (bf16[256,512]{1,0:T(8,128)(2,1)S(1)}, bf16[256,512]{1,0:T(8,128)(2,1)S(1)}, u32[]{:S(2)}, u32[]{:S(2)}) collective-permute-start(bf16[256,512]{1,0:T(8,128)(2,1)S(1)} %weight_step.23), channel_id=1, source_target_pairs={{0,2},{1,3},{2,6},{3,7},{4,0},{5,1},{6,10},{7,11},{8,4},{9,5},{10,... | collective-permute-start | bytes 786440 | tf_op jit(solution)/shard_map/ppermute | solution.py:552
  82.7 13.7 %collective-permute-start.22 = (bf16[256,512]{1,0:T(8,128)(2,1)S(1)}, bf16[256,512]{1,0:T(8,128)(2,1)S(1)}, u32[]{:S(2)}, u32[]{:S(2)}) collective-permute-start(bf16[256,512]{1,0:T(8,128)(2,1)S(1)} %weight_step.22), channel_id=1, source_target_pairs={{0,4},{1,5},{2,0},{3,1},{4,8},{5,9},{6,2},{7,3},{8,12},{9,13},{10,... | collective-permute-start | bytes 786440 | tf_op jit(solution)/shard_map/ppermute | solution.py:549
  84.3 10.1 %collective-permute-start.24 = (bf16[256,512]{1,0:T(8,128)(2,1)S(1)}, bf16[256,512]{1,0:T(8,128)(2,1)S(1)}, u32[]{:S(2)}, u32[]{:S(2)}) collective-permute-start(bf16[256,512]{1,0:T(8,128)(2,1)S(1)} %weight_step.21), channel_id=1, source_target_pairs={{0,2},{1,3},{2,6},{3,7},{4,0},{5,1},{6,10},{7,11},{8,4},{9,5},{10,... | collective-permute-start | bytes 786440 | tf_op jit(solution)/shard_map/ppermute | solution.py:552
  85.0 16.1 %collective-permute-start.28 = (bf16[256,512]{1,0:T(8,128)(2,1)S(1)}, bf16[256,512]{1,0:T(8,128)(2,1)S(1)}, u32[]{:S(2)}, u32[]{:S(2)}) collective-permute-start(bf16[256,512]{1,0:T(8,128)(2,1)S(1)} %weight_step.24), channel_id=1, source_target_pairs={{0,4},{1,5},{2,0},{3,1},{4,8},{5,9},{6,2},{7,3},{8,12},{9,13},{10,... | collective-permute-start | bytes 786440 | tf_op jit(solution)/shard_map/ppermute | solution.py:549
  94.7 6.4 %collective-permute-start.29 = (bf16[256,512]{1,0:T(8,128)(2,1)S(1)}, bf16[256,512]{1,0:T(8,128)(2,1)S(1)}, u32[]{:S(2)}, u32[]{:S(2)}) collective-permute-start(bf16[256,512]{1,0:T(8,128)(2,1)S(1)} %weight_step.25), channel_id=1, source_target_pairs={{0,2},{1,3},{2,6},{3,7},{4,0},{5,1},{6,10},{7,11},{8,4},{9,5},{10,... | collective-permute-start | bytes 786440 | tf_op jit(solution)/shard_map/ppermute | solution.py:552
  95.2 12.3 %collective-permute-start.31 = (bf16[128,1536]{1,0:T(8,128)(2,1)S(1)}, bf16[128,1536]{1,0:T(8,128)(2,1)S(1)}, u32[]{:S(2)}, u32[]{:S(2)}) collective-permute-start(bf16[128,1536]{1,0:T(8,128)(2,1)S(1)} %get-tuple-element.176), channel_id=1, source_target_pairs={{16,1},{17,0},{18,3},{19,2},{20,5},{21,4},{22,7},{23,6},{24,9},{25... | collective-permute-start | bytes 1179656 | tf_op jit(solution)/shard_map/ppermute | solution.py:561
  96.7 7.4 %collective-permute-start.27 = (bf16[256,512]{1,0:T(8,128)(2,1)S(1)}, bf16[256,512]{1,0:T(8,128)(2,1)S(1)}, u32[]{:S(2)}, u32[]{:S(2)}) collective-permute-start(bf16[256,512]{1,0:T(8,128)(2,1)S(1)} %weight_step.26), channel_id=1, source_target_pairs={{0,4},{1,5},{2,0},{3,1},{4,8},{5,9},{6,2},{7,3},{8,12},{9,13},{10,... | collective-permute-start | bytes 786440 | tf_op jit(solution)/shard_map/ppermute | solution.py:549
  98.6 6.4 %collective-permute-start.26 = (bf16[256,512]{1,0:T(8,128)(2,1)S(1)}, bf16[256,512]{1,0:T(8,128)(2,1)S(1)}, u32[]{:S(2)}, u32[]{:S(2)}) collective-permute-start(bf16[256,512]{1,0:T(8,128)(2,1)S(1)} %weight_step.27), channel_id=1, source_target_pairs={{0,2},{1,3},{2,6},{3,7},{4,0},{5,1},{6,10},{7,11},{8,4},{9,5},{10,... | collective-permute-start | bytes 786440 | tf_op jit(solution)/shard_map/ppermute | solution.py:552
  101.1 12.0 %collective-permute-start.30 = (bf16[128,1024]{1,0:T(8,128)(2,1)S(1)}, bf16[128,1024]{1,0:T(8,128)(2,1)S(1)}, u32[]{:S(2)}, u32[]{:S(2)}) collective-permute-start(bf16[128,1024]{1,0:T(8,128)(2,1)S(1)} %get-tuple-element.185), channel_id=1, source_target_pairs={{16,1},{17,0},{18,3},{19,2},{20,5},{21,4},{22,7},{23,6},{24,9},{25... | collective-permute-start | bytes 786440 | tf_op jit(solution)/shard_map/ppermute | solution.py:561

commit v3 on v2

--- a/solution.py
+++ b/solution.py
@@ -15,7 +15,7 @@
 EPS = 1e-05
 F32 = jnp.float32
 BF16 = jnp.bfloat16
-VMEM_LIMIT = 48 * 1024 * 1024
+VMEM_LIMIT = 20 * 1024 * 1024
 
 
 def cost(us):
@@ -23,11 +23,7 @@
 
 
 SMALL = cost(0.2)
-STAGE = 3.0
-SWAP = 12.0
-PACKED = 6.0
-RING = 6.0
-LITTLE = 1.0
+H = [12.0, 9.0, 1.5, 1.5, 1.5, 6.0, 3.0, 6.0]
 
 
 def params(**more):
@@ -194,9 +190,9 @@
             head,
         ],
         out_shape=[
-            sds((HK, tokens, SHARE * tokens), F32),
-            sds((HK, SHARE * tokens, HD), BF16),
-            sds((HK, tokens, HD), BF16),
+            pltpu.HBM((HK, tokens, SHARE * tokens), F32),
+            pltpu.HBM((HK, SHARE * tokens, HD), BF16),
+            pltpu.HBM((HK, tokens, HD), BF16),
             sds((tokens, HK * HD), BF16),
         ],
         compiler_params=params(),
@@ -347,21 +343,19 @@
     for part, w in zip(parts, weights, strict=True):
         r, at = part[0], span(part, rows)
         n = blocks.index(r)
-        share, i = (0, n) if n < len(shares[0]) else (1, n - len(shares[0]))
-        at_m = slice(n * rows + at.start, n * rows + at.stop)
-        at_t = slice(i * rows + at.start, i * rows + at.stop)
+        to = slice(n * rows + at.start, n * rows + at.stop)
         g = gain[r][:, at]
         over = 1.0 / g
         product = mm(left, w[...], (1, 1))
         h_m, h_t = features(mine, part).astype(F32), features(theirs, part).astype(F32)
-        outs[0][:, at_m] = (product[:tokens] * g - h_m * over * c_m[:, at]).astype(BF16)
-        outs[1 + share][:, at_t] = (product[tokens:] * g - h_t * over * c_t[:, at]).astype(BF16)
+        outs[0][:, to] = (product[:tokens] * g - h_m * over * c_m[:, at]).astype(BF16)
+        outs[1][:, to] = (product[tokens:] * g - h_t * over * c_t[:, at]).astype(BF16)
 
 
 def local_grads(mine, theirs, vgs, vgs_t, gain, inverse, own, got, shares, parts, weights, width):
     tokens, rows = mine.shape[1:]
-    wide = [len(share) * rows for share in shares]
-    out = [sds((tokens, w), BF16) for w in (sum(wide) + HD, *wide)]
+    wide = sum(len(share) for share in shares) * rows
+    out = [sds((tokens, wide + HD), BF16), sds((tokens, wide), BF16)]
     return pl.pallas_call(
         functools.partial(local_kernel, parts=parts, shares=shares, width=width),
         out_shape=out,
@@ -373,40 +367,40 @@
 
 def weight_kernel(*refs, part):
     mine, theirs, vgs, vgs_t = refs[:4]
-    right = both_vgs(vgs, vgs_t)
-    total = mm(pair(mine, theirs, part), right, (0, 0))
-    for arrived in refs[4:-1]:
-        total = total + arrived[...].astype(F32)
-    refs[-1][...] = total.astype(BF16)
-
-
-def weight_step(mine, theirs, vgs, vgs_t, part, arrived):
-    return pl.pallas_call(
-        functools.partial(weight_kernel, part=part),
-        out_shape=sds((mine.shape[2] // 2, vgs.shape[1]), BF16),
+    out = refs[-1]
+    total = mm(pair(mine, theirs, part), both_vgs(vgs, vgs_t), (0, 0))
+    rows = total.shape[0]
+    for side, arrived in enumerate(refs[4:-1]):
+        if arrived is None:
+            continue
+        if arrived.shape[0] == rows:
+            total = total + arrived[...].astype(F32)
+        elif side == 0:
+            total = jnp.concatenate([total[: rows // 2] + arrived[...].astype(F32), total[rows // 2 :]], axis=0)
+        else:
+            total = jnp.concatenate([total[: rows // 2], total[rows // 2 :] + arrived[...].astype(F32)], axis=0)
+    out[...] = total.astype(BF16)
+
+
+def weight_step(mine, theirs, vgs, vgs_t, part, from_behind=None, from_ahead=None):
+    at = span(part, mine.shape[2])
+
+    def kernel(*refs):
+        refs = list(refs)
+        if from_behind is None:
+            refs.insert(4, None)
+        if from_ahead is None:
+            refs.insert(5, None)
+        weight_kernel(*refs, part=part)
+
+    arrived = [x for x in (from_behind, from_ahead) if x is not None]
+    return pl.pallas_call(
+        kernel,
+        out_shape=sds((at.stop - at.start, vgs.shape[1]), BF16),
         compiler_params=params(),
         cost_estimate=SMALL,
         name="weight_step",
     )(mine, theirs, vgs, vgs_t, *arrived)
-
-
-def weight_last_kernel(mine, theirs, vgs, vgs_t, low_f, low_b, high_f, high_b, pin, out):
-    right = both_vgs(vgs, vgs_t)
-    half = low_f.shape[0]
-    for side, (one, two) in enumerate(((low_f, low_b), (high_f, high_b))):
-        total = mm(pair(mine, theirs, (0, side)), right, (0, 0))
-        total = total + one[...].astype(F32) + two[...].astype(F32)
-        out[side * half : (side + 1) * half, :] = total.astype(BF16)
-
-
-def weight_last(mine, theirs, vgs, vgs_t, arrived, pin):
-    return pl.pallas_call(
-        weight_last_kernel,
-        out_shape=sds((mine.shape[2], vgs.shape[1]), BF16),
-        compiler_params=params(),
-        cost_estimate=SMALL,
-        name="weight_last",
-    )(mine, theirs, vgs, vgs_t, *arrived, pin)
 
 
 def copies_of(pieces, shares, where, out, sem, first, rows):
@@ -419,7 +413,7 @@
     return copies
 
 
-def early_kernel(where, ones, twos, raw_m, raw_t, second, *refs, soon, shares, chips, rows):
+def early_kernel(where, pin, ones, twos, raw_m, raw_t, second, *refs, soon, shares, chips, rows):
     pieces, (out, done, sem, sems) = refs[:-4], refs[-4:]
     copies = copies_of(pieces, shares, where, out, sem, 1, rows)
     for copy in copies:
@@ -437,7 +431,7 @@
         copy.wait()
 
 
-def early_blocks(where, ones, twos, raw_m, raw_t, pieces, soon, shares, chips, width):
+def early_blocks(where, pin, ones, twos, raw_m, raw_t, pieces, soon, shares, chips, width):
     _, tokens, rows = ones.shape
     somewhere = pl.BlockSpec(memory_space=pl.ANY)
     return pl.pallas_call(
@@ -445,6 +439,7 @@
         grid=(1,),
         in_specs=[
             pl.BlockSpec(memory_space=pltpu.SMEM),
+            somewhere,
             pl.BlockSpec(ones.shape, lambda i: (0, 0, 0)),
             pl.BlockSpec(twos.shape, lambda i: (0, 0, 0)),
             pl.BlockSpec(ones.shape, lambda i: (0, 0, 0)),
@@ -462,7 +457,7 @@
         compiler_params=params(),
         cost_estimate=SMALL,
         name="early_blocks",
-    )(where, ones, twos, raw_m, raw_t, pieces[0], *pieces)
+    )(where, pin, ones, twos, raw_m, raw_t, pieces[0], *pieces)
 
 
 def join_kernel(where, base, *refs, shares, chips, rows):
@@ -573,7 +568,7 @@
 
     pin = [jnp.zeros((8, HD), F32)]
 
-    def hold(us=STAGE):
+    def hold(us):
         pin[0] = then(fence(after(pin[0]), us))
 
     def parts_of(some):
@@ -583,19 +578,19 @@
         return [held[part] for part in parts]
 
     held = {(0, None): weight}
-    moving = {}
-
-    def gather_step(step):
-        if step > 1:
-            for r in (chips - step + 1, step - 1):
-                held[r, None] = after(moving.pop(r))
-        f, b = held[(chips - step + 1) % chips, None], held[step - 1, None]
-        if step < half:
-            moving[chips - step], moving[step] = ahead(f), behind(b)
-        else:
-            moving[0], moving[1] = ahead(f[low]), behind(b[high])
-
-    gather_step(1)
+    moving = {(chips - 1, None): ahead(weight), (1, None): behind(weight)}
+
+    def gather_next(step, side):
+        for r, back_r, half_side, move in ((chips - step, chips - step + 1, side, ahead), (step, step - 1, 1 - side, behind)):
+            if step == 2:
+                source = held[back_r, None][high if half_side else low]
+            else:
+                source = held[back_r, half_side]
+            moving[r, half_side] = move(source)
+
+    def gather_here(step, side):
+        for key in ((chips - step, side), (step, 1 - side)):
+            held[key] = after(moving.pop(key))
 
     last = last_layer(layer_counts, gain_table.shape[0])
     where = jnp.concatenate([last[None], order + core, order + 1 - core]).astype(jnp.int32)
@@ -608,93 +603,84 @@
         *attention_probs(queries[0], keys[0], out_grad[0], cosine, sine, after(inverse))
     )
     vgs_t = swapped(vgs)
-    hold(SWAP)
-    gather_step(2)
+    hold(H[0])
+    for key in ((chips - 1, None), (1, None)):
+        held[key] = after(moving.pop(key))
+    gather_next(2, 0)
     theirs, vgs_t = after(theirs), after(vgs_t)
     soon_gain = jnp.concatenate([gain[r : r + 1] for r in soon], axis=0)
     parts = parts_of(soon)
     one, two = then(*first_terms(after(vgs), vgs_t, soon_gain, [held[r, None] for r in soon]))
+    late = {r: after(held[r, None]) for r in (chips - 1, 1)}
+    moving[chips - 2, 1] = ahead(late[chips - 1][high])
+    moving[2, 0] = behind(late[1][low])
     raw_m = after(raw_m)
     one = sent_down(after(one))
     total = then(values_sum(after(mine), theirs, parts, weights(parts)))
-    hold(RING)
-    for step in range(3, half + 1):
-        gather_step(step)
-        if step == 3:
+    hold(H[1])
+    for step in range(2, half):
+        gather_here(step, 0)
+        if step + 1 <= half:
+            gather_next(step + 1, 0)
+        hold(H[2])
+        gather_here(step, 1)
+        if step + 1 < half:
+            gather_next(step + 1, 1)
+        if step == 2:
             one = after(one)
             two = sent_across(after(two))
-        if step < half:
-            parts = parts_of([step - 1, chips - step + 1])
+        if step < half - 1:
+            parts = parts_of([step, chips - step])
             total = then(values_sum(after(mine), theirs, parts, weights(parts), (total,)))
-            hold(RING)
-
-    chains = [
-        (0, ahead, list(range(half, 0, -1))),
-        (1, behind, list(range(half, chips))),
-        (1, ahead, list(range(half - 1, 0, -1))),
-        (0, behind, list(range(half + 1, chips))),
-    ]
-    arrived = [()] * 4
-    at = [0] * 4
-
-    def weight_turn(*which):
-        for i in which:
-            side, move, route = chains[i]
-            got = tuple(after(x) for x in arrived[i])
-            part = (route[at[i]], side)
-            total = then(weight_step(after(mine), theirs, vgs, vgs_t, part, got))
-            arrived[i] = (move(total),)
-            at[i] += 1
-
-    hold(RING)
+            hold(H[3])
+
+    def weight_part(part, *arrived):
+        return then(weight_step(after(mine), theirs, vgs, vgs_t, part, *arrived))
+
+    f = ahead(weight_part((half, 0)))
+    b = behind(weight_part((half, 1)))
     two = after(two)
     raw_t = sent_down(after(raw_t))
-    weight_turn(0, 1)
+    hold(H[4])
     parts = parts_of([half - 1, half + 1])
     total = then(values_sum(after(mine), theirs, parts, weights(parts), (total,)))
-    hold(LITTLE)
-    held[half, 0], held[half, 1] = after(moving[0]), after(moving[1])
+    for key in ((half, 0), (half, 1)):
+        held[key] = after(moving.pop(key))
     parts = parts_of([half])
     u_mine, packed = values_sum(after(mine), theirs, parts, weights(parts), (total,), (vgs, vgs_t, inverse))
-    then(packed)
-    got = swapped(packed)
-    weight_turn(2)
-    hold(PACKED)
+    got = swapped(then(packed))
+
+    def weight_turn(r, f, b):
+        f, b = after(f), after(b)
+        return ahead(weight_part((r, None), f)), behind(weight_part((chips - r, None), None, b))
+
+    if half > 2:
+        f, b = weight_turn(half - 1, f, b)
+    hold(H[5])
     got = after(got)
-    weight_turn(3)
     parts = parts_of(sum(later, []))
-    m, t1, t2 = then(
+    m, t = then(
         *local_grads(
             mine, theirs, after(vgs), vgs_t, gain, inverse, packed, got, later, parts, weights(parts), width
         )
     )
-    raw_t = after(raw_t)
-    m = sent_down(after(m))
-    hold()
-    weight_turn(0, 1)
-    hold()
-    weight_turn(2, 3)
+    m, t = sent_down(m), sent_across(t)
     query_grad, key_grad = then(
         *attention_back(probs, q_rot, k_rot, out_grad[0], after(u_mine), got, cosine, sine, inverse)
     )
-    for turn in range(2, half - 1):
-        hold()
-        weight_turn(0, 1)
-        hold()
-        weight_turn(2, 3)
-        if turn == 2:
-            m = after(m)
-            t1 = sent_across(after(t1))
-    hold()
-    weight_turn(0, 1)
-    last_low, last_high = after(arrived[3][0]), after(arrived[2][0])
-    t2 = sent_across(after(t2))
-    hold()
-    upstream = then(early_blocks(where, one, two, raw_m, raw_t, [after(m)], soon, [sum(later, [])], chips, width))
-    arrived = [after(arrived[0][0]), last_low, after(arrived[1][0]), last_high]
-    weight_grad = then(weight_last(mine, theirs, after(vgs), vgs_t, arrived, pin[0]))
-    t1, t2 = after(t1), after(t2)
-    upstream = then(join(where, after(upstream), [t1, t2], later, chips, rows))
+    hold(H[6])
+    for r in range(half - 2, 0, -1):
+        f, b = weight_turn(r, f, b)
+        if r == 2:
+            raw_t = after(raw_t)
+        hold(H[7])
+    upstream = then(
+        early_blocks(where, pin[0], one, two, raw_m, raw_t, [after(m)], soon, [sum(later, [])], chips, width)
+    )
+    t = after(t)
+    upstream = then(join(where, after(upstream), [t], [sum(later, [])], chips, rows))
+    f, b = after(f), after(b)
+    weight_grad = weight_step(mine, theirs, vgs, vgs_t, (0, None), f, b)
     return (query_grad[None], key_grad[None], weight_grad[None], upstream[None])
 
 

time: 115 us -> 93.2 us (0.81)
  waiting for transfers between devices: 52.7 us -> 37.3 us
  starting transfers between devices: 33.6 us -> 30.4 us
  Pallas kernels: 22.7 us -> 20.1 us
  local copies, waits for them, and re-layouts: 3.21 us -> 1.72 us
    ppermute x11 -> x10, waiting for transfers between devices: 17.8 us -> 9.5 us  [behind(): return lax.ppermute(x, 'dp', back)]
    ppermute x4, waiting for transfers between devices: 6.24 us -> 0.01 us  [sent_down(): return lax.ppermute(x, ('section', 'dp'), down)]
    ppermute x11 -> x10, waiting for transfers between devices: 20 us -> 26.2 us  [ahead(): return lax.ppermute(x, 'dp', forth)]
    ppermute x3 -> x2, waiting for transfers between devices: 6.91 us -> 1.49 us  [sent_across(): return lax.ppermute(x, ('section', 'dp'), cross)]
    ppermute x11 -> x10, starting transfers between devices: 19.5 us -> 16.4 us  [ahead(): return lax.ppermute(x, 'dp', forth)]
    ppermute x3, waiting for transfers between devices: 1.8 us -> 0.01 us  [swapped(): return lax.ppermute(x, 'dp', swap)]
    unnamed x22 -> x20, local copies, waits for them, and re-layouts: 3.17 us -> 1.64 us
    pallas_call x1, Pallas kernels: 2.49 us -> 0.96 us  [local_grads(): pl.pallas_call(functools.partial(local_kernel, parts=parts, shares=shares...]
  transfers between devices with their start and end apart: 32 -> 29, of which waited for: 16 -> 17; matrix products, arithmetic and copies ran while one was open for 0% -> 1% of each run, Pallas kernels for 18% -> 21%
where the time goes in v3:
time: 93.2 us; the launch traced here: 91.7 us
  waiting for transfers between devices  37.3 us (40%)
  starting transfers between devices  30.4 us (33%)
  Pallas kernels  20.1 us (22%)
  between operations  1.73 us (2%)
  local copies, waits for them, and re-layouts  1.72 us (2%)
    ppermute x10, waiting for transfers between devices, ahead(): return lax.ppermute(x, 'dp', forth)  26.2 us
    ppermute x10, starting transfers between devices, ahead(): return lax.ppermute(x, 'dp', forth)  16.4 us
    ppermute x10, waiting for transfers between devices, behind(): return lax.ppermute(x, 'dp', back)  9.5 us
    ppermute x10, starting transfers between devices, behind(): return lax.ppermute(x, 'dp', back)  5.53 us
    ppermute x4, starting transfers between devices, sent_down(): return lax.ppermute(x, ('section', 'dp'), down)  5.29 us
    pallas_call x9, Pallas kernels, weight_step(): pl.pallas_call(kernel, out_shape=sds((at.stop - at.start, vgs.shape[1]),...  3.56 us
    pallas_call x1, Pallas kernels, attention_back(): pl.pallas_call(back_kernel, grid=(HK,), in_specs=[pl.BlockSpec((1, tokens...  3.49 us
    pallas_call x1, Pallas kernels, attention_probs(): pl.pallas_call(probs_kernel, grid=(HK,), in_specs=[group, head, group, ta...  3.44 us
  transfers between devices with their start and end apart: 29, of which 17 were waited for; matrix products, arithmetic and copies ran while one was open for 1% of the time, Pallas kernels for 21%

profile of v3, /device:TPU:0, one launch (start us, length us, event | category | flops | bytes accessed | tf_op | source)
XLA Modules:
  0.0 91.7 jit_solution(14223300003915675898)
XLA Ops:
  0.6 3.1 %collective-permute-start.1 = (bf16[512,512]{1,0:T(8,128)(2,1)}, bf16[512,512]{1,0:T(8,128)(2,1)S(1)}, u32[]{:S(2)}, u32[]{:S(2)}) collective-permute-start(bf16[512,512]{1,0:T(8,128)(2,1)} %bitcast.19), channel_id=1, source_target_pairs={{0,4},{1,5},{2,0},{3,1},{4,8},{5,9},{6,2},{7,3},{8,12},{9,13},{10,... | collective-permute-start | bytes 1572872 | tf_op jit(solution)/shard_map/ppermute | solution.py:544
  4.5 1.6 %copy-done = bf16[1,128,8192]{2,1,0:T(8,128)(2,1)S(1)} copy-done((bf16[1,128,8192]{2,1,0:T(8,128)(2,1)S(1)}, bf16[1,128,8192]{2,1,0:T(8,128)(2,1)}, u32[]{:S(2)}) %copy-start) | copy-done | bytes 2097176
  6.1 0.7 pick.1
  6.9 1.4 %collective-permute-start.6 = (bf16[3,128,512]{2,1,0:T(8,128)(2,1)S(1)}, bf16[3,128,512]{2,1,0:T(8,128)(2,1)S(1)}, u32[]{:S(2)}, u32[]{:S(2)}) collective-permute-start(bf16[3,128,512]{2,1,0:T(8,128)(2,1)S(1)} %get-tuple-element.84), channel_id=1, source_target_pairs={{16,0},{17,1},{18,2},{19,3},{20,4},{21,5},{22,6},{23,7},{24,8},{25... | collective-permute-start | bytes 1179656 | tf_op jit(solution)/shard_map/ppermute | solution.py:553
  8.3 2.3 %prep.1 = (bf16[8,128,512]{2,1,0:T(8,128)(2,1)S(1)}, bf16[8,128,512]{2,1,0:T(8,128)(2,1)S(1)}, f32[8,1,512]{2,1,0:T(1,128)S(1)}, f32[128,128]{1,0:T(8,128)S(1)}) custom-call(s32[17]{0:T(128)S(1)} %pad_add_fusion.where, bf16[128,8192]{1,0:T(8,128)(2,1)S(1)} %bitcast.15, bf16[128,8192]{1,0:T(8,128)(2,1)S(1)} %bitcast.16, bf16[10,8192]{1,0:T(8,128)(2,1)S(1)} %copy-done.5, ...), custom_call_target="tpu_custom_call" | custom-call | flops 200000000 | bytes 1024 | tf_op jit(solution)/shard_map/prep/pallas_call | solution.py:89
  11.2 3.4 %probs.1 = (f32[4,128,1024]{2,1,0:T(8,128)}, bf16[4,1024,128]{2,1,0:T(8,128)(2,1)}, bf16[4,128,128]{2,1,0:T(8,128)(2,1)}, bf16[128,512]{1,0:T(8,128)(2,1)S(1)}) custom-call(bf16[128,4096]{1,0:T(8,128)(2,1)S(1)} %bitcast.23, bf16[128,512]{1,0:T(8,128)(2,1)S(1)} %bitcast.24, bf16[128,4096]{1,0:T(8,128)(2,1)S(1)} %bitcast.17, ...), custom_call_target="tpu_custom_call" | custom-call | flops 200000000 | bytes 1024 | tf_op jit(solution)/shard_map/probs/pallas_call | solution.py:182
  15.2 0.6 collective-permute-done.1.refs_5_.refs_3_
  15.8 1.5 %collective-permute-done.refs_4_ = bf16[512,512]{1,0:T(8,128)(2,1)S(1)} collective-permute-done((bf16[512,512]{1,0:T(8,128)(2,1)}, bf16[512,512]{1,0:T(8,128)(2,1)S(1)}, u32[]{:S(2)}, u32[]{:S(2)}) %collective-permute-start) | collective-permute-done | bytes 524320 | tf_op jit(solution)/shard_map/ppermute | solution.py:547
  17.3 1.6 %collective-permute-start.3 = (bf16[256,512]{1,0:T(8,128)(2,1)S(1)}, bf16[256,512]{1,0:T(8,128)(2,1)S(1)}, u32[]{:S(2)}, u32[]{:S(2)}) collective-permute-start(bf16[256,512]{1,0:T(8,128)(2,1)S(1)} %slice.21), channel_id=1, source_target_pairs={{0,4},{1,5},{2,0},{3,1},{4,8},{5,9},{6,2},{7,3},{8,12},{9,13},{10,... | collective-permute-start | bytes 786440 | tf_op jit(solution)/shard_map/ppermute | solution.py:544
  19.4 0.6 first_terms.1
  20.1 1.3 %collective-permute-start.9 = (bf16[3,128,512]{2,1,0:T(8,128)(2,1)S(1)}, bf16[3,128,512]{2,1,0:T(8,128)(2,1)S(1)}, u32[]{:S(2)}, u32[]{:S(2)}) collective-permute-start(bf16[3,128,512]{2,1,0:T(8,128)(2,1)S(1)} %get-tuple-element.105), channel_id=1, source_target_pairs={{16,0},{17,1},{18,2},{19,3},{20,4},{21,5},{22,6},{23,7},{24,8},{25... | collective-permute-start | bytes 1179656 | tf_op jit(solution)/shard_map/ppermute | solution.py:553
  21.4 1.6 %collective-permute-start.11 = (bf16[256,512]{1,0:T(8,128)(2,1)S(1)}, bf16[256,512]{1,0:T(8,128)(2,1)S(1)}, u32[]{:S(2)}, u32[]{:S(2)}) collective-permute-start(bf16[256,512]{1,0:T(8,128)(2,1)S(1)} %slice.25), channel_id=1, source_target_pairs={{0,4},{1,5},{2,0},{3,1},{4,8},{5,9},{6,2},{7,3},{8,12},{9,13},{10,... | collective-permute-start | bytes 786440 | tf_op jit(solution)/shard_map/ppermute | solution.py:544
  23.5 0.6 values.4.refs_6_
  24.1 2.3 %collective-permute-done.3.refs_2_.refs_8_ = bf16[256,512]{1,0:T(8,128)(2,1)S(1)} collective-permute-done((bf16[256,512]{1,0:T(8,128)(2,1)S(1)}, bf16[256,512]{1,0:T(8,128)(2,1)S(1)}, u32[]{:S(2)}, u32[]{:S(2)}) %collective-permute-start.3) | collective-permute-done | bytes 262176 | tf_op jit(solution)/shard_map/ppermute | solution.py:544
  26.3 1.3 %collective-permute-done.2.refs_3_.refs_9_ = bf16[256,512]{1,0:T(8,128)(2,1)S(1)} collective-permute-done((bf16[256,512]{1,0:T(8,128)(2,1)S(1)}, bf16[256,512]{1,0:T(8,128)(2,1)S(1)}, u32[]{:S(2)}, u32[]{:S(2)}) %collective-permute-start.2) | collective-permute-done | bytes 262176 | tf_op jit(solution)/shard_map/ppermute | solution.py:547
  28.1 1.6 %collective-permute-start.8 = (bf16[256,512]{1,0:T(8,128)(2,1)S(1)}, bf16[256,512]{1,0:T(8,128)(2,1)S(1)}, u32[]{:S(2)}, u32[]{:S(2)}) collective-permute-start(bf16[256,512]{1,0:T(8,128)(2,1)S(1)} %collective-permute-done.3.refs_2_.refs_8_), channel_id=1, source_target_pairs={{0,4},{1,5},{2,0},{3,1},{4,8},{5,9},{6,2},{7,3},{8,12},{9,13},{10,... | collective-permute-start | bytes 786440 | tf_op jit(solution)/shard_map/ppermute | solution.py:544
  29.7 2.3 %collective-permute-done.11.refs_4_.refs_10_ = bf16[256,512]{1,0:T(8,128)(2,1)S(1)} collective-permute-done((bf16[256,512]{1,0:T(8,128)(2,1)S(1)}, bf16[256,512]{1,0:T(8,128)(2,1)S(1)}, u32[]{:S(2)}, u32[]{:S(2)}) %collective-permute-start.11) | collective-permute-done | bytes 262176 | tf_op jit(solution)/shard_map/ppermute | solution.py:544
  31.9 1.6 %collective-permute-start.16 = (bf16[256,512]{1,0:T(8,128)(2,1)S(1)}, bf16[256,512]{1,0:T(8,128)(2,1)S(1)}, u32[]{:S(2)}, u32[]{:S(2)}) collective-permute-start(bf16[256,512]{1,0:T(8,128)(2,1)S(1)} %collective-permute-done.11.refs_4_.refs_10_), channel_id=1, source_target_pairs={{0,4},{1,5},{2,0},{3,1},{4,8},{5,9},{6,2},{7,3},{8,12},{9,13},{10,... | collective-permute-start | bytes 786440 | tf_op jit(solution)/shard_map/ppermute | solution.py:544
  34.0 1.3 %collective-permute-start.14 = (bf16[3,128,512]{2,1,0:T(8,128)(2,1)S(1)}, bf16[3,128,512]{2,1,0:T(8,128)(2,1)S(1)}, u32[]{:S(2)}, u32[]{:S(2)}) collective-permute-start(bf16[3,128,512]{2,1,0:T(8,128)(2,1)S(1)} %get-tuple-element.115), channel_id=1, source_target_pairs={{16,1},{17,0},{18,3},{19,2},{20,5},{21,4},{22,7},{23,6},{24,9},{25... | collective-permute-start | bytes 1179656 | tf_op jit(solution)/shard_map/ppermute | solution.py:556
  35.7 1.8 %collective-permute-done.8.refs_2_.refs_12_ = bf16[256,512]{1,0:T(8,128)(2,1)S(1)} collective-permute-done((bf16[256,512]{1,0:T(8,128)(2,1)S(1)}, bf16[256,512]{1,0:T(8,128)(2,1)S(1)}, u32[]{:S(2)}, u32[]{:S(2)}) %collective-permute-start.8) | collective-permute-done | bytes 262176 | tf_op jit(solution)/shard_map/ppermute | solution.py:544
  37.6 1.3 %collective-permute-done.7.refs_3_.refs_13_ = bf16[256,512]{1,0:T(8,128)(2,1)S(1)} collective-permute-done((bf16[256,512]{1,0:T(8,128)(2,1)S(1)}, bf16[256,512]{1,0:T(8,128)(2,1)S(1)}, u32[]{:S(2)}, u32[]{:S(2)}) %collective-permute-start.7) | collective-permute-done | bytes 262176 | tf_op jit(solution)/shard_map/ppermute | solution.py:547
  39.3 1.6 %collective-permute-start.13 = (bf16[256,512]{1,0:T(8,128)(2,1)S(1)}, bf16[256,512]{1,0:T(8,128)(2,1)S(1)}, u32[]{:S(2)}, u32[]{:S(2)}) collective-permute-start(bf16[256,512]{1,0:T(8,128)(2,1)S(1)} %collective-permute-done.8.refs_2_.refs_12_), channel_id=1, source_target_pairs={{0,4},{1,5},{2,0},{3,1},{4,8},{5,9},{6,2},{7,3},{8,12},{9,13},{10,... | collective-permute-start | bytes 786440 | tf_op jit(solution)/shard_map/ppermute | solution.py:544
  40.9 2.3 %collective-permute-done.16.refs_4_.refs_14_ = bf16[256,512]{1,0:T(8,128)(2,1)S(1)} collective-permute-done((bf16[256,512]{1,0:T(8,128)(2,1)S(1)}, bf16[256,512]{1,0:T(8,128)(2,1)S(1)}, u32[]{:S(2)}, u32[]{:S(2)}) %collective-permute-start.16) | collective-permute-done | bytes 262176 | tf_op jit(solution)/shard_map/ppermute | solution.py:544
  43.2 1.3 %collective-permute-done.15.refs_5_.refs_15_ = bf16[256,512]{1,0:T(8,128)(2,1)S(1)} collective-permute-done((bf16[256,512]{1,0:T(8,128)(2,1)S(1)}, bf16[256,512]{1,0:T(8,128)(2,1)S(1)}, u32[]{:S(2)}, u32[]{:S(2)}) %collective-permute-start.15) | collective-permute-done | bytes 262176 | tf_op jit(solution)/shard_map/ppermute | solution.py:547
  44.8 1.6 %collective-permute-start.19 = (bf16[256,512]{1,0:T(8,128)(2,1)S(1)}, bf16[256,512]{1,0:T(8,128)(2,1)S(1)}, u32[]{:S(2)}, u32[]{:S(2)}) collective-permute-start(bf16[256,512]{1,0:T(8,128)(2,1)S(1)} %weight_step.9), channel_id=1, source_target_pairs={{0,4},{1,5},{2,0},{3,1},{4,8},{5,9},{6,2},{7,3},{8,12},{9,13},{10,... | collective-permute-start | bytes 786440 | tf_op jit(solution)/shard_map/ppermute | solution.py:544
  46.6 0.5 collective-permute-start.18
  47.1 1.3 %collective-permute-start.24 = (bf16[3,128,512]{2,1,0:T(8,128)(2,1)S(1)}, bf16[3,128,512]{2,1,0:T(8,128)(2,1)S(1)}, u32[]{:S(2)}, u32[]{:S(2)}) collective-permute-start(bf16[3,128,512]{2,1,0:T(8,128)(2,1)S(1)} %get-tuple-element.127), channel_id=1, source_target_pairs={{16,0},{17,1},{18,2},{19,3},{20,4},{21,5},{22,6},{23,7},{24,8},{25... | collective-permute-start | bytes 1179656 | tf_op jit(solution)/shard_map/ppermute | solution.py:553
  48.9 1.2 %collective-permute-done.12.refs_3_.refs_17_ = bf16[256,512]{1,0:T(8,128)(2,1)S(1)} collective-permute-done((bf16[256,512]{1,0:T(8,128)(2,1)S(1)}, bf16[256,512]{1,0:T(8,128)(2,1)S(1)}, u32[]{:S(2)}, u32[]{:S(2)}) %collective-permute-start.12) | collective-permute-done | bytes 262176 | tf_op jit(solution)/shard_map/ppermute | solution.py:547
  50.6 1.7 %collective-permute-done.19.refs_4_ = bf16[256,512]{1,0:T(8,128)(2,1)S(1)} collective-permute-done((bf16[256,512]{1,0:T(8,128)(2,1)S(1)}, bf16[256,512]{1,0:T(8,128)(2,1)S(1)}, u32[]{:S(2)}, u32[]{:S(2)}) %collective-permute-start.19) | collective-permute-done | bytes 262176 | tf_op jit(solution)/shard_map/ppermute | solution.py:544
  52.3 1.3 %collective-permute-done.18.refs_4_ = bf16[256,512]{1,0:T(8,128)(2,1)S(1)} collective-permute-done((bf16[256,512]{1,0:T(8,128)(2,1)S(1)}, bf16[256,512]{1,0:T(8,128)(2,1)S(1)}, u32[]{:S(2)}, u32[]{:S(2)}) %collective-permute-start.18) | collective-permute-done | bytes 262176 | tf_op jit(solution)/shard_map/ppermute | solution.py:547
  54.3 0.5 collective-permute-start.20
  54.8 1.6 %collective-permute-start.21 = (bf16[512,512]{1,0:T(8,128)(2,1)S(1)}, bf16[512,512]{1,0:T(8,128)(2,1)S(1)}, u32[]{:S(2)}, u32[]{:S(2)}) collective-permute-start(bf16[512,512]{1,0:T(8,128)(2,1)S(1)} %weight_step.11), channel_id=1, source_target_pairs={{0,4},{1,5},{2,0},{3,1},{4,8},{5,9},{6,2},{7,3},{8,12},{9,13},{10,... | collective-permute-start | bytes 1572872 | tf_op jit(solution)/shard_map/ppermute | solution.py:544
  56.4 1.0 %local_grad.1 = (bf16[128,2688]{1,0:T(8,128)(2,1)S(1)}, bf16[128,2560]{1,0:T(8,128)(2,1)S(1)}) custom-call(bf16[8,128,512]{2,1,0:T(8,128)(2,1)S(1)} %get-tuple-element.156.refs_0_, bf16[8,128,512]{2,1,0:T(8,128)(2,1)S(1)} %collective-permute-done.5.refs_1_, bf16[128,512]{1,0:T(8,128)(2,1)S(1)} %get-tuple-element.141.refs_0_.refs_2_.refs_5_, ...), custom_call_target="tpu_custom_call" | custom-call | flops 200000000 | bytes 1024 | tf_op jit(solution)/shard_map/local_grad/pallas_call | solution.py:359
  57.3 1.3 %collective-permute-start.26 = (bf16[128,2688]{1,0:T(8,128)(2,1)S(1)}, bf16[128,2688]{1,0:T(8,128)(2,1)S(1)}, u32[]{:S(2)}, u32[]{:S(2)}) collective-permute-start(bf16[128,2688]{1,0:T(8,128)(2,1)S(1)} %get-tuple-element.142), channel_id=1, source_target_pairs={{16,0},{17,1},{18,2},{19,3},{20,4},{21,5},{22,6},{23,7},{24,8},{25... | collective-permute-start | bytes 2064392 | tf_op jit(solution)/shard_map/ppermute | solution.py:553
  58.7 3.5 %back.1 = (bf16[128,4096]{1,0:T(8,128)(2,1)}, bf16[128,512]{1,0:T(8,128)(2,1)}) custom-call(f32[4,128,1024]{2,1,0:T(8,128)S(1)} %copy-done.2, bf16[4,1024,128]{2,1,0:T(8,128)(2,1)S(1)} %copy-done.4, bf16[4,128,128]{2,1,0:T(8,128)(2,1)S(1)} %copy-done.8, bf16[128,4096]{1,0:T(8,128)(2,1)S(1)} %bitcast.18, f32[128,512]{1,0:T(8,128)S(1)} %get-tuple-element.143.u_one, ...), custom_call_target="tpu_custom_call" | custom-call | flops 200000000 | bytes 1024 | tf_op jit(solution)/shard_map/back/pallas_call | solution.py:224
  62.2 1.3 %collective-permute-start.27 = (bf16[128,2560]{1,0:T(8,128)(2,1)S(1)}, bf16[128,2560]{1,0:T(8,128)(2,1)S(1)}, u32[]{:S(2)}, u32[]{:S(2)}) collective-permute-start(bf16[128,2560]{1,0:T(8,128)(2,1)S(1)} %get-tuple-element.159), channel_id=1, source_target_pairs={{16,1},{17,0},{18,3},{19,2},{20,5},{21,4},{22,7},{23,6},{24,9},{25... | collective-permute-start | bytes 1966088 | tf_op jit(solution)/shard_map/ppermute | solution.py:556
  63.5 3.1 %collective-permute-done.21.refs_4_ = bf16[512,512]{1,0:T(8,128)(2,1)S(1)} collective-permute-done((bf16[512,512]{1,0:T(8,128)(2,1)S(1)}, bf16[512,512]{1,0:T(8,128)(2,1)S(1)}, u32[]{:S(2)}, u32[]{:S(2)}) %collective-permute-start.21) | collective-permute-done | bytes 524320 | tf_op jit(solution)/shard_map/ppermute | solution.py:544
  66.9 1.3 %collective-permute-start.23 = (bf16[512,512]{1,0:T(8,128)(2,1)S(1)}, bf16[512,512]{1,0:T(8,128)(2,1)S(1)}, u32[]{:S(2)}, u32[]{:S(2)}) collective-permute-start(bf16[512,512]{1,0:T(8,128)(2,1)S(1)} %weight_step.13), channel_id=1, source_target_pairs={{0,4},{1,5},{2,0},{3,1},{4,8},{5,9},{6,2},{7,3},{8,12},{9,13},{10,... | collective-permute-start | bytes 1572872 | tf_op jit(solution)/shard_map/ppermute | solution.py:544
  68.6 0.8 collective-permute-start.22
  69.3 8.4 %collective-permute-done.23.refs_4_ = bf16[512,512]{1,0:T(8,128)(2,1)S(1)} collective-permute-done((bf16[512,512]{1,0:T(8,128)(2,1)S(1)}, bf16[512,512]{1,0:T(8,128)(2,1)S(1)}, u32[]{:S(2)}, u32[]{:S(2)}) %collective-permute-start.23) | collective-permute-done | bytes 524320 | tf_op jit(solution)/shard_map/ppermute | solution.py:544
  77.8 1.5 %collective-permute-done.22.refs_4_ = bf16[512,512]{1,0:T(8,128)(2,1)S(1)} collective-permute-done((bf16[512,512]{1,0:T(8,128)(2,1)S(1)}, bf16[512,512]{1,0:T(8,128)(2,1)S(1)}, u32[]{:S(2)}, u32[]{:S(2)}) %collective-permute-start.22) | collective-permute-done | bytes 524320 | tf_op jit(solution)/shard_map/ppermute | solution.py:547
  79.9 1.5 %collective-permute-start.28 = (bf16[512,512]{1,0:T(8,128)(2,1)S(1)}, bf16[512,512]{1,0:T(8,128)(2,1)S(1)}, u32[]{:S(2)}, u32[]{:S(2)}) collective-permute-start(bf16[512,512]{1,0:T(8,128)(2,1)S(1)} %weight_step.16), channel_id=1, source_target_pairs={{0,2},{1,3},{2,6},{3,7},{4,0},{5,1},{6,10},{7,11},{8,4},{9,5},{10,... | collective-permute-start | bytes 1572872 | tf_op jit(solution)/shard_map/ppermute | solution.py:547
  81.4 0.8 collective-permute-start.25
  82.2 1.7 %early_blocks.1.base = bf16[128,8192]{1,0:T(8,128)(2,1)} custom-call(s32[17]{0:T(128)S(1)} %pad_add_fusion.where, f32[8,128]{1,0:T(8,128)S(1)} %fence.19.pin, bf16[3,128,512]{2,1,0:T(8,128)(2,1)S(1)} %collective-permute-done.9.ones, bf16[3,128,512]{2,1,0:T(8,128)(2,1)S(1)} %collective-permute-done.14.twos, ...), custom_call_target="tpu_custom_call" | custom-call | flops 200000000 | bytes 1024 | tf_op jit(solution)/shard_map/early_blocks/pallas_call | solution.py:437
  83.9 1.5 %collective-permute-done.27.refs_0_ = bf16[128,2560]{1,0:T(8,128)(2,1)S(1)} collective-permute-done((bf16[128,2560]{1,0:T(8,128)(2,1)S(1)}, bf16[128,2560]{1,0:T(8,128)(2,1)S(1)}, u32[]{:S(2)}, u32[]{:S(2)}) %collective-permute-start.27) | collective-permute-done | bytes 655392 | tf_op jit(solution)/shard_map/ppermute | solution.py:556
  85.4 1.4 %join.1 = bf16[128,8192]{1,0:T(8,128)(2,1)} custom-call(s32[17]{0:T(128)S(1)} %pad_add_fusion.where, bf16[128,8192]{1,0:T(8,128)(2,1)} %early_blocks.1.base, bf16[128,2560]{1,0:T(8,128)(2,1)S(1)} %collective-permute-done.27.refs_0_), custom_call_target="tpu_custom_call", output_to_operand_aliasing={{}: (1, {})} | custom-call | flops 200000000 | bytes 1024 | tf_op jit(solution)/shard_map/join/pallas_call | solution.py:474
  86.8 3.8 %collective-permute-done.25.refs_4_ = bf16[512,512]{1,0:T(8,128)(2,1)S(1)} collective-permute-done((bf16[512,512]{1,0:T(8,128)(2,1)S(1)}, bf16[512,512]{1,0:T(8,128)(2,1)S(1)}, u32[]{:S(2)}, u32[]{:S(2)}) %collective-permute-start.25) | collective-permute-done | bytes 524320 | tf_op jit(solution)/shard_map/ppermute | solution.py:544
  90.6 1.1 %weight_step.17 = bf16[512,512]{1,0:T(8,128)(2,1)} custom-call(bf16[8,128,512]{2,1,0:T(8,128)(2,1)S(1)} %get-tuple-element.156.refs_0_, bf16[8,128,512]{2,1,0:T(8,128)(2,1)S(1)} %collective-permute-done.5.refs_1_, bf16[128,512]{1,0:T(8,128)(2,1)S(1)} %get-tuple-element.141.refs_0_.refs_2_.refs_5_, ...), custom_call_target="tpu_custom_call" | custom-call | flops 200000000 | bytes 1024 | tf_op jit(solution)/shard_map/weight_step/pallas_call | solution.py:397
  (75 shorter events, 7.3 us)
Async XLA Ops:
  0.6 15.2 %collective-permute-start.1 = (bf16[512,512]{1,0:T(8,128)(2,1)}, bf16[512,512]{1,0:T(8,128)(2,1)S(1)}, u32[]{:S(2)}, u32[]{:S(2)}) collective-permute-start(bf16[512,512]{1,0:T(8,128)(2,1)} %bitcast.19), channel_id=1, source_target_pairs={{0,4},{1,5},{2,0},{3,1},{4,8},{5,9},{6,2},{7,3},{8,12},{9,13},{10,... | collective-permute-start | bytes 1572872 | tf_op jit(solution)/shard_map/ppermute | solution.py:544
  3.7 13.6 %collective-permute-start = (bf16[512,512]{1,0:T(8,128)(2,1)}, bf16[512,512]{1,0:T(8,128)(2,1)S(1)}, u32[]{:S(2)}, u32[]{:S(2)}) collective-permute-start(bf16[512,512]{1,0:T(8,128)(2,1)} %bitcast.20), channel_id=1, source_target_pairs={{0,2},{1,3},{2,6},{3,7},{4,0},{5,1},{6,10},{7,11},{8,4},{9,5},{10,... | collective-permute-start | bytes 1572872 | tf_op jit(solution)/shard_map/ppermute | solution.py:547
  4.5 1.6 %copy-start = (bf16[1,128,8192]{2,1,0:T(8,128)(2,1)S(1)}, bf16[1,128,8192]{2,1,0:T(8,128)(2,1)}, u32[]{:S(2)}) copy-start(bf16[1,128,8192]{2,1,0:T(8,128)(2,1)} %param.8) | copy-start | bytes 6291460
  6.1 2.2 %copy-start.5 = (bf16[10,8192]{1,0:T(8,128)(2,1)S(1)}, bf16[10,8192]{1,0:T(8,128)(2,1)}, u32[]{:S(2)}) copy-start(bf16[10,8192]{1,0:T(8,128)(2,1)} %gain_t.1) | copy-start | bytes 491524
  6.8 3.9 %copy-start.9 = (s32[1,128]{1,0:T(1,128)S(1)}, s32[1,128]{1,0:T(1,128)}, u32[]{:S(2)}) copy-start(s32[1,128]{1,0:T(1,128)} %param.11) | copy-start | bytes 1540
  6.8 4.4 %copy-start.1 = (bf16[1,128,4096]{2,1,0:T(8,128)(2,1)S(1)}, bf16[1,128,4096]{2,1,0:T(8,128)(2,1)}, u32[]{:S(2)}) copy-start(bf16[1,128,4096]{2,1,0:T(8,128)(2,1)} %param.15) | copy-start | bytes 3145732
  6.8 4.4 %copy-start.6 = (bf16[1,128,4096]{2,1,0:T(8,128)(2,1)S(1)}, bf16[1,128,4096]{2,1,0:T(8,128)(2,1)}, u32[]{:S(2)}) copy-start(bf16[1,128,4096]{2,1,0:T(8,128)(2,1)} %param.12) | copy-start | bytes 3145732
  6.8 4.4 %copy-start.7 = (bf16[1,128,512]{2,1,0:T(8,128)(2,1)S(1)}, bf16[1,128,512]{2,1,0:T(8,128)(2,1)}, u32[]{:S(2)}) copy-start(bf16[1,128,512]{2,1,0:T(8,128)(2,1)} %param.13) | copy-start | bytes 393220
  6.9 13.2 %collective-permute-start.6 = (bf16[3,128,512]{2,1,0:T(8,128)(2,1)S(1)}, bf16[3,128,512]{2,1,0:T(8,128)(2,1)S(1)}, u32[]{:S(2)}, u32[]{:S(2)}) collective-permute-start(bf16[3,128,512]{2,1,0:T(8,128)(2,1)S(1)} %get-tuple-element.84), channel_id=1, source_target_pairs={{16,0},{17,1},{18,2},{19,3},{20,4},{21,5},{22,6},{23,7},{24,8},{25... | collective-permute-start | bytes 1179656 | tf_op jit(solution)/shard_map/ppermute | solution.py:553
  10.6 8.8 %collective-permute-start.5 = (bf16[8,128,512]{2,1,0:T(8,128)(2,1)S(1)}, bf16[8,128,512]{2,1,0:T(8,128)(2,1)S(1)}, u32[]{:S(2)}, u32[]{:S(2)}) collective-permute-start(bf16[8,128,512]{2,1,0:T(8,128)(2,1)S(1)} %get-tuple-element.96), channel_id=1, source_target_pairs={{0,1},{1,0},{2,3},{3,2},{4,5},{5,4},{6,7},{7,6},{8,9},{9,8},{10,11... | collective-permute-start | bytes 3145736 | tf_op jit(solution)/shard_map/ppermute | solution.py:550
  14.7 4.8 %collective-permute-start.4 = (bf16[128,512]{1,0:T(8,128)(2,1)S(1)}, bf16[128,512]{1,0:T(8,128)(2,1)S(1)}, u32[]{:S(2)}, u32[]{:S(2)}) collective-permute-start(bf16[128,512]{1,0:T(8,128)(2,1)S(1)} %get-tuple-element.141.refs_0_.refs_2_.refs_5_), channel_id=1, source_target_pairs={{0,1},{1,0},{2,3},{3,2},{4,5},{5,4},{6,7},{7,6},{8,9},{9,8},{10,11... | collective-permute-start | bytes 393224 | tf_op jit(solution)/shard_map/ppermute | solution.py:550
  15.1 4.3 %copy-start.3 = (bf16[1,512,512]{2,1,0:T(8,128)(2,1)S(1)}, bf16[1,512,512]{2,1,0:T(8,128)(2,1)}, u32[]{:S(2)}) copy-start(bf16[1,512,512]{2,1,0:T(8,128)(2,1)} %param.14) | copy-start | bytes 1572868
  17.3 9.0 %collective-permute-start.3 = (bf16[256,512]{1,0:T(8,128)(2,1)S(1)}, bf16[256,512]{1,0:T(8,128)(2,1)S(1)}, u32[]{:S(2)}, u32[]{:S(2)}) collective-permute-start(bf16[256,512]{1,0:T(8,128)(2,1)S(1)} %slice.21), channel_id=1, source_target_pairs={{0,4},{1,5},{2,0},{3,1},{4,8},{5,9},{6,2},{7,3},{8,12},{9,13},{10,... | collective-permute-start | bytes 786440 | tf_op jit(solution)/shard_map/ppermute | solution.py:544
  19.0 8.7 %collective-permute-start.2 = (bf16[256,512]{1,0:T(8,128)(2,1)S(1)}, bf16[256,512]{1,0:T(8,128)(2,1)S(1)}, u32[]{:S(2)}, u32[]{:S(2)}) collective-permute-start(bf16[256,512]{1,0:T(8,128)(2,1)S(1)} %slice.20), channel_id=1, source_target_pairs={{0,2},{1,3},{2,6},{3,7},{4,0},{5,1},{6,10},{7,11},{8,4},{9,5},{10,... | collective-permute-start | bytes 786440 | tf_op jit(solution)/shard_map/ppermute | solution.py:547
  20.1 13.9 %collective-permute-start.9 = (bf16[3,128,512]{2,1,0:T(8,128)(2,1)S(1)}, bf16[3,128,512]{2,1,0:T(8,128)(2,1)S(1)}, u32[]{:S(2)}, u32[]{:S(2)}) collective-permute-start(bf16[3,128,512]{2,1,0:T(8,128)(2,1)S(1)} %get-tuple-element.105), channel_id=1, source_target_pairs={{16,0},{17,1},{18,2},{19,3},{20,4},{21,5},{22,6},{23,7},{24,8},{25... | collective-permute-start | bytes 1179656 | tf_op jit(solution)/shard_map/ppermute | solution.py:553
  21.4 10.5 %collective-permute-start.11 = (bf16[256,512]{1,0:T(8,128)(2,1)S(1)}, bf16[256,512]{1,0:T(8,128)(2,1)S(1)}, u32[]{:S(2)}, u32[]{:S(2)}) collective-permute-start(bf16[256,512]{1,0:T(8,128)(2,1)S(1)} %slice.25), channel_id=1, source_target_pairs={{0,4},{1,5},{2,0},{3,1},{4,8},{5,9},{6,2},{7,3},{8,12},{9,13},{10,... | collective-permute-start | bytes 786440 | tf_op jit(solution)/shard_map/ppermute | solution.py:544
  23.0 10.5 %collective-permute-start.10 = (bf16[256,512]{1,0:T(8,128)(2,1)S(1)}, bf16[256,512]{1,0:T(8,128)(2,1)S(1)}, u32[]{:S(2)}, u32[]{:S(2)}) collective-permute-start(bf16[256,512]{1,0:T(8,128)(2,1)S(1)} %slice.24), channel_id=1, source_target_pairs={{0,2},{1,3},{2,6},{3,7},{4,0},{5,1},{6,10},{7,11},{8,4},{9,5},{10,... | collective-permute-start | bytes 786440 | tf_op jit(solution)/shard_map/ppermute | solution.py:547
  27.7 11.2 %collective-permute-start.7 = (bf16[256,512]{1,0:T(8,128)(2,1)S(1)}, bf16[256,512]{1,0:T(8,128)(2,1)S(1)}, u32[]{:S(2)}, u32[]{:S(2)}) collective-permute-start(bf16[256,512]{1,0:T(8,128)(2,1)S(1)} %collective-permute-done.2.refs_3_.refs_9_), channel_id=1, source_target_pairs={{0,2},{1,3},{2,6},{3,7},{4,0},{5,1},{6,10},{7,11},{8,4},{9,5},{10,... | collective-permute-start | bytes 786440 | tf_op jit(solution)/shard_map/ppermute | solution.py:547
  28.1 9.4 %collective-permute-start.8 = (bf16[256,512]{1,0:T(8,128)(2,1)S(1)}, bf16[256,512]{1,0:T(8,128)(2,1)S(1)}, u32[]{:S(2)}, u32[]{:S(2)}) collective-permute-start(bf16[256,512]{1,0:T(8,128)(2,1)S(1)} %collective-permute-done.3.refs_2_.refs_8_), channel_id=1, source_target_pairs={{0,4},{1,5},{2,0},{3,1},{4,8},{5,9},{6,2},{7,3},{8,12},{9,13},{10,... | collective-permute-start | bytes 786440 | tf_op jit(solution)/shard_map/ppermute | solution.py:544
  31.9 11.2 %collective-permute-start.16 = (bf16[256,512]{1,0:T(8,128)(2,1)S(1)}, bf16[256,512]{1,0:T(8,128)(2,1)S(1)}, u32[]{:S(2)}, u32[]{:S(2)}) collective-permute-start(bf16[256,512]{1,0:T(8,128)(2,1)S(1)} %collective-permute-done.11.refs_4_.refs_10_), channel_id=1, source_target_pairs={{0,4},{1,5},{2,0},{3,1},{4,8},{5,9},{6,2},{7,3},{8,12},{9,13},{10,... | collective-permute-start | bytes 786440 | tf_op jit(solution)/shard_map/ppermute | solution.py:544
  33.5 11.0 %collective-permute-start.15 = (bf16[256,512]{1,0:T(8,128)(2,1)S(1)}, bf16[256,512]{1,0:T(8,128)(2,1)S(1)}, u32[]{:S(2)}, u32[]{:S(2)}) collective-permute-start(bf16[256,512]{1,0:T(8,128)(2,1)S(1)} %collective-permute-done.10.refs_5_.refs_11_), channel_id=1, source_target_pairs={{0,2},{1,3},{2,6},{3,7},{4,0},{5,1},{6,10},{7,11},{8,4},{9,5},{10,... | collective-permute-start | bytes 786440 | tf_op jit(solution)/shard_map/ppermute | solution.py:547
  34.0 13.2 %collective-permute-start.14 = (bf16[3,128,512]{2,1,0:T(8,128)(2,1)S(1)}, bf16[3,128,512]{2,1,0:T(8,128)(2,1)S(1)}, u32[]{:S(2)}, u32[]{:S(2)}) collective-permute-start(bf16[3,128,512]{2,1,0:T(8,128)(2,1)S(1)} %get-tuple-element.115), channel_id=1, source_target_pairs={{16,1},{17,0},{18,3},{19,2},{20,5},{21,4},{22,7},{23,6},{24,9},{25... | collective-permute-start | bytes 1179656 | tf_op jit(solution)/shard_map/ppermute | solution.py:556
  38.9 11.2 %collective-permute-start.12 = (bf16[256,512]{1,0:T(8,128)(2,1)S(1)}, bf16[256,512]{1,0:T(8,128)(2,1)S(1)}, u32[]{:S(2)}, u32[]{:S(2)}) collective-permute-start(bf16[256,512]{1,0:T(8,128)(2,1)S(1)} %collective-permute-done.7.refs_3_.refs_13_), channel_id=1, source_target_pairs={{0,2},{1,3},{2,6},{3,7},{4,0},{5,1},{6,10},{7,11},{8,4},{9,5},{10,... | collective-permute-start | bytes 786440 | tf_op jit(solution)/shard_map/ppermute | solution.py:547
  39.3 9.5 %collective-permute-start.13 = (bf16[256,512]{1,0:T(8,128)(2,1)S(1)}, bf16[256,512]{1,0:T(8,128)(2,1)S(1)}, u32[]{:S(2)}, u32[]{:S(2)}) collective-permute-start(bf16[256,512]{1,0:T(8,128)(2,1)S(1)} %collective-permute-done.8.refs_2_.refs_12_), channel_id=1, source_target_pairs={{0,4},{1,5},{2,0},{3,1},{4,8},{5,9},{6,2},{7,3},{8,12},{9,13},{10,... | collective-permute-start | bytes 786440 | tf_op jit(solution)/shard_map/ppermute | solution.py:544
  44.8 7.6 %collective-permute-start.19 = (bf16[256,512]{1,0:T(8,128)(2,1)S(1)}, bf16[256,512]{1,0:T(8,128)(2,1)S(1)}, u32[]{:S(2)}, u32[]{:S(2)}) collective-permute-start(bf16[256,512]{1,0:T(8,128)(2,1)S(1)} %weight_step.9), channel_id=1, source_target_pairs={{0,4},{1,5},{2,0},{3,1},{4,8},{5,9},{6,2},{7,3},{8,12},{9,13},{10,... | collective-permute-start | bytes 786440 | tf_op jit(solution)/shard_map/ppermute | solution.py:544
  46.6 7.0 %collective-permute-start.18 = (bf16[256,512]{1,0:T(8,128)(2,1)S(1)}, bf16[256,512]{1,0:T(8,128)(2,1)S(1)}, u32[]{:S(2)}, u32[]{:S(2)}) collective-permute-start(bf16[256,512]{1,0:T(8,128)(2,1)S(1)} %weight_step.10), channel_id=1, source_target_pairs={{0,2},{1,3},{2,6},{3,7},{4,0},{5,1},{6,10},{7,11},{8,4},{9,5},{10,... | collective-permute-start | bytes 786440 | tf_op jit(solution)/shard_map/ppermute | solution.py:547
  47.1 22.2 %collective-permute-start.24 = (bf16[3,128,512]{2,1,0:T(8,128)(2,1)S(1)}, bf16[3,128,512]{2,1,0:T(8,128)(2,1)S(1)}, u32[]{:S(2)}, u32[]{:S(2)}) collective-permute-start(bf16[3,128,512]{2,1,0:T(8,128)(2,1)S(1)} %get-tuple-element.127), channel_id=1, source_target_pairs={{16,0},{17,1},{18,2},{19,3},{20,4},{21,5},{22,6},{23,7},{24,8},{25... | collective-permute-start | bytes 1179656 | tf_op jit(solution)/shard_map/ppermute | solution.py:553
  50.5 5.9 %collective-permute-start.17 = (f32[128,896]{1,0:T(8,128)S(1)}, f32[128,896]{1,0:T(8,128)S(1)}, u32[]{:S(2)}, u32[]{:S(2)}) collective-permute-start(f32[128,896]{1,0:T(8,128)S(1)} %get-tuple-element.134.refs_6_), channel_id=1, source_target_pairs={{0,1},{1,0},{2,3},{3,2},{4,5},{5,4},{6,7},{7,6},{8,9},{9,8},{10,11... | collective-permute-start | bytes 1376264 | tf_op jit(solution)/shard_map/ppermute | solution.py:550
  54.3 12.3 %collective-permute-start.20 = (bf16[512,512]{1,0:T(8,128)(2,1)S(1)}, bf16[512,512]{1,0:T(8,128)(2,1)S(1)}, u32[]{:S(2)}, u32[]{:S(2)}) collective-permute-start(bf16[512,512]{1,0:T(8,128)(2,1)S(1)} %weight_step.12), channel_id=1, source_target_pairs={{0,2},{1,3},{2,6},{3,7},{4,0},{5,1},{6,10},{7,11},{8,4},{9,5},{10,... | collective-permute-start | bytes 1572872 | tf_op jit(solution)/shard_map/ppermute | solution.py:547
  54.8 11.8 %collective-permute-start.21 = (bf16[512,512]{1,0:T(8,128)(2,1)S(1)}, bf16[512,512]{1,0:T(8,128)(2,1)S(1)}, u32[]{:S(2)}, u32[]{:S(2)}) collective-permute-start(bf16[512,512]{1,0:T(8,128)(2,1)S(1)} %weight_step.11), channel_id=1, source_target_pairs={{0,4},{1,5},{2,0},{3,1},{4,8},{5,9},{6,2},{7,3},{8,12},{9,13},{10,... | collective-permute-start | bytes 1572872 | tf_op jit(solution)/shard_map/ppermute | solution.py:544
  56.4 2.3 %copy-start.2 = (f32[4,128,1024]{2,1,0:T(8,128)S(1)}, f32[4,128,1024]{2,1,0:T(8,128)}, u32[]{:S(2)}) copy-start(f32[4,128,1024]{2,1,0:T(8,128)} %get-tuple-element.89.probs) | copy-start | bytes 6291460
  56.4 2.3 %copy-start.4 = (bf16[4,1024,128]{2,1,0:T(8,128)(2,1)S(1)}, bf16[4,1024,128]{2,1,0:T(8,128)(2,1)}, u32[]{:S(2)}) copy-start(bf16[4,1024,128]{2,1,0:T(8,128)(2,1)} %get-tuple-element.90.q_rot) | copy-start | bytes 3145732
  56.4 2.3 %copy-start.8 = (bf16[4,128,128]{2,1,0:T(8,128)(2,1)S(1)}, bf16[4,128,128]{2,1,0:T(8,128)(2,1)}, u32[]{:S(2)}) copy-start(bf16[4,128,128]{2,1,0:T(8,128)(2,1)} %get-tuple-element.91.k_rot) | copy-start | bytes 393220
  57.3 24.8 %collective-permute-start.26 = (bf16[128,2688]{1,0:T(8,128)(2,1)S(1)}, bf16[128,2688]{1,0:T(8,128)(2,1)S(1)}, u32[]{:S(2)}, u32[]{:S(2)}) collective-permute-start(bf16[128,2688]{1,0:T(8,128)(2,1)S(1)} %get-tuple-element.142), channel_id=1, source_target_pairs={{16,0},{17,1},{18,2},{19,3},{20,4},{21,5},{22,6},{23,7},{24,8},{25... | collective-permute-start | bytes 2064392 | tf_op jit(solution)/shard_map/ppermute | solution.py:553
  62.2 23.2 %collective-permute-start.27 = (bf16[128,2560]{1,0:T(8,128)(2,1)S(1)}, bf16[128,2560]{1,0:T(8,128)(2,1)S(1)}, u32[]{:S(2)}, u32[]{:S(2)}) collective-permute-start(bf16[128,2560]{1,0:T(8,128)(2,1)S(1)} %get-tuple-element.159), channel_id=1, source_target_pairs={{16,1},{17,0},{18,3},{19,2},{20,5},{21,4},{22,7},{23,6},{24,9},{25... | collective-permute-start | bytes 1966088 | tf_op jit(solution)/shard_map/ppermute | solution.py:556
  66.9 10.9 %collective-permute-start.23 = (bf16[512,512]{1,0:T(8,128)(2,1)S(1)}, bf16[512,512]{1,0:T(8,128)(2,1)S(1)}, u32[]{:S(2)}, u32[]{:S(2)}) collective-permute-start(bf16[512,512]{1,0:T(8,128)(2,1)S(1)} %weight_step.13), channel_id=1, source_target_pairs={{0,4},{1,5},{2,0},{3,1},{4,8},{5,9},{6,2},{7,3},{8,12},{9,13},{10,... | collective-permute-start | bytes 1572872 | tf_op jit(solution)/shard_map/ppermute | solution.py:544
  68.6 10.7 %collective-permute-start.22 = (bf16[512,512]{1,0:T(8,128)(2,1)S(1)}, bf16[512,512]{1,0:T(8,128)(2,1)S(1)}, u32[]{:S(2)}, u32[]{:S(2)}) collective-permute-start(bf16[512,512]{1,0:T(8,128)(2,1)S(1)} %weight_step.14), channel_id=1, source_target_pairs={{0,2},{1,3},{2,6},{3,7},{4,0},{5,1},{6,10},{7,11},{8,4},{9,5},{10,... | collective-permute-start | bytes 1572872 | tf_op jit(solution)/shard_map/ppermute | solution.py:547
  79.9 10.7 %collective-permute-start.28 = (bf16[512,512]{1,0:T(8,128)(2,1)S(1)}, bf16[512,512]{1,0:T(8,128)(2,1)S(1)}, u32[]{:S(2)}, u32[]{:S(2)}) collective-permute-start(bf16[512,512]{1,0:T(8,128)(2,1)S(1)} %weight_step.16), channel_id=1, source_target_pairs={{0,2},{1,3},{2,6},{3,7},{4,0},{5,1},{6,10},{7,11},{8,4},{9,5},{10,... | collective-permute-start | bytes 1572872 | tf_op jit(solution)/shard_map/ppermute | solution.py:547
  81.4 9.2 %collective-permute-start.25 = (bf16[512,512]{1,0:T(8,128)(2,1)S(1)}, bf16[512,512]{1,0:T(8,128)(2,1)S(1)}, u32[]{:S(2)}, u32[]{:S(2)}) collective-permute-start(bf16[512,512]{1,0:T(8,128)(2,1)S(1)} %weight_step.15), channel_id=1, source_target_pairs={{0,4},{1,5},{2,0},{3,1},{4,8},{5,9},{6,2},{7,3},{8,12},{9,13},{10,... | collective-permute-start | bytes 1572872 | tf_op jit(solution)/shard_map/ppermute | solution.py:544

commit v4 on v3

--- a/solution.py
+++ b/solution.py
@@ -403,6 +403,32 @@
     )(mine, theirs, vgs, vgs_t, *arrived)
 
 
+def weight_last_kernel(mine, theirs, vgs, vgs_t, f, b, out, held, sem):
+    right = both_vgs(vgs, vgs_t)
+    half = f.shape[0] // 2
+    copies = []
+    for side in range(2):
+        at = slice(side * half, (side + 1) * half)
+        total = mm(pair(mine, theirs, (0, side)), right, (0, 0))
+        held[at, :] = (total + f[at, :].astype(F32) + b[at, :].astype(F32)).astype(BF16)
+        copies.append(pltpu.make_async_copy(held.at[at, :], out.at[at, :], sem.at[side]))
+        copies[-1].start()
+    for copy in copies:
+        copy.wait()
+
+
+def weight_last(mine, theirs, vgs, vgs_t, f, b):
+    return pl.pallas_call(
+        weight_last_kernel,
+        out_specs=pl.BlockSpec(memory_space=pl.ANY),
+        out_shape=sds(f.shape, BF16),
+        scratch_shapes=[pltpu.VMEM(f.shape, BF16), pltpu.SemaphoreType.DMA((2,))],
+        compiler_params=params(),
+        cost_estimate=SMALL,
+        name="weight_last",
+    )(mine, theirs, vgs, vgs_t, f, b)
+
+
 def copies_of(pieces, shares, where, out, sem, first, rows):
     copies = []
     for piece, blocks in zip(pieces, shares, strict=True):
@@ -538,7 +564,7 @@
     half = chips // 2
     low, high = slice(0, rows // 2), slice(rows // 2, rows)
     soon = [0, 1, chips - 1]
-    later = [[2, chips - 2, 3], list(range(4, chips - 2))]
+    later = [[r for r in range(chips) if r not in soon]]
 
     def ahead(x):
         return lax.ppermute(x, "dp", forth)
@@ -651,8 +677,9 @@
     got = swapped(then(packed))
 
     def weight_turn(r, f, b):
-        f, b = after(f), after(b)
-        return ahead(weight_part((r, None), f)), behind(weight_part((chips - r, None), None, b))
+        f = ahead(weight_part((r, None), after(f)))
+        b = behind(weight_part((chips - r, None), None, after(b)))
+        return f, b
 
     if half > 2:
         f, b = weight_turn(half - 1, f, b)
@@ -680,7 +707,7 @@
     t = after(t)
     upstream = then(join(where, after(upstream), [t], [sum(later, [])], chips, rows))
     f, b = after(f), after(b)
-    weight_grad = weight_step(mine, theirs, vgs, vgs_t, (0, None), f, b)
+    weight_grad = weight_last(mine, theirs, vgs, vgs_t, f, b)
     return (query_grad[None], key_grad[None], weight_grad[None], upstream[None])
 
 

time: 93.2 us -> 93 us (level)
    pallas_call x9 -> x8, Pallas kernels: 3.56 us -> 2.42 us  [weight_step(): pl.pallas_call(kernel, out_shape=sds((at.stop - at.start, vgs.shape[1]),...]
    ppermute x10, waiting for transfers between devices: 9.5 us -> 8.38 us  [behind(): return lax.ppermute(x, 'dp', back)]
    pallas_call x0 -> x1, Pallas kernels: none -> 1.08 us  [weight_last(): pl.pallas_call(weight_last_kernel, out_specs=pl.BlockSpec(memory_space=pl...]
    ppermute x2, waiting for transfers between devices: 1.49 us -> 2.47 us  [sent_across(): return lax.ppermute(x, ('section', 'dp'), cross)]
    ppermute x10, starting transfers between devices: 16.4 us -> 15.4 us  [ahead(): return lax.ppermute(x, 'dp', forth)]
where the time goes in v4:
time: 93 us; the launch traced here: 91.6 us
  waiting for transfers between devices  37.4 us (40%)
  starting transfers between devices  30.2 us (32%)
  Pallas kernels  20 us (22%)
  between operations  1.73 us (2%)
  local copies, waits for them, and re-layouts  1.72 us (2%)
    ppermute x10, waiting for transfers between devices, ahead(): return lax.ppermute(x, 'dp', forth)  26.5 us
    ppermute x10, starting transfers between devices, ahead(): return lax.ppermute(x, 'dp', forth)  15.4 us
    ppermute x10, waiting for transfers between devices, behind(): return lax.ppermute(x, 'dp', back)  8.38 us
    ppermute x10, starting transfers between devices, behind(): return lax.ppermute(x, 'dp', back)  6.29 us
    ppermute x4, starting transfers between devices, sent_down(): return lax.ppermute(x, ('section', 'dp'), down)  5.29 us
    pallas_call x1, Pallas kernels, attention_back(): pl.pallas_call(back_kernel, grid=(HK,), in_specs=[pl.BlockSpec((1, tokens...  3.49 us
    pallas_call x1, Pallas kernels, attention_probs(): pl.pallas_call(probs_kernel, grid=(HK,), in_specs=[group, head, group, ta...  3.44 us
    ppermute x2, starting transfers between devices, sent_across(): return lax.ppermute(x, ('section', 'dp'), cross)  2.56 us
  transfers between devices with their start and end apart: 29, of which 17 were waited for; matrix products, arithmetic and copies ran while one was open for 1% of the time, Pallas kernels for 21%

profile of v4, /device:TPU:0, one launch (start us, length us, event | category | flops | bytes accessed | tf_op | source)
XLA Modules:
  0.0 91.6 jit_solution(14499348715003474498)
XLA Ops:
  0.6 3.1 %collective-permute-start.1 = (bf16[512,512]{1,0:T(8,128)(2,1)}, bf16[512,512]{1,0:T(8,128)(2,1)S(1)}, u32[]{:S(2)}, u32[]{:S(2)}) collective-permute-start(bf16[512,512]{1,0:T(8,128)(2,1)} %bitcast.19), channel_id=1, source_target_pairs={{0,4},{1,5},{2,0},{3,1},{4,8},{5,9},{6,2},{7,3},{8,12},{9,13},{10,... | collective-permute-start | bytes 1572872 | tf_op jit(solution)/shard_map/ppermute | solution.py:570
  4.5 1.6 %copy-done = bf16[1,128,8192]{2,1,0:T(8,128)(2,1)S(1)} copy-done((bf16[1,128,8192]{2,1,0:T(8,128)(2,1)S(1)}, bf16[1,128,8192]{2,1,0:T(8,128)(2,1)}, u32[]{:S(2)}) %copy-start) | copy-done | bytes 2097176
  6.1 0.7 pick.1
  6.9 1.4 %collective-permute-start.6 = (bf16[3,128,512]{2,1,0:T(8,128)(2,1)S(1)}, bf16[3,128,512]{2,1,0:T(8,128)(2,1)S(1)}, u32[]{:S(2)}, u32[]{:S(2)}) collective-permute-start(bf16[3,128,512]{2,1,0:T(8,128)(2,1)S(1)} %get-tuple-element.84), channel_id=1, source_target_pairs={{16,0},{17,1},{18,2},{19,3},{20,4},{21,5},{22,6},{23,7},{24,8},{25... | collective-permute-start | bytes 1179656 | tf_op jit(solution)/shard_map/ppermute | solution.py:579
  8.3 2.3 %prep.1 = (bf16[8,128,512]{2,1,0:T(8,128)(2,1)S(1)}, bf16[8,128,512]{2,1,0:T(8,128)(2,1)S(1)}, f32[8,1,512]{2,1,0:T(1,128)S(1)}, f32[128,128]{1,0:T(8,128)S(1)}) custom-call(s32[17]{0:T(128)S(1)} %pad_add_fusion.where, bf16[128,8192]{1,0:T(8,128)(2,1)S(1)} %bitcast.15, bf16[128,8192]{1,0:T(8,128)(2,1)S(1)} %bitcast.16, bf16[10,8192]{1,0:T(8,128)(2,1)S(1)} %copy-done.5, ...), custom_call_target="tpu_custom_call" | custom-call | flops 200000000 | bytes 1024 | tf_op jit(solution)/shard_map/prep/pallas_call | solution.py:89
  11.2 3.4 %probs.1 = (f32[4,128,1024]{2,1,0:T(8,128)}, bf16[4,1024,128]{2,1,0:T(8,128)(2,1)}, bf16[4,128,128]{2,1,0:T(8,128)(2,1)}, bf16[128,512]{1,0:T(8,128)(2,1)S(1)}) custom-call(bf16[128,4096]{1,0:T(8,128)(2,1)S(1)} %bitcast.23, bf16[128,512]{1,0:T(8,128)(2,1)S(1)} %bitcast.24, bf16[128,4096]{1,0:T(8,128)(2,1)S(1)} %bitcast.17, ...), custom_call_target="tpu_custom_call" | custom-call | flops 200000000 | bytes 1024 | tf_op jit(solution)/shard_map/probs/pallas_call | solution.py:182
  14.7 0.5 collective-permute-start.4
  15.2 0.6 collective-permute-done.1.refs_5_.refs_3_
  15.8 1.5 %collective-permute-done.refs_4_ = bf16[512,512]{1,0:T(8,128)(2,1)S(1)} collective-permute-done((bf16[512,512]{1,0:T(8,128)(2,1)}, bf16[512,512]{1,0:T(8,128)(2,1)S(1)}, u32[]{:S(2)}, u32[]{:S(2)}) %collective-permute-start) | collective-permute-done | bytes 524320 | tf_op jit(solution)/shard_map/ppermute | solution.py:573
  17.3 1.6 %collective-permute-start.3 = (bf16[256,512]{1,0:T(8,128)(2,1)S(1)}, bf16[256,512]{1,0:T(8,128)(2,1)S(1)}, u32[]{:S(2)}, u32[]{:S(2)}) collective-permute-start(bf16[256,512]{1,0:T(8,128)(2,1)S(1)} %slice.21), channel_id=1, source_target_pairs={{0,4},{1,5},{2,0},{3,1},{4,8},{5,9},{6,2},{7,3},{8,12},{9,13},{10,... | collective-permute-start | bytes 786440 | tf_op jit(solution)/shard_map/ppermute | solution.py:570
  19.4 0.6 first_terms.1
  20.1 1.3 %collective-permute-start.9 = (bf16[3,128,512]{2,1,0:T(8,128)(2,1)S(1)}, bf16[3,128,512]{2,1,0:T(8,128)(2,1)S(1)}, u32[]{:S(2)}, u32[]{:S(2)}) collective-permute-start(bf16[3,128,512]{2,1,0:T(8,128)(2,1)S(1)} %get-tuple-element.105), channel_id=1, source_target_pairs={{16,0},{17,1},{18,2},{19,3},{20,4},{21,5},{22,6},{23,7},{24,8},{25... | collective-permute-start | bytes 1179656 | tf_op jit(solution)/shard_map/ppermute | solution.py:579
  21.4 1.6 %collective-permute-start.11 = (bf16[256,512]{1,0:T(8,128)(2,1)S(1)}, bf16[256,512]{1,0:T(8,128)(2,1)S(1)}, u32[]{:S(2)}, u32[]{:S(2)}) collective-permute-start(bf16[256,512]{1,0:T(8,128)(2,1)S(1)} %slice.25), channel_id=1, source_target_pairs={{0,4},{1,5},{2,0},{3,1},{4,8},{5,9},{6,2},{7,3},{8,12},{9,13},{10,... | collective-permute-start | bytes 786440 | tf_op jit(solution)/shard_map/ppermute | solution.py:570
  23.5 0.6 values.4.refs_6_
  24.1 2.3 %collective-permute-done.3.refs_2_.refs_8_ = bf16[256,512]{1,0:T(8,128)(2,1)S(1)} collective-permute-done((bf16[256,512]{1,0:T(8,128)(2,1)S(1)}, bf16[256,512]{1,0:T(8,128)(2,1)S(1)}, u32[]{:S(2)}, u32[]{:S(2)}) %collective-permute-start.3) | collective-permute-done | bytes 262176 | tf_op jit(solution)/shard_map/ppermute | solution.py:570
  26.3 1.3 %collective-permute-done.2.refs_3_.refs_9_ = bf16[256,512]{1,0:T(8,128)(2,1)S(1)} collective-permute-done((bf16[256,512]{1,0:T(8,128)(2,1)S(1)}, bf16[256,512]{1,0:T(8,128)(2,1)S(1)}, u32[]{:S(2)}, u32[]{:S(2)}) %collective-permute-start.2) | collective-permute-done | bytes 262176 | tf_op jit(solution)/shard_map/ppermute | solution.py:573
  28.1 1.6 %collective-permute-start.8 = (bf16[256,512]{1,0:T(8,128)(2,1)S(1)}, bf16[256,512]{1,0:T(8,128)(2,1)S(1)}, u32[]{:S(2)}, u32[]{:S(2)}) collective-permute-start(bf16[256,512]{1,0:T(8,128)(2,1)S(1)} %collective-permute-done.3.refs_2_.refs_8_), channel_id=1, source_target_pairs={{0,4},{1,5},{2,0},{3,1},{4,8},{5,9},{6,2},{7,3},{8,12},{9,13},{10,... | collective-permute-start | bytes 786440 | tf_op jit(solution)/shard_map/ppermute | solution.py:570
  29.7 2.3 %collective-permute-done.11.refs_4_.refs_10_ = bf16[256,512]{1,0:T(8,128)(2,1)S(1)} collective-permute-done((bf16[256,512]{1,0:T(8,128)(2,1)S(1)}, bf16[256,512]{1,0:T(8,128)(2,1)S(1)}, u32[]{:S(2)}, u32[]{:S(2)}) %collective-permute-start.11) | collective-permute-done | bytes 262176 | tf_op jit(solution)/shard_map/ppermute | solution.py:570
  31.9 1.6 %collective-permute-start.16 = (bf16[256,512]{1,0:T(8,128)(2,1)S(1)}, bf16[256,512]{1,0:T(8,128)(2,1)S(1)}, u32[]{:S(2)}, u32[]{:S(2)}) collective-permute-start(bf16[256,512]{1,0:T(8,128)(2,1)S(1)} %collective-permute-done.11.refs_4_.refs_10_), channel_id=1, source_target_pairs={{0,4},{1,5},{2,0},{3,1},{4,8},{5,9},{6,2},{7,3},{8,12},{9,13},{10,... | collective-permute-start | bytes 786440 | tf_op jit(solution)/shard_map/ppermute | solution.py:570
  34.0 1.3 %collective-permute-start.14 = (bf16[3,128,512]{2,1,0:T(8,128)(2,1)S(1)}, bf16[3,128,512]{2,1,0:T(8,128)(2,1)S(1)}, u32[]{:S(2)}, u32[]{:S(2)}) collective-permute-start(bf16[3,128,512]{2,1,0:T(8,128)(2,1)S(1)} %get-tuple-element.115), channel_id=1, source_target_pairs={{16,1},{17,0},{18,3},{19,2},{20,5},{21,4},{22,7},{23,6},{24,9},{25... | collective-permute-start | bytes 1179656 | tf_op jit(solution)/shard_map/ppermute | solution.py:582
  35.7 1.8 %collective-permute-done.8.refs_2_.refs_12_ = bf16[256,512]{1,0:T(8,128)(2,1)S(1)} collective-permute-done((bf16[256,512]{1,0:T(8,128)(2,1)S(1)}, bf16[256,512]{1,0:T(8,128)(2,1)S(1)}, u32[]{:S(2)}, u32[]{:S(2)}) %collective-permute-start.8) | collective-permute-done | bytes 262176 | tf_op jit(solution)/shard_map/ppermute | solution.py:570
  37.6 1.3 %collective-permute-done.7.refs_3_.refs_13_ = bf16[256,512]{1,0:T(8,128)(2,1)S(1)} collective-permute-done((bf16[256,512]{1,0:T(8,128)(2,1)S(1)}, bf16[256,512]{1,0:T(8,128)(2,1)S(1)}, u32[]{:S(2)}, u32[]{:S(2)}) %collective-permute-start.7) | collective-permute-done | bytes 262176 | tf_op jit(solution)/shard_map/ppermute | solution.py:573
  39.3 1.6 %collective-permute-start.13 = (bf16[256,512]{1,0:T(8,128)(2,1)S(1)}, bf16[256,512]{1,0:T(8,128)(2,1)S(1)}, u32[]{:S(2)}, u32[]{:S(2)}) collective-permute-start(bf16[256,512]{1,0:T(8,128)(2,1)S(1)} %collective-permute-done.8.refs_2_.refs_12_), channel_id=1, source_target_pairs={{0,4},{1,5},{2,0},{3,1},{4,8},{5,9},{6,2},{7,3},{8,12},{9,13},{10,... | collective-permute-start | bytes 786440 | tf_op jit(solution)/shard_map/ppermute | solution.py:570
  40.9 2.3 %collective-permute-done.16.refs_4_.refs_14_ = bf16[256,512]{1,0:T(8,128)(2,1)S(1)} collective-permute-done((bf16[256,512]{1,0:T(8,128)(2,1)S(1)}, bf16[256,512]{1,0:T(8,128)(2,1)S(1)}, u32[]{:S(2)}, u32[]{:S(2)}) %collective-permute-start.16) | collective-permute-done | bytes 262176 | tf_op jit(solution)/shard_map/ppermute | solution.py:570
  43.2 1.3 %collective-permute-done.15.refs_5_.refs_15_ = bf16[256,512]{1,0:T(8,128)(2,1)S(1)} collective-permute-done((bf16[256,512]{1,0:T(8,128)(2,1)S(1)}, bf16[256,512]{1,0:T(8,128)(2,1)S(1)}, u32[]{:S(2)}, u32[]{:S(2)}) %collective-permute-start.15) | collective-permute-done | bytes 262176 | tf_op jit(solution)/shard_map/ppermute | solution.py:573
  44.8 1.6 %collective-permute-start.19 = (bf16[256,512]{1,0:T(8,128)(2,1)S(1)}, bf16[256,512]{1,0:T(8,128)(2,1)S(1)}, u32[]{:S(2)}, u32[]{:S(2)}) collective-permute-start(bf16[256,512]{1,0:T(8,128)(2,1)S(1)} %weight_step.8), channel_id=1, source_target_pairs={{0,4},{1,5},{2,0},{3,1},{4,8},{5,9},{6,2},{7,3},{8,12},{9,13},{10,... | collective-permute-start | bytes 786440 | tf_op jit(solution)/shard_map/ppermute | solution.py:570
  46.6 0.5 collective-permute-start.18
  47.1 1.3 %collective-permute-start.22 = (bf16[3,128,512]{2,1,0:T(8,128)(2,1)S(1)}, bf16[3,128,512]{2,1,0:T(8,128)(2,1)S(1)}, u32[]{:S(2)}, u32[]{:S(2)}) collective-permute-start(bf16[3,128,512]{2,1,0:T(8,128)(2,1)S(1)} %get-tuple-element.127), channel_id=1, source_target_pairs={{16,0},{17,1},{18,2},{19,3},{20,4},{21,5},{22,6},{23,7},{24,8},{25... | collective-permute-start | bytes 1179656 | tf_op jit(solution)/shard_map/ppermute | solution.py:579
  48.9 1.2 %collective-permute-done.12.refs_3_.refs_17_ = bf16[256,512]{1,0:T(8,128)(2,1)S(1)} collective-permute-done((bf16[256,512]{1,0:T(8,128)(2,1)S(1)}, bf16[256,512]{1,0:T(8,128)(2,1)S(1)}, u32[]{:S(2)}, u32[]{:S(2)}) %collective-permute-start.12) | collective-permute-done | bytes 262176 | tf_op jit(solution)/shard_map/ppermute | solution.py:573
  50.6 1.7 %collective-permute-done.19.refs_4_ = bf16[256,512]{1,0:T(8,128)(2,1)S(1)} collective-permute-done((bf16[256,512]{1,0:T(8,128)(2,1)S(1)}, bf16[256,512]{1,0:T(8,128)(2,1)S(1)}, u32[]{:S(2)}, u32[]{:S(2)}) %collective-permute-start.19) | collective-permute-done | bytes 262176 | tf_op jit(solution)/shard_map/ppermute | solution.py:570
  52.6 1.0 %collective-permute-done.18.refs_4_ = bf16[256,512]{1,0:T(8,128)(2,1)S(1)} collective-permute-done((bf16[256,512]{1,0:T(8,128)(2,1)S(1)}, bf16[256,512]{1,0:T(8,128)(2,1)S(1)}, u32[]{:S(2)}, u32[]{:S(2)}) %collective-permute-start.18) | collective-permute-done | bytes 262176 | tf_op jit(solution)/shard_map/ppermute | solution.py:573
  53.9 0.5 collective-permute-start.23
  54.4 1.6 %collective-permute-start.20 = (bf16[512,512]{1,0:T(8,128)(2,1)S(1)}, bf16[512,512]{1,0:T(8,128)(2,1)S(1)}, u32[]{:S(2)}, u32[]{:S(2)}) collective-permute-start(bf16[512,512]{1,0:T(8,128)(2,1)S(1)} %weight_step.10), channel_id=1, source_target_pairs={{0,4},{1,5},{2,0},{3,1},{4,8},{5,9},{6,2},{7,3},{8,12},{9,13},{10,... | collective-permute-start | bytes 1572872 | tf_op jit(solution)/shard_map/ppermute | solution.py:570
  56.0 1.0 %local_grad.1 = (bf16[128,2688]{1,0:T(8,128)(2,1)S(1)}, bf16[128,2560]{1,0:T(8,128)(2,1)S(1)}) custom-call(bf16[8,128,512]{2,1,0:T(8,128)(2,1)S(1)} %get-tuple-element.156.refs_0_.mine, bf16[8,128,512]{2,1,0:T(8,128)(2,1)S(1)} %collective-permute-done.5.refs_1_.theirs, bf16[128,512]{1,0:T(8,128)(2,1)S(1)} %get-tuple-element.141.refs_0_.refs_2_.refs_5_.vgs, ...), custom_call_target="tpu_custom_call" | custom-call | flops 200000000 | bytes 1024 | tf_op jit(solution)/shard_map/local_grad/pallas_call | solution.py:359
  57.0 1.3 %collective-permute-start.26 = (bf16[128,2688]{1,0:T(8,128)(2,1)S(1)}, bf16[128,2688]{1,0:T(8,128)(2,1)S(1)}, u32[]{:S(2)}, u32[]{:S(2)}) collective-permute-start(bf16[128,2688]{1,0:T(8,128)(2,1)S(1)} %get-tuple-element.142), channel_id=1, source_target_pairs={{16,0},{17,1},{18,2},{19,3},{20,4},{21,5},{22,6},{23,7},{24,8},{25... | collective-permute-start | bytes 2064392 | tf_op jit(solution)/shard_map/ppermute | solution.py:579
  58.3 3.5 %back.1 = (bf16[128,4096]{1,0:T(8,128)(2,1)}, bf16[128,512]{1,0:T(8,128)(2,1)}) custom-call(f32[4,128,1024]{2,1,0:T(8,128)S(1)} %copy-done.2, bf16[4,1024,128]{2,1,0:T(8,128)(2,1)S(1)} %copy-done.4, bf16[4,128,128]{2,1,0:T(8,128)(2,1)S(1)} %copy-done.8, bf16[128,4096]{1,0:T(8,128)(2,1)S(1)} %bitcast.18, f32[128,512]{1,0:T(8,128)S(1)} %get-tuple-element.143.u_one, ...), custom_call_target="tpu_custom_call" | custom-call | flops 200000000 | bytes 1024 | tf_op jit(solution)/shard_map/back/pallas_call | solution.py:224
  61.8 1.3 %collective-permute-start.27 = (bf16[128,2560]{1,0:T(8,128)(2,1)S(1)}, bf16[128,2560]{1,0:T(8,128)(2,1)S(1)}, u32[]{:S(2)}, u32[]{:S(2)}) collective-permute-start(bf16[128,2560]{1,0:T(8,128)(2,1)S(1)} %get-tuple-element.159), channel_id=1, source_target_pairs={{16,1},{17,0},{18,3},{19,2},{20,5},{21,4},{22,7},{23,6},{24,9},{25... | collective-permute-start | bytes 1966088 | tf_op jit(solution)/shard_map/ppermute | solution.py:582
  63.1 3.4 %collective-permute-done.20.refs_4_ = bf16[512,512]{1,0:T(8,128)(2,1)S(1)} collective-permute-done((bf16[512,512]{1,0:T(8,128)(2,1)S(1)}, bf16[512,512]{1,0:T(8,128)(2,1)S(1)}, u32[]{:S(2)}, u32[]{:S(2)}) %collective-permute-start.20) | collective-permute-done | bytes 524320 | tf_op jit(solution)/shard_map/ppermute | solution.py:570
  66.9 1.0 %collective-permute-start.21 = (bf16[512,512]{1,0:T(8,128)(2,1)S(1)}, bf16[512,512]{1,0:T(8,128)(2,1)S(1)}, u32[]{:S(2)}, u32[]{:S(2)}) collective-permute-start(bf16[512,512]{1,0:T(8,128)(2,1)S(1)} %weight_step.12), channel_id=1, source_target_pairs={{0,4},{1,5},{2,0},{3,1},{4,8},{5,9},{6,2},{7,3},{8,12},{9,13},{10,... | collective-permute-start | bytes 1572872 | tf_op jit(solution)/shard_map/ppermute | solution.py:570
  68.2 1.1 %collective-permute-start.25 = (bf16[512,512]{1,0:T(8,128)(2,1)S(1)}, bf16[512,512]{1,0:T(8,128)(2,1)S(1)}, u32[]{:S(2)}, u32[]{:S(2)}) collective-permute-start(bf16[512,512]{1,0:T(8,128)(2,1)S(1)} %weight_step.13), channel_id=1, source_target_pairs={{0,2},{1,3},{2,6},{3,7},{4,0},{5,1},{6,10},{7,11},{8,4},{9,5},{10,... | collective-permute-start | bytes 1572872 | tf_op jit(solution)/shard_map/ppermute | solution.py:573
  69.3 8.8 %collective-permute-done.21.refs_4_ = bf16[512,512]{1,0:T(8,128)(2,1)S(1)} collective-permute-done((bf16[512,512]{1,0:T(8,128)(2,1)S(1)}, bf16[512,512]{1,0:T(8,128)(2,1)S(1)}, u32[]{:S(2)}, u32[]{:S(2)}) %collective-permute-start.21) | collective-permute-done | bytes 524320 | tf_op jit(solution)/shard_map/ppermute | solution.py:570
  78.4 0.7 collective-permute-done.25.refs_4_
  79.4 1.9 %collective-permute-start.28 = (bf16[512,512]{1,0:T(8,128)(2,1)S(1)}, bf16[512,512]{1,0:T(8,128)(2,1)S(1)}, u32[]{:S(2)}, u32[]{:S(2)}) collective-permute-start(bf16[512,512]{1,0:T(8,128)(2,1)S(1)} %weight_step.15), channel_id=1, source_target_pairs={{0,2},{1,3},{2,6},{3,7},{4,0},{5,1},{6,10},{7,11},{8,4},{9,5},{10,... | collective-permute-start | bytes 1572872 | tf_op jit(solution)/shard_map/ppermute | solution.py:573
  81.5 1.7 %early_blocks.1.base = bf16[128,8192]{1,0:T(8,128)(2,1)} custom-call(s32[17]{0:T(128)S(1)} %pad_add_fusion.where, f32[8,128]{1,0:T(8,128)S(1)} %fence.19.pin, bf16[3,128,512]{2,1,0:T(8,128)(2,1)S(1)} %collective-permute-done.9.ones, bf16[3,128,512]{2,1,0:T(8,128)(2,1)S(1)} %collective-permute-done.14.twos, ...), custom_call_target="tpu_custom_call" | custom-call | flops 200000000 | bytes 1024 | tf_op jit(solution)/shard_map/early_blocks/pallas_call | solution.py:463
  83.3 2.5 %collective-permute-done.27.refs_0_ = bf16[128,2560]{1,0:T(8,128)(2,1)S(1)} collective-permute-done((bf16[128,2560]{1,0:T(8,128)(2,1)S(1)}, bf16[128,2560]{1,0:T(8,128)(2,1)S(1)}, u32[]{:S(2)}, u32[]{:S(2)}) %collective-permute-start.27) | collective-permute-done | bytes 655392 | tf_op jit(solution)/shard_map/ppermute | solution.py:582
  85.7 1.4 %join.1 = bf16[128,8192]{1,0:T(8,128)(2,1)} custom-call(s32[17]{0:T(128)S(1)} %pad_add_fusion.where, bf16[128,8192]{1,0:T(8,128)(2,1)} %early_blocks.1.base, bf16[128,2560]{1,0:T(8,128)(2,1)S(1)} %collective-permute-done.27.refs_0_), custom_call_target="tpu_custom_call", output_to_operand_aliasing={{}: (1, {})} | custom-call | flops 200000000 | bytes 1024 | tf_op jit(solution)/shard_map/join/pallas_call | solution.py:500
  87.1 3.4 %collective-permute-done.24.f = bf16[512,512]{1,0:T(8,128)(2,1)S(1)} collective-permute-done((bf16[512,512]{1,0:T(8,128)(2,1)S(1)}, bf16[512,512]{1,0:T(8,128)(2,1)S(1)}, u32[]{:S(2)}, u32[]{:S(2)}) %collective-permute-start.24) | collective-permute-done | bytes 524320 | tf_op jit(solution)/shard_map/ppermute | solution.py:570
  90.5 1.1 %weight_last.1 = bf16[512,512]{1,0:T(8,128)(2,1)} custom-call(bf16[8,128,512]{2,1,0:T(8,128)(2,1)S(1)} %get-tuple-element.156.refs_0_.mine, bf16[8,128,512]{2,1,0:T(8,128)(2,1)S(1)} %collective-permute-done.5.refs_1_.theirs, bf16[128,512]{1,0:T(8,128)(2,1)S(1)} %get-tuple-element.141.refs_0_.refs_2_.refs_5_.vgs, ...), custom_call_target="tpu_custom_call" | custom-call | flops 200000000 | bytes 1024 | tf_op jit(solution)/shard_map/weight_last/pallas_call | solution.py:421
  (75 shorter events, 6.9 us)
Async XLA Ops:
  0.6 15.2 %collective-permute-start.1 = (bf16[512,512]{1,0:T(8,128)(2,1)}, bf16[512,512]{1,0:T(8,128)(2,1)S(1)}, u32[]{:S(2)}, u32[]{:S(2)}) collective-permute-start(bf16[512,512]{1,0:T(8,128)(2,1)} %bitcast.19), channel_id=1, source_target_pairs={{0,4},{1,5},{2,0},{3,1},{4,8},{5,9},{6,2},{7,3},{8,12},{9,13},{10,... | collective-permute-start | bytes 1572872 | tf_op jit(solution)/shard_map/ppermute | solution.py:570
  3.7 13.6 %collective-permute-start = (bf16[512,512]{1,0:T(8,128)(2,1)}, bf16[512,512]{1,0:T(8,128)(2,1)S(1)}, u32[]{:S(2)}, u32[]{:S(2)}) collective-permute-start(bf16[512,512]{1,0:T(8,128)(2,1)} %bitcast.20), channel_id=1, source_target_pairs={{0,2},{1,3},{2,6},{3,7},{4,0},{5,1},{6,10},{7,11},{8,4},{9,5},{10,... | collective-permute-start | bytes 1572872 | tf_op jit(solution)/shard_map/ppermute | solution.py:573
  4.5 1.6 %copy-start = (bf16[1,128,8192]{2,1,0:T(8,128)(2,1)S(1)}, bf16[1,128,8192]{2,1,0:T(8,128)(2,1)}, u32[]{:S(2)}) copy-start(bf16[1,128,8192]{2,1,0:T(8,128)(2,1)} %param.8) | copy-start | bytes 6291460
  6.1 2.2 %copy-start.5 = (bf16[10,8192]{1,0:T(8,128)(2,1)S(1)}, bf16[10,8192]{1,0:T(8,128)(2,1)}, u32[]{:S(2)}) copy-start(bf16[10,8192]{1,0:T(8,128)(2,1)} %gain_t.1) | copy-start | bytes 491524
  6.8 3.9 %copy-start.9 = (s32[1,128]{1,0:T(1,128)S(1)}, s32[1,128]{1,0:T(1,128)}, u32[]{:S(2)}) copy-start(s32[1,128]{1,0:T(1,128)} %param.11) | copy-start | bytes 1540
  6.8 4.4 %copy-start.1 = (bf16[1,128,4096]{2,1,0:T(8,128)(2,1)S(1)}, bf16[1,128,4096]{2,1,0:T(8,128)(2,1)}, u32[]{:S(2)}) copy-start(bf16[1,128,4096]{2,1,0:T(8,128)(2,1)} %param.15) | copy-start | bytes 3145732
  6.8 4.4 %copy-start.6 = (bf16[1,128,4096]{2,1,0:T(8,128)(2,1)S(1)}, bf16[1,128,4096]{2,1,0:T(8,128)(2,1)}, u32[]{:S(2)}) copy-start(bf16[1,128,4096]{2,1,0:T(8,128)(2,1)} %param.12) | copy-start | bytes 3145732
  6.8 4.4 %copy-start.7 = (bf16[1,128,512]{2,1,0:T(8,128)(2,1)S(1)}, bf16[1,128,512]{2,1,0:T(8,128)(2,1)}, u32[]{:S(2)}) copy-start(bf16[1,128,512]{2,1,0:T(8,128)(2,1)} %param.13) | copy-start | bytes 393220
  6.9 13.2 %collective-permute-start.6 = (bf16[3,128,512]{2,1,0:T(8,128)(2,1)S(1)}, bf16[3,128,512]{2,1,0:T(8,128)(2,1)S(1)}, u32[]{:S(2)}, u32[]{:S(2)}) collective-permute-start(bf16[3,128,512]{2,1,0:T(8,128)(2,1)S(1)} %get-tuple-element.84), channel_id=1, source_target_pairs={{16,0},{17,1},{18,2},{19,3},{20,4},{21,5},{22,6},{23,7},{24,8},{25... | collective-permute-start | bytes 1179656 | tf_op jit(solution)/shard_map/ppermute | solution.py:579
  10.6 8.8 %collective-permute-start.5 = (bf16[8,128,512]{2,1,0:T(8,128)(2,1)S(1)}, bf16[8,128,512]{2,1,0:T(8,128)(2,1)S(1)}, u32[]{:S(2)}, u32[]{:S(2)}) collective-permute-start(bf16[8,128,512]{2,1,0:T(8,128)(2,1)S(1)} %get-tuple-element.96), channel_id=1, source_target_pairs={{0,1},{1,0},{2,3},{3,2},{4,5},{5,4},{6,7},{7,6},{8,9},{9,8},{10,11... | collective-permute-start | bytes 3145736 | tf_op jit(solution)/shard_map/ppermute | solution.py:576
  14.7 4.8 %collective-permute-start.4 = (bf16[128,512]{1,0:T(8,128)(2,1)S(1)}, bf16[128,512]{1,0:T(8,128)(2,1)S(1)}, u32[]{:S(2)}, u32[]{:S(2)}) collective-permute-start(bf16[128,512]{1,0:T(8,128)(2,1)S(1)} %get-tuple-element.141.refs_0_.refs_2_.refs_5_.vgs), channel_id=1, source_target_pairs={{0,1},{1,0},{2,3},{3,2},{4,5},{5,4},{6,7},{7,6},{8,9},{9,8},{10,11... | collective-permute-start | bytes 393224 | tf_op jit(solution)/shard_map/ppermute | solution.py:576
  15.1 4.3 %copy-start.3 = (bf16[1,512,512]{2,1,0:T(8,128)(2,1)S(1)}, bf16[1,512,512]{2,1,0:T(8,128)(2,1)}, u32[]{:S(2)}) copy-start(bf16[1,512,512]{2,1,0:T(8,128)(2,1)} %param.14) | copy-start | bytes 1572868
  17.3 9.0 %collective-permute-start.3 = (bf16[256,512]{1,0:T(8,128)(2,1)S(1)}, bf16[256,512]{1,0:T(8,128)(2,1)S(1)}, u32[]{:S(2)}, u32[]{:S(2)}) collective-permute-start(bf16[256,512]{1,0:T(8,128)(2,1)S(1)} %slice.21), channel_id=1, source_target_pairs={{0,4},{1,5},{2,0},{3,1},{4,8},{5,9},{6,2},{7,3},{8,12},{9,13},{10,... | collective-permute-start | bytes 786440 | tf_op jit(solution)/shard_map/ppermute | solution.py:570
  19.0 8.7 %collective-permute-start.2 = (bf16[256,512]{1,0:T(8,128)(2,1)S(1)}, bf16[256,512]{1,0:T(8,128)(2,1)S(1)}, u32[]{:S(2)}, u32[]{:S(2)}) collective-permute-start(bf16[256,512]{1,0:T(8,128)(2,1)S(1)} %slice.20), channel_id=1, source_target_pairs={{0,2},{1,3},{2,6},{3,7},{4,0},{5,1},{6,10},{7,11},{8,4},{9,5},{10,... | collective-permute-start | bytes 786440 | tf_op jit(solution)/shard_map/ppermute | solution.py:573
  20.1 13.9 %collective-permute-start.9 = (bf16[3,128,512]{2,1,0:T(8,128)(2,1)S(1)}, bf16[3,128,512]{2,1,0:T(8,128)(2,1)S(1)}, u32[]{:S(2)}, u32[]{:S(2)}) collective-permute-start(bf16[3,128,512]{2,1,0:T(8,128)(2,1)S(1)} %get-tuple-element.105), channel_id=1, source_target_pairs={{16,0},{17,1},{18,2},{19,3},{20,4},{21,5},{22,6},{23,7},{24,8},{25... | collective-permute-start | bytes 1179656 | tf_op jit(solution)/shard_map/ppermute | solution.py:579
  21.4 10.5 %collective-permute-start.11 = (bf16[256,512]{1,0:T(8,128)(2,1)S(1)}, bf16[256,512]{1,0:T(8,128)(2,1)S(1)}, u32[]{:S(2)}, u32[]{:S(2)}) collective-permute-start(bf16[256,512]{1,0:T(8,128)(2,1)S(1)} %slice.25), channel_id=1, source_target_pairs={{0,4},{1,5},{2,0},{3,1},{4,8},{5,9},{6,2},{7,3},{8,12},{9,13},{10,... | collective-permute-start | bytes 786440 | tf_op jit(solution)/shard_map/ppermute | solution.py:570
  23.0 10.5 %collective-permute-start.10 = (bf16[256,512]{1,0:T(8,128)(2,1)S(1)}, bf16[256,512]{1,0:T(8,128)(2,1)S(1)}, u32[]{:S(2)}, u32[]{:S(2)}) collective-permute-start(bf16[256,512]{1,0:T(8,128)(2,1)S(1)} %slice.24), channel_id=1, source_target_pairs={{0,2},{1,3},{2,6},{3,7},{4,0},{5,1},{6,10},{7,11},{8,4},{9,5},{10,... | collective-permute-start | bytes 786440 | tf_op jit(solution)/shard_map/ppermute | solution.py:573
  27.7 11.2 %collective-permute-start.7 = (bf16[256,512]{1,0:T(8,128)(2,1)S(1)}, bf16[256,512]{1,0:T(8,128)(2,1)S(1)}, u32[]{:S(2)}, u32[]{:S(2)}) collective-permute-start(bf16[256,512]{1,0:T(8,128)(2,1)S(1)} %collective-permute-done.2.refs_3_.refs_9_), channel_id=1, source_target_pairs={{0,2},{1,3},{2,6},{3,7},{4,0},{5,1},{6,10},{7,11},{8,4},{9,5},{10,... | collective-permute-start | bytes 786440 | tf_op jit(solution)/shard_map/ppermute | solution.py:573
  28.1 9.4 %collective-permute-start.8 = (bf16[256,512]{1,0:T(8,128)(2,1)S(1)}, bf16[256,512]{1,0:T(8,128)(2,1)S(1)}, u32[]{:S(2)}, u32[]{:S(2)}) collective-permute-start(bf16[256,512]{1,0:T(8,128)(2,1)S(1)} %collective-permute-done.3.refs_2_.refs_8_), channel_id=1, source_target_pairs={{0,4},{1,5},{2,0},{3,1},{4,8},{5,9},{6,2},{7,3},{8,12},{9,13},{10,... | collective-permute-start | bytes 786440 | tf_op jit(solution)/shard_map/ppermute | solution.py:570
  31.9 11.2 %collective-permute-start.16 = (bf16[256,512]{1,0:T(8,128)(2,1)S(1)}, bf16[256,512]{1,0:T(8,128)(2,1)S(1)}, u32[]{:S(2)}, u32[]{:S(2)}) collective-permute-start(bf16[256,512]{1,0:T(8,128)(2,1)S(1)} %collective-permute-done.11.refs_4_.refs_10_), channel_id=1, source_target_pairs={{0,4},{1,5},{2,0},{3,1},{4,8},{5,9},{6,2},{7,3},{8,12},{9,13},{10,... | collective-permute-start | bytes 786440 | tf_op jit(solution)/shard_map/ppermute | solution.py:570
  33.5 11.0 %collective-permute-start.15 = (bf16[256,512]{1,0:T(8,128)(2,1)S(1)}, bf16[256,512]{1,0:T(8,128)(2,1)S(1)}, u32[]{:S(2)}, u32[]{:S(2)}) collective-permute-start(bf16[256,512]{1,0:T(8,128)(2,1)S(1)} %collective-permute-done.10.refs_5_.refs_11_), channel_id=1, source_target_pairs={{0,2},{1,3},{2,6},{3,7},{4,0},{5,1},{6,10},{7,11},{8,4},{9,5},{10,... | collective-permute-start | bytes 786440 | tf_op jit(solution)/shard_map/ppermute | solution.py:573
  34.0 13.2 %collective-permute-start.14 = (bf16[3,128,512]{2,1,0:T(8,128)(2,1)S(1)}, bf16[3,128,512]{2,1,0:T(8,128)(2,1)S(1)}, u32[]{:S(2)}, u32[]{:S(2)}) collective-permute-start(bf16[3,128,512]{2,1,0:T(8,128)(2,1)S(1)} %get-tuple-element.115), channel_id=1, source_target_pairs={{16,1},{17,0},{18,3},{19,2},{20,5},{21,4},{22,7},{23,6},{24,9},{25... | collective-permute-start | bytes 1179656 | tf_op jit(solution)/shard_map/ppermute | solution.py:582
  38.9 11.2 %collective-permute-start.12 = (bf16[256,512]{1,0:T(8,128)(2,1)S(1)}, bf16[256,512]{1,0:T(8,128)(2,1)S(1)}, u32[]{:S(2)}, u32[]{:S(2)}) collective-permute-start(bf16[256,512]{1,0:T(8,128)(2,1)S(1)} %collective-permute-done.7.refs_3_.refs_13_), channel_id=1, source_target_pairs={{0,2},{1,3},{2,6},{3,7},{4,0},{5,1},{6,10},{7,11},{8,4},{9,5},{10,... | collective-permute-start | bytes 786440 | tf_op jit(solution)/shard_map/ppermute | solution.py:573
  39.3 9.5 %collective-permute-start.13 = (bf16[256,512]{1,0:T(8,128)(2,1)S(1)}, bf16[256,512]{1,0:T(8,128)(2,1)S(1)}, u32[]{:S(2)}, u32[]{:S(2)}) collective-permute-start(bf16[256,512]{1,0:T(8,128)(2,1)S(1)} %collective-permute-done.8.refs_2_.refs_12_), channel_id=1, source_target_pairs={{0,4},{1,5},{2,0},{3,1},{4,8},{5,9},{6,2},{7,3},{8,12},{9,13},{10,... | collective-permute-start | bytes 786440 | tf_op jit(solution)/shard_map/ppermute | solution.py:570
  44.8 7.6 %collective-permute-start.19 = (bf16[256,512]{1,0:T(8,128)(2,1)S(1)}, bf16[256,512]{1,0:T(8,128)(2,1)S(1)}, u32[]{:S(2)}, u32[]{:S(2)}) collective-permute-start(bf16[256,512]{1,0:T(8,128)(2,1)S(1)} %weight_step.8), channel_id=1, source_target_pairs={{0,4},{1,5},{2,0},{3,1},{4,8},{5,9},{6,2},{7,3},{8,12},{9,13},{10,... | collective-permute-start | bytes 786440 | tf_op jit(solution)/shard_map/ppermute | solution.py:570
  46.6 7.0 %collective-permute-start.18 = (bf16[256,512]{1,0:T(8,128)(2,1)S(1)}, bf16[256,512]{1,0:T(8,128)(2,1)S(1)}, u32[]{:S(2)}, u32[]{:S(2)}) collective-permute-start(bf16[256,512]{1,0:T(8,128)(2,1)S(1)} %weight_step.9), channel_id=1, source_target_pairs={{0,2},{1,3},{2,6},{3,7},{4,0},{5,1},{6,10},{7,11},{8,4},{9,5},{10,... | collective-permute-start | bytes 786440 | tf_op jit(solution)/shard_map/ppermute | solution.py:573
  47.1 22.2 %collective-permute-start.22 = (bf16[3,128,512]{2,1,0:T(8,128)(2,1)S(1)}, bf16[3,128,512]{2,1,0:T(8,128)(2,1)S(1)}, u32[]{:S(2)}, u32[]{:S(2)}) collective-permute-start(bf16[3,128,512]{2,1,0:T(8,128)(2,1)S(1)} %get-tuple-element.127), channel_id=1, source_target_pairs={{16,0},{17,1},{18,2},{19,3},{20,4},{21,5},{22,6},{23,7},{24,8},{25... | collective-permute-start | bytes 1179656 | tf_op jit(solution)/shard_map/ppermute | solution.py:579
  50.5 5.5 %collective-permute-start.17 = (f32[128,896]{1,0:T(8,128)S(1)}, f32[128,896]{1,0:T(8,128)S(1)}, u32[]{:S(2)}, u32[]{:S(2)}) collective-permute-start(f32[128,896]{1,0:T(8,128)S(1)} %get-tuple-element.134.refs_6_), channel_id=1, source_target_pairs={{0,1},{1,0},{2,3},{3,2},{4,5},{5,4},{6,7},{7,6},{8,9},{9,8},{10,11... | collective-permute-start | bytes 1376264 | tf_op jit(solution)/shard_map/ppermute | solution.py:576
  53.9 14.0 %collective-permute-start.23 = (bf16[512,512]{1,0:T(8,128)(2,1)S(1)}, bf16[512,512]{1,0:T(8,128)(2,1)S(1)}, u32[]{:S(2)}, u32[]{:S(2)}) collective-permute-start(bf16[512,512]{1,0:T(8,128)(2,1)S(1)} %weight_step.11), channel_id=1, source_target_pairs={{0,2},{1,3},{2,6},{3,7},{4,0},{5,1},{6,10},{7,11},{8,4},{9,5},{10,... | collective-permute-start | bytes 1572872 | tf_op jit(solution)/shard_map/ppermute | solution.py:573
  54.4 12.1 %collective-permute-start.20 = (bf16[512,512]{1,0:T(8,128)(2,1)S(1)}, bf16[512,512]{1,0:T(8,128)(2,1)S(1)}, u32[]{:S(2)}, u32[]{:S(2)}) collective-permute-start(bf16[512,512]{1,0:T(8,128)(2,1)S(1)} %weight_step.10), channel_id=1, source_target_pairs={{0,4},{1,5},{2,0},{3,1},{4,8},{5,9},{6,2},{7,3},{8,12},{9,13},{10,... | collective-permute-start | bytes 1572872 | tf_op jit(solution)/shard_map/ppermute | solution.py:570
  56.0 2.3 %copy-start.2 = (f32[4,128,1024]{2,1,0:T(8,128)S(1)}, f32[4,128,1024]{2,1,0:T(8,128)}, u32[]{:S(2)}) copy-start(f32[4,128,1024]{2,1,0:T(8,128)} %get-tuple-element.89.probs) | copy-start | bytes 6291460
  56.0 2.3 %copy-start.4 = (bf16[4,1024,128]{2,1,0:T(8,128)(2,1)S(1)}, bf16[4,1024,128]{2,1,0:T(8,128)(2,1)}, u32[]{:S(2)}) copy-start(bf16[4,1024,128]{2,1,0:T(8,128)(2,1)} %get-tuple-element.90.q_rot) | copy-start | bytes 3145732
  56.0 2.3 %copy-start.8 = (bf16[4,128,128]{2,1,0:T(8,128)(2,1)S(1)}, bf16[4,128,128]{2,1,0:T(8,128)(2,1)}, u32[]{:S(2)}) copy-start(bf16[4,128,128]{2,1,0:T(8,128)(2,1)} %get-tuple-element.91.k_rot) | copy-start | bytes 393220
  57.0 24.5 %collective-permute-start.26 = (bf16[128,2688]{1,0:T(8,128)(2,1)S(1)}, bf16[128,2688]{1,0:T(8,128)(2,1)S(1)}, u32[]{:S(2)}, u32[]{:S(2)}) collective-permute-start(bf16[128,2688]{1,0:T(8,128)(2,1)S(1)} %get-tuple-element.142), channel_id=1, source_target_pairs={{16,0},{17,1},{18,2},{19,3},{20,4},{21,5},{22,6},{23,7},{24,8},{25... | collective-permute-start | bytes 2064392 | tf_op jit(solution)/shard_map/ppermute | solution.py:579
  61.8 23.9 %collective-permute-start.27 = (bf16[128,2560]{1,0:T(8,128)(2,1)S(1)}, bf16[128,2560]{1,0:T(8,128)(2,1)S(1)}, u32[]{:S(2)}, u32[]{:S(2)}) collective-permute-start(bf16[128,2560]{1,0:T(8,128)(2,1)S(1)} %get-tuple-element.159), channel_id=1, source_target_pairs={{16,1},{17,0},{18,3},{19,2},{20,5},{21,4},{22,7},{23,6},{24,9},{25... | collective-permute-start | bytes 1966088 | tf_op jit(solution)/shard_map/ppermute | solution.py:582
  66.9 11.2 %collective-permute-start.21 = (bf16[512,512]{1,0:T(8,128)(2,1)S(1)}, bf16[512,512]{1,0:T(8,128)(2,1)S(1)}, u32[]{:S(2)}, u32[]{:S(2)}) collective-permute-start(bf16[512,512]{1,0:T(8,128)(2,1)S(1)} %weight_step.12), channel_id=1, source_target_pairs={{0,4},{1,5},{2,0},{3,1},{4,8},{5,9},{6,2},{7,3},{8,12},{9,13},{10,... | collective-permute-start | bytes 1572872 | tf_op jit(solution)/shard_map/ppermute | solution.py:570
  68.2 10.9 %collective-permute-start.25 = (bf16[512,512]{1,0:T(8,128)(2,1)S(1)}, bf16[512,512]{1,0:T(8,128)(2,1)S(1)}, u32[]{:S(2)}, u32[]{:S(2)}) collective-permute-start(bf16[512,512]{1,0:T(8,128)(2,1)S(1)} %weight_step.13), channel_id=1, source_target_pairs={{0,2},{1,3},{2,6},{3,7},{4,0},{5,1},{6,10},{7,11},{8,4},{9,5},{10,... | collective-permute-start | bytes 1572872 | tf_op jit(solution)/shard_map/ppermute | solution.py:573
  79.4 11.1 %collective-permute-start.28 = (bf16[512,512]{1,0:T(8,128)(2,1)S(1)}, bf16[512,512]{1,0:T(8,128)(2,1)S(1)}, u32[]{:S(2)}, u32[]{:S(2)}) collective-permute-start(bf16[512,512]{1,0:T(8,128)(2,1)S(1)} %weight_step.15), channel_id=1, source_target_pairs={{0,2},{1,3},{2,6},{3,7},{4,0},{5,1},{6,10},{7,11},{8,4},{9,5},{10,... | collective-permute-start | bytes 1572872 | tf_op jit(solution)/shard_map/ppermute | solution.py:573
  81.4 9.2 %collective-permute-start.24 = (bf16[512,512]{1,0:T(8,128)(2,1)S(1)}, bf16[512,512]{1,0:T(8,128)(2,1)S(1)}, u32[]{:S(2)}, u32[]{:S(2)}) collective-permute-start(bf16[512,512]{1,0:T(8,128)(2,1)S(1)} %weight_step.14), channel_id=1, source_target_pairs={{0,4},{1,5},{2,0},{3,1},{4,8},{5,9},{6,2},{7,3},{8,12},{9,13},{10,... | collective-permute-start | bytes 1572872 | tf_op jit(solution)/shard_map/ppermute | solution.py:570

commit v5 on v4

--- a/solution.py
+++ b/solution.py
@@ -400,6 +400,35 @@
         compiler_params=params(),
         cost_estimate=SMALL,
         name="weight_step",
+    )(mine, theirs, vgs, vgs_t, *arrived)
+
+
+def weight_both_kernel(*refs, parts):
+    mine, theirs, vgs, vgs_t = refs[:4]
+    arrived, outs = refs[4:-2], refs[-2:]
+    right = both_vgs(vgs, vgs_t)
+    for i, (part, out) in enumerate(zip(parts, outs, strict=True)):
+        total = mm(pair(mine, theirs, part), right, (0, 0))
+        rows = total.shape[0]
+        if arrived:
+            more = arrived[i][...].astype(F32)
+            if more.shape[0] == rows:
+                total = total + more
+            elif i == 0:
+                total = jnp.concatenate([total[: rows // 2] + more, total[rows // 2 :]], axis=0)
+            else:
+                total = jnp.concatenate([total[: rows // 2], total[rows // 2 :] + more], axis=0)
+        out[...] = total.astype(BF16)
+
+
+def weight_both(mine, theirs, vgs, vgs_t, parts, arrived):
+    ats = [span(part, mine.shape[2]) for part in parts]
+    return pl.pallas_call(
+        functools.partial(weight_both_kernel, parts=parts),
+        out_shape=[sds((at.stop - at.start, vgs.shape[1]), BF16) for at in ats],
+        compiler_params=params(),
+        cost_estimate=SMALL,
+        name="weight_both",
     )(mine, theirs, vgs, vgs_t, *arrived)
 
 
@@ -660,11 +689,12 @@
             total = then(values_sum(after(mine), theirs, parts, weights(parts), (total,)))
             hold(H[3])
 
-    def weight_part(part, *arrived):
-        return then(weight_step(after(mine), theirs, vgs, vgs_t, part, *arrived))
-
-    f = ahead(weight_part((half, 0)))
-    b = behind(weight_part((half, 1)))
+    def weight_parts(parts, *arrived):
+        arrived = [after(x) for x in arrived]
+        f, b = then(*weight_both(after(mine), theirs, vgs, vgs_t, parts, arrived))
+        return ahead(f), behind(b)
+
+    f, b = weight_parts(((half, 0), (half, 1)))
     two = after(two)
     raw_t = sent_down(after(raw_t))
     hold(H[4])
@@ -676,13 +706,16 @@
     u_mine, packed = values_sum(after(mine), theirs, parts, weights(parts), (total,), (vgs, vgs_t, inverse))
     got = swapped(then(packed))
 
+    def weight_part(part, *arrived):
+        return then(weight_step(after(mine), theirs, vgs, vgs_t, part, *arrived))
+
     def weight_turn(r, f, b):
         f = ahead(weight_part((r, None), after(f)))
         b = behind(weight_part((chips - r, None), None, after(b)))
         return f, b
 
     if half > 2:
-        f, b = weight_turn(half - 1, f, b)
+        f, b = weight_parts(((half - 1, None), (half + 1, None)), f, b)
     hold(H[5])
     got = after(got)
     parts = parts_of(sum(later, []))

time: 93 us -> 92.7 us (level)
    ppermute x10, waiting for transfers between devices: 8.38 us -> 10.5 us  [behind(): return lax.ppermute(x, 'dp', back)]
    ppermute x10, starting transfers between devices: 6.29 us -> 4.41 us  [behind(): return lax.ppermute(x, 'dp', back)]
    ppermute x10, starting transfers between devices: 15.4 us -> 17.3 us  [ahead(): return lax.ppermute(x, 'dp', forth)]
    ppermute x10, waiting for transfers between devices: 26.5 us -> 25.2 us  [ahead(): return lax.ppermute(x, 'dp', forth)]
    pallas_call x8 -> x4, Pallas kernels: 2.42 us -> 1.29 us  [weight_step(): pl.pallas_call(kernel, out_shape=sds((at.stop - at.start, vgs.shape[1]),...]
  transfers between devices with their start and end apart: 29 -> 29, of which waited for: 17 -> 19; matrix products, arithmetic and copies ran while one was open for 1% -> 1% of each run, Pallas kernels for 21% -> 20%
where the time goes in v5:
time: 92.7 us; the launch traced here: 91.2 us
  waiting for transfers between devices  37.4 us (40%)
  starting transfers between devices  30.2 us (33%)
  Pallas kernels  19.7 us (21%)
  local copies, waits for them, and re-layouts  1.72 us (2%)
  between operations  1.71 us (2%)
    ppermute x10, waiting for transfers between devices, ahead(): return lax.ppermute(x, 'dp', forth)  25.2 us
    ppermute x10, starting transfers between devices, ahead(): return lax.ppermute(x, 'dp', forth)  17.3 us
    ppermute x10, waiting for transfers between devices, behind(): return lax.ppermute(x, 'dp', back)  10.5 us
    ppermute x4, starting transfers between devices, sent_down(): return lax.ppermute(x, ('section', 'dp'), down)  5.29 us
    ppermute x10, starting transfers between devices, behind(): return lax.ppermute(x, 'dp', back)  4.41 us
    pallas_call x1, Pallas kernels, attention_back(): pl.pallas_call(back_kernel, grid=(HK,), in_specs=[pl.BlockSpec((1, tokens...  3.49 us
    pallas_call x1, Pallas kernels, attention_probs(): pl.pallas_call(probs_kernel, grid=(HK,), in_specs=[group, head, group, ta...  3.44 us
    ppermute x2, starting transfers between devices, sent_across(): return lax.ppermute(x, ('section', 'dp'), cross)  2.56 us
  transfers between devices with their start and end apart: 29, of which 19 were waited for; matrix products, arithmetic and copies ran while one was open for 1% of the time, Pallas kernels for 20%

profile of v5, /device:TPU:0, one launch (start us, length us, event | category | flops | bytes accessed | tf_op | source)
XLA Modules:
  0.0 91.2 jit_solution(6872908337458712356)
XLA Ops:
  0.6 3.1 %collective-permute-start.1 = (bf16[512,512]{1,0:T(8,128)(2,1)}, bf16[512,512]{1,0:T(8,128)(2,1)S(1)}, u32[]{:S(2)}, u32[]{:S(2)}) collective-permute-start(bf16[512,512]{1,0:T(8,128)(2,1)} %bitcast.19), channel_id=1, source_target_pairs={{0,4},{1,5},{2,0},{3,1},{4,8},{5,9},{6,2},{7,3},{8,12},{9,13},{10,... | collective-permute-start | bytes 1572872 | tf_op jit(solution)/shard_map/ppermute | solution.py:599
  4.5 1.6 %copy-done = bf16[1,128,8192]{2,1,0:T(8,128)(2,1)S(1)} copy-done((bf16[1,128,8192]{2,1,0:T(8,128)(2,1)S(1)}, bf16[1,128,8192]{2,1,0:T(8,128)(2,1)}, u32[]{:S(2)}) %copy-start) | copy-done | bytes 2097176
  6.1 0.7 pick.1
  6.9 1.4 %collective-permute-start.6 = (bf16[3,128,512]{2,1,0:T(8,128)(2,1)S(1)}, bf16[3,128,512]{2,1,0:T(8,128)(2,1)S(1)}, u32[]{:S(2)}, u32[]{:S(2)}) collective-permute-start(bf16[3,128,512]{2,1,0:T(8,128)(2,1)S(1)} %get-tuple-element.86), channel_id=1, source_target_pairs={{16,0},{17,1},{18,2},{19,3},{20,4},{21,5},{22,6},{23,7},{24,8},{25... | collective-permute-start | bytes 1179656 | tf_op jit(solution)/shard_map/ppermute | solution.py:608
  8.3 2.3 %prep.1 = (bf16[8,128,512]{2,1,0:T(8,128)(2,1)S(1)}, bf16[8,128,512]{2,1,0:T(8,128)(2,1)S(1)}, f32[8,1,512]{2,1,0:T(1,128)S(1)}, f32[128,128]{1,0:T(8,128)S(1)}) custom-call(s32[17]{0:T(128)S(1)} %pad_add_fusion.where, bf16[128,8192]{1,0:T(8,128)(2,1)S(1)} %bitcast.15, bf16[128,8192]{1,0:T(8,128)(2,1)S(1)} %bitcast.16, bf16[10,8192]{1,0:T(8,128)(2,1)S(1)} %copy-done.5, ...), custom_call_target="tpu_custom_call" | custom-call | flops 200000000 | bytes 1024 | tf_op jit(solution)/shard_map/prep/pallas_call | solution.py:89
  11.2 3.4 %probs.1 = (f32[4,128,1024]{2,1,0:T(8,128)}, bf16[4,1024,128]{2,1,0:T(8,128)(2,1)}, bf16[4,128,128]{2,1,0:T(8,128)(2,1)}, bf16[128,512]{1,0:T(8,128)(2,1)S(1)}) custom-call(bf16[128,4096]{1,0:T(8,128)(2,1)S(1)} %bitcast.23, bf16[128,512]{1,0:T(8,128)(2,1)S(1)} %bitcast.24, bf16[128,4096]{1,0:T(8,128)(2,1)S(1)} %bitcast.17, ...), custom_call_target="tpu_custom_call" | custom-call | flops 200000000 | bytes 1024 | tf_op jit(solution)/shard_map/probs/pallas_call | solution.py:182
  14.7 0.5 collective-permute-start.4
  15.2 0.6 collective-permute-done.1.refs_5_.refs_3_
  15.8 1.5 %collective-permute-done.refs_4_ = bf16[512,512]{1,0:T(8,128)(2,1)S(1)} collective-permute-done((bf16[512,512]{1,0:T(8,128)(2,1)}, bf16[512,512]{1,0:T(8,128)(2,1)S(1)}, u32[]{:S(2)}, u32[]{:S(2)}) %collective-permute-start) | collective-permute-done | bytes 524320 | tf_op jit(solution)/shard_map/ppermute | solution.py:602
  17.3 1.6 %collective-permute-start.3 = (bf16[256,512]{1,0:T(8,128)(2,1)S(1)}, bf16[256,512]{1,0:T(8,128)(2,1)S(1)}, u32[]{:S(2)}, u32[]{:S(2)}) collective-permute-start(bf16[256,512]{1,0:T(8,128)(2,1)S(1)} %slice.21), channel_id=1, source_target_pairs={{0,4},{1,5},{2,0},{3,1},{4,8},{5,9},{6,2},{7,3},{8,12},{9,13},{10,... | collective-permute-start | bytes 786440 | tf_op jit(solution)/shard_map/ppermute | solution.py:599
  19.4 0.6 first_terms.1
  20.1 1.3 %collective-permute-start.9 = (bf16[3,128,512]{2,1,0:T(8,128)(2,1)S(1)}, bf16[3,128,512]{2,1,0:T(8,128)(2,1)S(1)}, u32[]{:S(2)}, u32[]{:S(2)}) collective-permute-start(bf16[3,128,512]{2,1,0:T(8,128)(2,1)S(1)} %get-tuple-element.107), channel_id=1, source_target_pairs={{16,0},{17,1},{18,2},{19,3},{20,4},{21,5},{22,6},{23,7},{24,8},{25... | collective-permute-start | bytes 1179656 | tf_op jit(solution)/shard_map/ppermute | solution.py:608
  21.4 1.6 %collective-permute-start.11 = (bf16[256,512]{1,0:T(8,128)(2,1)S(1)}, bf16[256,512]{1,0:T(8,128)(2,1)S(1)}, u32[]{:S(2)}, u32[]{:S(2)}) collective-permute-start(bf16[256,512]{1,0:T(8,128)(2,1)S(1)} %slice.25), channel_id=1, source_target_pairs={{0,4},{1,5},{2,0},{3,1},{4,8},{5,9},{6,2},{7,3},{8,12},{9,13},{10,... | collective-permute-start | bytes 786440 | tf_op jit(solution)/shard_map/ppermute | solution.py:599
  23.5 0.6 values.4.refs_6_
  24.1 2.3 %collective-permute-done.3.refs_2_.refs_8_ = bf16[256,512]{1,0:T(8,128)(2,1)S(1)} collective-permute-done((bf16[256,512]{1,0:T(8,128)(2,1)S(1)}, bf16[256,512]{1,0:T(8,128)(2,1)S(1)}, u32[]{:S(2)}, u32[]{:S(2)}) %collective-permute-start.3) | collective-permute-done | bytes 262176 | tf_op jit(solution)/shard_map/ppermute | solution.py:599
  26.3 1.3 %collective-permute-done.2.refs_3_.refs_9_ = bf16[256,512]{1,0:T(8,128)(2,1)S(1)} collective-permute-done((bf16[256,512]{1,0:T(8,128)(2,1)S(1)}, bf16[256,512]{1,0:T(8,128)(2,1)S(1)}, u32[]{:S(2)}, u32[]{:S(2)}) %collective-permute-start.2) | collective-permute-done | bytes 262176 | tf_op jit(solution)/shard_map/ppermute | solution.py:602
  28.1 1.6 %collective-permute-start.8 = (bf16[256,512]{1,0:T(8,128)(2,1)S(1)}, bf16[256,512]{1,0:T(8,128)(2,1)S(1)}, u32[]{:S(2)}, u32[]{:S(2)}) collective-permute-start(bf16[256,512]{1,0:T(8,128)(2,1)S(1)} %collective-permute-done.3.refs_2_.refs_8_), channel_id=1, source_target_pairs={{0,4},{1,5},{2,0},{3,1},{4,8},{5,9},{6,2},{7,3},{8,12},{9,13},{10,... | collective-permute-start | bytes 786440 | tf_op jit(solution)/shard_map/ppermute | solution.py:599
  29.7 2.3 %collective-permute-done.11.refs_4_.refs_10_ = bf16[256,512]{1,0:T(8,128)(2,1)S(1)} collective-permute-done((bf16[256,512]{1,0:T(8,128)(2,1)S(1)}, bf16[256,512]{1,0:T(8,128)(2,1)S(1)}, u32[]{:S(2)}, u32[]{:S(2)}) %collective-permute-start.11) | collective-permute-done | bytes 262176 | tf_op jit(solution)/shard_map/ppermute | solution.py:599
  31.9 1.6 %collective-permute-start.16 = (bf16[256,512]{1,0:T(8,128)(2,1)S(1)}, bf16[256,512]{1,0:T(8,128)(2,1)S(1)}, u32[]{:S(2)}, u32[]{:S(2)}) collective-permute-start(bf16[256,512]{1,0:T(8,128)(2,1)S(1)} %collective-permute-done.11.refs_4_.refs_10_), channel_id=1, source_target_pairs={{0,4},{1,5},{2,0},{3,1},{4,8},{5,9},{6,2},{7,3},{8,12},{9,13},{10,... | collective-permute-start | bytes 786440 | tf_op jit(solution)/shard_map/ppermute | solution.py:599
  34.0 1.3 %collective-permute-start.14 = (bf16[3,128,512]{2,1,0:T(8,128)(2,1)S(1)}, bf16[3,128,512]{2,1,0:T(8,128)(2,1)S(1)}, u32[]{:S(2)}, u32[]{:S(2)}) collective-permute-start(bf16[3,128,512]{2,1,0:T(8,128)(2,1)S(1)} %get-tuple-element.117), channel_id=1, source_target_pairs={{16,1},{17,0},{18,3},{19,2},{20,5},{21,4},{22,7},{23,6},{24,9},{25... | collective-permute-start | bytes 1179656 | tf_op jit(solution)/shard_map/ppermute | solution.py:611
  35.7 1.8 %collective-permute-done.8.refs_2_.refs_12_ = bf16[256,512]{1,0:T(8,128)(2,1)S(1)} collective-permute-done((bf16[256,512]{1,0:T(8,128)(2,1)S(1)}, bf16[256,512]{1,0:T(8,128)(2,1)S(1)}, u32[]{:S(2)}, u32[]{:S(2)}) %collective-permute-start.8) | collective-permute-done | bytes 262176 | tf_op jit(solution)/shard_map/ppermute | solution.py:599
  37.6 1.3 %collective-permute-done.7.refs_3_.refs_13_ = bf16[256,512]{1,0:T(8,128)(2,1)S(1)} collective-permute-done((bf16[256,512]{1,0:T(8,128)(2,1)S(1)}, bf16[256,512]{1,0:T(8,128)(2,1)S(1)}, u32[]{:S(2)}, u32[]{:S(2)}) %collective-permute-start.7) | collective-permute-done | bytes 262176 | tf_op jit(solution)/shard_map/ppermute | solution.py:602
  39.3 1.6 %collective-permute-start.13 = (bf16[256,512]{1,0:T(8,128)(2,1)S(1)}, bf16[256,512]{1,0:T(8,128)(2,1)S(1)}, u32[]{:S(2)}, u32[]{:S(2)}) collective-permute-start(bf16[256,512]{1,0:T(8,128)(2,1)S(1)} %collective-permute-done.8.refs_2_.refs_12_), channel_id=1, source_target_pairs={{0,4},{1,5},{2,0},{3,1},{4,8},{5,9},{6,2},{7,3},{8,12},{9,13},{10,... | collective-permute-start | bytes 786440 | tf_op jit(solution)/shard_map/ppermute | solution.py:599
  40.9 2.3 %collective-permute-done.16.refs_4_.refs_14_ = bf16[256,512]{1,0:T(8,128)(2,1)S(1)} collective-permute-done((bf16[256,512]{1,0:T(8,128)(2,1)S(1)}, bf16[256,512]{1,0:T(8,128)(2,1)S(1)}, u32[]{:S(2)}, u32[]{:S(2)}) %collective-permute-start.16) | collective-permute-done | bytes 262176 | tf_op jit(solution)/shard_map/ppermute | solution.py:599
  43.2 1.3 %collective-permute-done.15.refs_5_.refs_15_ = bf16[256,512]{1,0:T(8,128)(2,1)S(1)} collective-permute-done((bf16[256,512]{1,0:T(8,128)(2,1)S(1)}, bf16[256,512]{1,0:T(8,128)(2,1)S(1)}, u32[]{:S(2)}, u32[]{:S(2)}) %collective-permute-start.15) | collective-permute-done | bytes 262176 | tf_op jit(solution)/shard_map/ppermute | solution.py:602
  44.8 1.6 %collective-permute-start.19 = (bf16[256,512]{1,0:T(8,128)(2,1)S(1)}, bf16[256,512]{1,0:T(8,128)(2,1)S(1)}, u32[]{:S(2)}, u32[]{:S(2)}) collective-permute-start(bf16[256,512]{1,0:T(8,128)(2,1)S(1)} %get-tuple-element.127), channel_id=1, source_target_pairs={{0,4},{1,5},{2,0},{3,1},{4,8},{5,9},{6,2},{7,3},{8,12},{9,13},{10,... | collective-permute-start | bytes 786440 | tf_op jit(solution)/shard_map/ppermute | solution.py:599
  47.0 1.3 %collective-permute-start.22 = (bf16[3,128,512]{2,1,0:T(8,128)(2,1)S(1)}, bf16[3,128,512]{2,1,0:T(8,128)(2,1)S(1)}, u32[]{:S(2)}, u32[]{:S(2)}) collective-permute-start(bf16[3,128,512]{2,1,0:T(8,128)(2,1)S(1)} %get-tuple-element.129), channel_id=1, source_target_pairs={{16,0},{17,1},{18,2},{19,3},{20,4},{21,5},{22,6},{23,7},{24,8},{25... | collective-permute-start | bytes 1179656 | tf_op jit(solution)/shard_map/ppermute | solution.py:608
  48.8 1.3 %collective-permute-done.12.refs_3_.refs_17_ = bf16[256,512]{1,0:T(8,128)(2,1)S(1)} collective-permute-done((bf16[256,512]{1,0:T(8,128)(2,1)S(1)}, bf16[256,512]{1,0:T(8,128)(2,1)S(1)}, u32[]{:S(2)}, u32[]{:S(2)}) %collective-permute-start.12) | collective-permute-done | bytes 262176 | tf_op jit(solution)/shard_map/ppermute | solution.py:602
  50.6 1.7 %collective-permute-done.19.refs_4_ = bf16[256,512]{1,0:T(8,128)(2,1)S(1)} collective-permute-done((bf16[256,512]{1,0:T(8,128)(2,1)S(1)}, bf16[256,512]{1,0:T(8,128)(2,1)S(1)}, u32[]{:S(2)}, u32[]{:S(2)}) %collective-permute-start.19) | collective-permute-done | bytes 262176 | tf_op jit(solution)/shard_map/ppermute | solution.py:599
  52.3 1.3 %collective-permute-done.18.refs_5_ = bf16[256,512]{1,0:T(8,128)(2,1)S(1)} collective-permute-done((bf16[256,512]{1,0:T(8,128)(2,1)S(1)}, bf16[256,512]{1,0:T(8,128)(2,1)S(1)}, u32[]{:S(2)}, u32[]{:S(2)}) %collective-permute-start.18) | collective-permute-done | bytes 262176 | tf_op jit(solution)/shard_map/ppermute | solution.py:602
  53.6 0.5 weight_both.3
  54.1 1.6 %collective-permute-start.20 = (bf16[512,512]{1,0:T(8,128)(2,1)S(1)}, bf16[512,512]{1,0:T(8,128)(2,1)S(1)}, u32[]{:S(2)}, u32[]{:S(2)}) collective-permute-start(bf16[512,512]{1,0:T(8,128)(2,1)S(1)} %get-tuple-element.141), channel_id=1, source_target_pairs={{0,4},{1,5},{2,0},{3,1},{4,8},{5,9},{6,2},{7,3},{8,12},{9,13},{10,... | collective-permute-start | bytes 1572872 | tf_op jit(solution)/shard_map/ppermute | solution.py:599
  56.2 1.0 %local_grad.1 = (bf16[128,2688]{1,0:T(8,128)(2,1)S(1)}, bf16[128,2560]{1,0:T(8,128)(2,1)S(1)}) custom-call(bf16[8,128,512]{2,1,0:T(8,128)(2,1)S(1)} %get-tuple-element.160.refs_0_.mine, bf16[8,128,512]{2,1,0:T(8,128)(2,1)S(1)} %collective-permute-done.5.refs_1_.theirs, bf16[128,512]{1,0:T(8,128)(2,1)S(1)} %get-tuple-element.144.refs_0_.refs_2_.refs_5_.vgs, ...), custom_call_target="tpu_custom_call" | custom-call | flops 200000000 | bytes 1024 | tf_op jit(solution)/shard_map/local_grad/pallas_call | solution.py:359
  57.2 1.3 %collective-permute-start.26 = (bf16[128,2688]{1,0:T(8,128)(2,1)S(1)}, bf16[128,2688]{1,0:T(8,128)(2,1)S(1)}, u32[]{:S(2)}, u32[]{:S(2)}) collective-permute-start(bf16[128,2688]{1,0:T(8,128)(2,1)S(1)} %get-tuple-element.145), channel_id=1, source_target_pairs={{16,0},{17,1},{18,2},{19,3},{20,4},{21,5},{22,6},{23,7},{24,8},{25... | collective-permute-start | bytes 2064392 | tf_op jit(solution)/shard_map/ppermute | solution.py:608
  58.5 3.5 %back.1 = (bf16[128,4096]{1,0:T(8,128)(2,1)}, bf16[128,512]{1,0:T(8,128)(2,1)}) custom-call(f32[4,128,1024]{2,1,0:T(8,128)S(1)} %copy-done.2, bf16[4,1024,128]{2,1,0:T(8,128)(2,1)S(1)} %copy-done.4, bf16[4,128,128]{2,1,0:T(8,128)(2,1)S(1)} %copy-done.8, bf16[128,4096]{1,0:T(8,128)(2,1)S(1)} %bitcast.18, f32[128,512]{1,0:T(8,128)S(1)} %get-tuple-element.146.u_one, ...), custom_call_target="tpu_custom_call" | custom-call | flops 200000000 | bytes 1024 | tf_op jit(solution)/shard_map/back/pallas_call | solution.py:224
  62.0 1.3 %collective-permute-start.27 = (bf16[128,2560]{1,0:T(8,128)(2,1)S(1)}, bf16[128,2560]{1,0:T(8,128)(2,1)S(1)}, u32[]{:S(2)}, u32[]{:S(2)}) collective-permute-start(bf16[128,2560]{1,0:T(8,128)(2,1)S(1)} %get-tuple-element.163), channel_id=1, source_target_pairs={{16,1},{17,0},{18,3},{19,2},{20,5},{21,4},{22,7},{23,6},{24,9},{25... | collective-permute-start | bytes 1966088 | tf_op jit(solution)/shard_map/ppermute | solution.py:611
  63.3 2.7 %collective-permute-done.20.refs_4_ = bf16[512,512]{1,0:T(8,128)(2,1)S(1)} collective-permute-done((bf16[512,512]{1,0:T(8,128)(2,1)S(1)}, bf16[512,512]{1,0:T(8,128)(2,1)S(1)}, u32[]{:S(2)}, u32[]{:S(2)}) %collective-permute-start.20) | collective-permute-done | bytes 524320 | tf_op jit(solution)/shard_map/ppermute | solution.py:599
  66.3 1.6 %collective-permute-start.21 = (bf16[512,512]{1,0:T(8,128)(2,1)S(1)}, bf16[512,512]{1,0:T(8,128)(2,1)S(1)}, u32[]{:S(2)}, u32[]{:S(2)}) collective-permute-start(bf16[512,512]{1,0:T(8,128)(2,1)S(1)} %weight_step.4), channel_id=1, source_target_pairs={{0,4},{1,5},{2,0},{3,1},{4,8},{5,9},{6,2},{7,3},{8,12},{9,13},{10,... | collective-permute-start | bytes 1572872 | tf_op jit(solution)/shard_map/ppermute | solution.py:599
  68.2 0.5 collective-permute-start.25
  68.8 8.5 %collective-permute-done.21.refs_4_ = bf16[512,512]{1,0:T(8,128)(2,1)S(1)} collective-permute-done((bf16[512,512]{1,0:T(8,128)(2,1)S(1)}, bf16[512,512]{1,0:T(8,128)(2,1)S(1)}, u32[]{:S(2)}, u32[]{:S(2)}) %collective-permute-start.21) | collective-permute-done | bytes 524320 | tf_op jit(solution)/shard_map/ppermute | solution.py:599
  77.6 2.2 %collective-permute-done.25.refs_4_ = bf16[512,512]{1,0:T(8,128)(2,1)S(1)} collective-permute-done((bf16[512,512]{1,0:T(8,128)(2,1)S(1)}, bf16[512,512]{1,0:T(8,128)(2,1)S(1)}, u32[]{:S(2)}, u32[]{:S(2)}) %collective-permute-start.25) | collective-permute-done | bytes 524320 | tf_op jit(solution)/shard_map/ppermute | solution.py:602
  80.1 0.8 collective-permute-start.28
  80.8 1.3 %collective-permute-start.24 = (bf16[512,512]{1,0:T(8,128)(2,1)S(1)}, bf16[512,512]{1,0:T(8,128)(2,1)S(1)}, u32[]{:S(2)}, u32[]{:S(2)}) collective-permute-start(bf16[512,512]{1,0:T(8,128)(2,1)S(1)} %weight_step.6), channel_id=1, source_target_pairs={{0,4},{1,5},{2,0},{3,1},{4,8},{5,9},{6,2},{7,3},{8,12},{9,13},{10,... | collective-permute-start | bytes 1572872 | tf_op jit(solution)/shard_map/ppermute | solution.py:599
  82.2 1.7 %early_blocks.1.base = bf16[128,8192]{1,0:T(8,128)(2,1)} custom-call(s32[17]{0:T(128)S(1)} %pad_add_fusion.where, f32[8,128]{1,0:T(8,128)S(1)} %fence.19.pin, bf16[3,128,512]{2,1,0:T(8,128)(2,1)S(1)} %collective-permute-done.9.ones, bf16[3,128,512]{2,1,0:T(8,128)(2,1)S(1)} %collective-permute-done.14.twos, ...), custom_call_target="tpu_custom_call" | custom-call | flops 200000000 | bytes 1024 | tf_op jit(solution)/shard_map/early_blocks/pallas_call | solution.py:492
  83.9 1.7 %collective-permute-done.27.refs_0_ = bf16[128,2560]{1,0:T(8,128)(2,1)S(1)} collective-permute-done((bf16[128,2560]{1,0:T(8,128)(2,1)S(1)}, bf16[128,2560]{1,0:T(8,128)(2,1)S(1)}, u32[]{:S(2)}, u32[]{:S(2)}) %collective-permute-start.27) | collective-permute-done | bytes 655392 | tf_op jit(solution)/shard_map/ppermute | solution.py:611
  85.6 1.4 %join.1 = bf16[128,8192]{1,0:T(8,128)(2,1)} custom-call(s32[17]{0:T(128)S(1)} %pad_add_fusion.where, bf16[128,8192]{1,0:T(8,128)(2,1)} %early_blocks.1.base, bf16[128,2560]{1,0:T(8,128)(2,1)S(1)} %collective-permute-done.27.refs_0_), custom_call_target="tpu_custom_call", output_to_operand_aliasing={{}: (1, {})} | custom-call | flops 200000000 | bytes 1024 | tf_op jit(solution)/shard_map/join/pallas_call | solution.py:529
  87.0 3.0 %collective-permute-done.24.f = bf16[512,512]{1,0:T(8,128)(2,1)S(1)} collective-permute-done((bf16[512,512]{1,0:T(8,128)(2,1)S(1)}, bf16[512,512]{1,0:T(8,128)(2,1)S(1)}, u32[]{:S(2)}, u32[]{:S(2)}) %collective-permute-start.24) | collective-permute-done | bytes 524320 | tf_op jit(solution)/shard_map/ppermute | solution.py:599
  90.2 1.1 %weight_last.1 = bf16[512,512]{1,0:T(8,128)(2,1)} custom-call(bf16[8,128,512]{2,1,0:T(8,128)(2,1)S(1)} %get-tuple-element.160.refs_0_.mine, bf16[8,128,512]{2,1,0:T(8,128)(2,1)S(1)} %collective-permute-done.5.refs_1_.theirs, bf16[128,512]{1,0:T(8,128)(2,1)S(1)} %get-tuple-element.144.refs_0_.refs_2_.refs_5_.vgs, ...), custom_call_target="tpu_custom_call" | custom-call | flops 200000000 | bytes 1024 | tf_op jit(solution)/shard_map/weight_last/pallas_call | solution.py:450
  (73 shorter events, 7.1 us)
Async XLA Ops:
  0.6 15.2 %collective-permute-start.1 = (bf16[512,512]{1,0:T(8,128)(2,1)}, bf16[512,512]{1,0:T(8,128)(2,1)S(1)}, u32[]{:S(2)}, u32[]{:S(2)}) collective-permute-start(bf16[512,512]{1,0:T(8,128)(2,1)} %bitcast.19), channel_id=1, source_target_pairs={{0,4},{1,5},{2,0},{3,1},{4,8},{5,9},{6,2},{7,3},{8,12},{9,13},{10,... | collective-permute-start | bytes 1572872 | tf_op jit(solution)/shard_map/ppermute | solution.py:599
  3.7 13.6 %collective-permute-start = (bf16[512,512]{1,0:T(8,128)(2,1)}, bf16[512,512]{1,0:T(8,128)(2,1)S(1)}, u32[]{:S(2)}, u32[]{:S(2)}) collective-permute-start(bf16[512,512]{1,0:T(8,128)(2,1)} %bitcast.20), channel_id=1, source_target_pairs={{0,2},{1,3},{2,6},{3,7},{4,0},{5,1},{6,10},{7,11},{8,4},{9,5},{10,... | collective-permute-start | bytes 1572872 | tf_op jit(solution)/shard_map/ppermute | solution.py:602
  4.5 1.6 %copy-start = (bf16[1,128,8192]{2,1,0:T(8,128)(2,1)S(1)}, bf16[1,128,8192]{2,1,0:T(8,128)(2,1)}, u32[]{:S(2)}) copy-start(bf16[1,128,8192]{2,1,0:T(8,128)(2,1)} %param.8) | copy-start | bytes 6291460
  6.1 2.2 %copy-start.5 = (bf16[10,8192]{1,0:T(8,128)(2,1)S(1)}, bf16[10,8192]{1,0:T(8,128)(2,1)}, u32[]{:S(2)}) copy-start(bf16[10,8192]{1,0:T(8,128)(2,1)} %gain_t.1) | copy-start | bytes 491524
  6.8 3.9 %copy-start.9 = (s32[1,128]{1,0:T(1,128)S(1)}, s32[1,128]{1,0:T(1,128)}, u32[]{:S(2)}) copy-start(s32[1,128]{1,0:T(1,128)} %param.11) | copy-start | bytes 1540
  6.8 4.4 %copy-start.1 = (bf16[1,128,4096]{2,1,0:T(8,128)(2,1)S(1)}, bf16[1,128,4096]{2,1,0:T(8,128)(2,1)}, u32[]{:S(2)}) copy-start(bf16[1,128,4096]{2,1,0:T(8,128)(2,1)} %param.15) | copy-start | bytes 3145732
  6.8 4.4 %copy-start.6 = (bf16[1,128,4096]{2,1,0:T(8,128)(2,1)S(1)}, bf16[1,128,4096]{2,1,0:T(8,128)(2,1)}, u32[]{:S(2)}) copy-start(bf16[1,128,4096]{2,1,0:T(8,128)(2,1)} %param.12) | copy-start | bytes 3145732
  6.8 4.4 %copy-start.7 = (bf16[1,128,512]{2,1,0:T(8,128)(2,1)S(1)}, bf16[1,128,512]{2,1,0:T(8,128)(2,1)}, u32[]{:S(2)}) copy-start(bf16[1,128,512]{2,1,0:T(8,128)(2,1)} %param.13) | copy-start | bytes 393220
  6.9 13.2 %collective-permute-start.6 = (bf16[3,128,512]{2,1,0:T(8,128)(2,1)S(1)}, bf16[3,128,512]{2,1,0:T(8,128)(2,1)S(1)}, u32[]{:S(2)}, u32[]{:S(2)}) collective-permute-start(bf16[3,128,512]{2,1,0:T(8,128)(2,1)S(1)} %get-tuple-element.86), channel_id=1, source_target_pairs={{16,0},{17,1},{18,2},{19,3},{20,4},{21,5},{22,6},{23,7},{24,8},{25... | collective-permute-start | bytes 1179656 | tf_op jit(solution)/shard_map/ppermute | solution.py:608
  10.6 8.8 %collective-permute-start.5 = (bf16[8,128,512]{2,1,0:T(8,128)(2,1)S(1)}, bf16[8,128,512]{2,1,0:T(8,128)(2,1)S(1)}, u32[]{:S(2)}, u32[]{:S(2)}) collective-permute-start(bf16[8,128,512]{2,1,0:T(8,128)(2,1)S(1)} %get-tuple-element.98), channel_id=1, source_target_pairs={{0,1},{1,0},{2,3},{3,2},{4,5},{5,4},{6,7},{7,6},{8,9},{9,8},{10,11... | collective-permute-start | bytes 3145736 | tf_op jit(solution)/shard_map/ppermute | solution.py:605
  14.7 4.8 %collective-permute-start.4 = (bf16[128,512]{1,0:T(8,128)(2,1)S(1)}, bf16[128,512]{1,0:T(8,128)(2,1)S(1)}, u32[]{:S(2)}, u32[]{:S(2)}) collective-permute-start(bf16[128,512]{1,0:T(8,128)(2,1)S(1)} %get-tuple-element.144.refs_0_.refs_2_.refs_5_.vgs), channel_id=1, source_target_pairs={{0,1},{1,0},{2,3},{3,2},{4,5},{5,4},{6,7},{7,6},{8,9},{9,8},{10,11... | collective-permute-start | bytes 393224 | tf_op jit(solution)/shard_map/ppermute | solution.py:605
  15.1 4.3 %copy-start.3 = (bf16[1,512,512]{2,1,0:T(8,128)(2,1)S(1)}, bf16[1,512,512]{2,1,0:T(8,128)(2,1)}, u32[]{:S(2)}) copy-start(bf16[1,512,512]{2,1,0:T(8,128)(2,1)} %param.14) | copy-start | bytes 1572868
  17.3 9.0 %collective-permute-start.3 = (bf16[256,512]{1,0:T(8,128)(2,1)S(1)}, bf16[256,512]{1,0:T(8,128)(2,1)S(1)}, u32[]{:S(2)}, u32[]{:S(2)}) collective-permute-start(bf16[256,512]{1,0:T(8,128)(2,1)S(1)} %slice.21), channel_id=1, source_target_pairs={{0,4},{1,5},{2,0},{3,1},{4,8},{5,9},{6,2},{7,3},{8,12},{9,13},{10,... | collective-permute-start | bytes 786440 | tf_op jit(solution)/shard_map/ppermute | solution.py:599
  19.0 8.7 %collective-permute-start.2 = (bf16[256,512]{1,0:T(8,128)(2,1)S(1)}, bf16[256,512]{1,0:T(8,128)(2,1)S(1)}, u32[]{:S(2)}, u32[]{:S(2)}) collective-permute-start(bf16[256,512]{1,0:T(8,128)(2,1)S(1)} %slice.20), channel_id=1, source_target_pairs={{0,2},{1,3},{2,6},{3,7},{4,0},{5,1},{6,10},{7,11},{8,4},{9,5},{10,... | collective-permute-start | bytes 786440 | tf_op jit(solution)/shard_map/ppermute | solution.py:602
  20.1 13.9 %collective-permute-start.9 = (bf16[3,128,512]{2,1,0:T(8,128)(2,1)S(1)}, bf16[3,128,512]{2,1,0:T(8,128)(2,1)S(1)}, u32[]{:S(2)}, u32[]{:S(2)}) collective-permute-start(bf16[3,128,512]{2,1,0:T(8,128)(2,1)S(1)} %get-tuple-element.107), channel_id=1, source_target_pairs={{16,0},{17,1},{18,2},{19,3},{20,4},{21,5},{22,6},{23,7},{24,8},{25... | collective-permute-start | bytes 1179656 | tf_op jit(solution)/shard_map/ppermute | solution.py:608
  21.4 10.5 %collective-permute-start.11 = (bf16[256,512]{1,0:T(8,128)(2,1)S(1)}, bf16[256,512]{1,0:T(8,128)(2,1)S(1)}, u32[]{:S(2)}, u32[]{:S(2)}) collective-permute-start(bf16[256,512]{1,0:T(8,128)(2,1)S(1)} %slice.25), channel_id=1, source_target_pairs={{0,4},{1,5},{2,0},{3,1},{4,8},{5,9},{6,2},{7,3},{8,12},{9,13},{10,... | collective-permute-start | bytes 786440 | tf_op jit(solution)/shard_map/ppermute | solution.py:599
  23.0 10.5 %collective-permute-start.10 = (bf16[256,512]{1,0:T(8,128)(2,1)S(1)}, bf16[256,512]{1,0:T(8,128)(2,1)S(1)}, u32[]{:S(2)}, u32[]{:S(2)}) collective-permute-start(bf16[256,512]{1,0:T(8,128)(2,1)S(1)} %slice.24), channel_id=1, source_target_pairs={{0,2},{1,3},{2,6},{3,7},{4,0},{5,1},{6,10},{7,11},{8,4},{9,5},{10,... | collective-permute-start | bytes 786440 | tf_op jit(solution)/shard_map/ppermute | solution.py:602
  27.7 11.2 %collective-permute-start.7 = (bf16[256,512]{1,0:T(8,128)(2,1)S(1)}, bf16[256,512]{1,0:T(8,128)(2,1)S(1)}, u32[]{:S(2)}, u32[]{:S(2)}) collective-permute-start(bf16[256,512]{1,0:T(8,128)(2,1)S(1)} %collective-permute-done.2.refs_3_.refs_9_), channel_id=1, source_target_pairs={{0,2},{1,3},{2,6},{3,7},{4,0},{5,1},{6,10},{7,11},{8,4},{9,5},{10,... | collective-permute-start | bytes 786440 | tf_op jit(solution)/shard_map/ppermute | solution.py:602
  28.1 9.4 %collective-permute-start.8 = (bf16[256,512]{1,0:T(8,128)(2,1)S(1)}, bf16[256,512]{1,0:T(8,128)(2,1)S(1)}, u32[]{:S(2)}, u32[]{:S(2)}) collective-permute-start(bf16[256,512]{1,0:T(8,128)(2,1)S(1)} %collective-permute-done.3.refs_2_.refs_8_), channel_id=1, source_target_pairs={{0,4},{1,5},{2,0},{3,1},{4,8},{5,9},{6,2},{7,3},{8,12},{9,13},{10,... | collective-permute-start | bytes 786440 | tf_op jit(solution)/shard_map/ppermute | solution.py:599
  31.9 11.2 %collective-permute-start.16 = (bf16[256,512]{1,0:T(8,128)(2,1)S(1)}, bf16[256,512]{1,0:T(8,128)(2,1)S(1)}, u32[]{:S(2)}, u32[]{:S(2)}) collective-permute-start(bf16[256,512]{1,0:T(8,128)(2,1)S(1)} %collective-permute-done.11.refs_4_.refs_10_), channel_id=1, source_target_pairs={{0,4},{1,5},{2,0},{3,1},{4,8},{5,9},{6,2},{7,3},{8,12},{9,13},{10,... | collective-permute-start | bytes 786440 | tf_op jit(solution)/shard_map/ppermute | solution.py:599
  33.5 11.0 %collective-permute-start.15 = (bf16[256,512]{1,0:T(8,128)(2,1)S(1)}, bf16[256,512]{1,0:T(8,128)(2,1)S(1)}, u32[]{:S(2)}, u32[]{:S(2)}) collective-permute-start(bf16[256,512]{1,0:T(8,128)(2,1)S(1)} %collective-permute-done.10.refs_5_.refs_11_), channel_id=1, source_target_pairs={{0,2},{1,3},{2,6},{3,7},{4,0},{5,1},{6,10},{7,11},{8,4},{9,5},{10,... | collective-permute-start | bytes 786440 | tf_op jit(solution)/shard_map/ppermute | solution.py:602
  34.0 13.0 %collective-permute-start.14 = (bf16[3,128,512]{2,1,0:T(8,128)(2,1)S(1)}, bf16[3,128,512]{2,1,0:T(8,128)(2,1)S(1)}, u32[]{:S(2)}, u32[]{:S(2)}) collective-permute-start(bf16[3,128,512]{2,1,0:T(8,128)(2,1)S(1)} %get-tuple-element.117), channel_id=1, source_target_pairs={{16,1},{17,0},{18,3},{19,2},{20,5},{21,4},{22,7},{23,6},{24,9},{25... | collective-permute-start | bytes 1179656 | tf_op jit(solution)/shard_map/ppermute | solution.py:611
  38.9 11.2 %collective-permute-start.12 = (bf16[256,512]{1,0:T(8,128)(2,1)S(1)}, bf16[256,512]{1,0:T(8,128)(2,1)S(1)}, u32[]{:S(2)}, u32[]{:S(2)}) collective-permute-start(bf16[256,512]{1,0:T(8,128)(2,1)S(1)} %collective-permute-done.7.refs_3_.refs_13_), channel_id=1, source_target_pairs={{0,2},{1,3},{2,6},{3,7},{4,0},{5,1},{6,10},{7,11},{8,4},{9,5},{10,... | collective-permute-start | bytes 786440 | tf_op jit(solution)/shard_map/ppermute | solution.py:602
  39.3 9.4 %collective-permute-start.13 = (bf16[256,512]{1,0:T(8,128)(2,1)S(1)}, bf16[256,512]{1,0:T(8,128)(2,1)S(1)}, u32[]{:S(2)}, u32[]{:S(2)}) collective-permute-start(bf16[256,512]{1,0:T(8,128)(2,1)S(1)} %collective-permute-done.8.refs_2_.refs_12_), channel_id=1, source_target_pairs={{0,4},{1,5},{2,0},{3,1},{4,8},{5,9},{6,2},{7,3},{8,12},{9,13},{10,... | collective-permute-start | bytes 786440 | tf_op jit(solution)/shard_map/ppermute | solution.py:599
  44.8 7.5 %collective-permute-start.19 = (bf16[256,512]{1,0:T(8,128)(2,1)S(1)}, bf16[256,512]{1,0:T(8,128)(2,1)S(1)}, u32[]{:S(2)}, u32[]{:S(2)}) collective-permute-start(bf16[256,512]{1,0:T(8,128)(2,1)S(1)} %get-tuple-element.127), channel_id=1, source_target_pairs={{0,4},{1,5},{2,0},{3,1},{4,8},{5,9},{6,2},{7,3},{8,12},{9,13},{10,... | collective-permute-start | bytes 786440 | tf_op jit(solution)/shard_map/ppermute | solution.py:599
  46.5 7.2 %collective-permute-start.18 = (bf16[256,512]{1,0:T(8,128)(2,1)S(1)}, bf16[256,512]{1,0:T(8,128)(2,1)S(1)}, u32[]{:S(2)}, u32[]{:S(2)}) collective-permute-start(bf16[256,512]{1,0:T(8,128)(2,1)S(1)} %get-tuple-element.137), channel_id=1, source_target_pairs={{0,2},{1,3},{2,6},{3,7},{4,0},{5,1},{6,10},{7,11},{8,4},{9,5},{10,... | collective-permute-start | bytes 786440 | tf_op jit(solution)/shard_map/ppermute | solution.py:602
  47.0 21.8 %collective-permute-start.22 = (bf16[3,128,512]{2,1,0:T(8,128)(2,1)S(1)}, bf16[3,128,512]{2,1,0:T(8,128)(2,1)S(1)}, u32[]{:S(2)}, u32[]{:S(2)}) collective-permute-start(bf16[3,128,512]{2,1,0:T(8,128)(2,1)S(1)} %get-tuple-element.129), channel_id=1, source_target_pairs={{16,0},{17,1},{18,2},{19,3},{20,4},{21,5},{22,6},{23,7},{24,8},{25... | collective-permute-start | bytes 1179656 | tf_op jit(solution)/shard_map/ppermute | solution.py:608
  50.5 5.7 %collective-permute-start.17 = (f32[128,896]{1,0:T(8,128)S(1)}, f32[128,896]{1,0:T(8,128)S(1)}, u32[]{:S(2)}, u32[]{:S(2)}) collective-permute-start(f32[128,896]{1,0:T(8,128)S(1)} %get-tuple-element.136.refs_6_), channel_id=1, source_target_pairs={{0,1},{1,0},{2,3},{3,2},{4,5},{5,4},{6,7},{7,6},{8,9},{9,8},{10,11... | collective-permute-start | bytes 1376264 | tf_op jit(solution)/shard_map/ppermute | solution.py:605
  54.1 11.9 %collective-permute-start.20 = (bf16[512,512]{1,0:T(8,128)(2,1)S(1)}, bf16[512,512]{1,0:T(8,128)(2,1)S(1)}, u32[]{:S(2)}, u32[]{:S(2)}) collective-permute-start(bf16[512,512]{1,0:T(8,128)(2,1)S(1)} %get-tuple-element.141), channel_id=1, source_target_pairs={{0,4},{1,5},{2,0},{3,1},{4,8},{5,9},{6,2},{7,3},{8,12},{9,13},{10,... | collective-permute-start | bytes 1572872 | tf_op jit(solution)/shard_map/ppermute | solution.py:599
  55.7 12.2 %collective-permute-start.23 = (bf16[512,512]{1,0:T(8,128)(2,1)S(1)}, bf16[512,512]{1,0:T(8,128)(2,1)S(1)}, u32[]{:S(2)}, u32[]{:S(2)}) collective-permute-start(bf16[512,512]{1,0:T(8,128)(2,1)S(1)} %get-tuple-element.152), channel_id=1, source_target_pairs={{0,2},{1,3},{2,6},{3,7},{4,0},{5,1},{6,10},{7,11},{8,4},{9,5},{10,... | collective-permute-start | bytes 1572872 | tf_op jit(solution)/shard_map/ppermute | solution.py:602
  56.2 2.3 %copy-start.2 = (f32[4,128,1024]{2,1,0:T(8,128)S(1)}, f32[4,128,1024]{2,1,0:T(8,128)}, u32[]{:S(2)}) copy-start(f32[4,128,1024]{2,1,0:T(8,128)} %get-tuple-element.91.probs) | copy-start | bytes 6291460
  56.2 2.3 %copy-start.4 = (bf16[4,1024,128]{2,1,0:T(8,128)(2,1)S(1)}, bf16[4,1024,128]{2,1,0:T(8,128)(2,1)}, u32[]{:S(2)}) copy-start(bf16[4,1024,128]{2,1,0:T(8,128)(2,1)} %get-tuple-element.92.q_rot) | copy-start | bytes 3145732
  56.2 2.3 %copy-start.8 = (bf16[4,128,128]{2,1,0:T(8,128)(2,1)S(1)}, bf16[4,128,128]{2,1,0:T(8,128)(2,1)}, u32[]{:S(2)}) copy-start(bf16[4,128,128]{2,1,0:T(8,128)(2,1)} %get-tuple-element.93.k_rot) | copy-start | bytes 393220
  57.2 25.0 %collective-permute-start.26 = (bf16[128,2688]{1,0:T(8,128)(2,1)S(1)}, bf16[128,2688]{1,0:T(8,128)(2,1)S(1)}, u32[]{:S(2)}, u32[]{:S(2)}) collective-permute-start(bf16[128,2688]{1,0:T(8,128)(2,1)S(1)} %get-tuple-element.145), channel_id=1, source_target_pairs={{16,0},{17,1},{18,2},{19,3},{20,4},{21,5},{22,6},{23,7},{24,8},{25... | collective-permute-start | bytes 2064392 | tf_op jit(solution)/shard_map/ppermute | solution.py:608
  62.0 23.6 %collective-permute-start.27 = (bf16[128,2560]{1,0:T(8,128)(2,1)S(1)}, bf16[128,2560]{1,0:T(8,128)(2,1)S(1)}, u32[]{:S(2)}, u32[]{:S(2)}) collective-permute-start(bf16[128,2560]{1,0:T(8,128)(2,1)S(1)} %get-tuple-element.163), channel_id=1, source_target_pairs={{16,1},{17,0},{18,3},{19,2},{20,5},{21,4},{22,7},{23,6},{24,9},{25... | collective-permute-start | bytes 1966088 | tf_op jit(solution)/shard_map/ppermute | solution.py:611
  66.3 10.9 %collective-permute-start.21 = (bf16[512,512]{1,0:T(8,128)(2,1)S(1)}, bf16[512,512]{1,0:T(8,128)(2,1)S(1)}, u32[]{:S(2)}, u32[]{:S(2)}) collective-permute-start(bf16[512,512]{1,0:T(8,128)(2,1)S(1)} %weight_step.4), channel_id=1, source_target_pairs={{0,4},{1,5},{2,0},{3,1},{4,8},{5,9},{6,2},{7,3},{8,12},{9,13},{10,... | collective-permute-start | bytes 1572872 | tf_op jit(solution)/shard_map/ppermute | solution.py:599
  68.2 11.5 %collective-permute-start.25 = (bf16[512,512]{1,0:T(8,128)(2,1)S(1)}, bf16[512,512]{1,0:T(8,128)(2,1)S(1)}, u32[]{:S(2)}, u32[]{:S(2)}) collective-permute-start(bf16[512,512]{1,0:T(8,128)(2,1)S(1)} %weight_step.5), channel_id=1, source_target_pairs={{0,2},{1,3},{2,6},{3,7},{4,0},{5,1},{6,10},{7,11},{8,4},{9,5},{10,... | collective-permute-start | bytes 1572872 | tf_op jit(solution)/shard_map/ppermute | solution.py:602
  80.1 10.1 %collective-permute-start.28 = (bf16[512,512]{1,0:T(8,128)(2,1)S(1)}, bf16[512,512]{1,0:T(8,128)(2,1)S(1)}, u32[]{:S(2)}, u32[]{:S(2)}) collective-permute-start(bf16[512,512]{1,0:T(8,128)(2,1)S(1)} %weight_step.7), channel_id=1, source_target_pairs={{0,2},{1,3},{2,6},{3,7},{4,0},{5,1},{6,10},{7,11},{8,4},{9,5},{10,... | collective-permute-start | bytes 1572872 | tf_op jit(solution)/shard_map/ppermute | solution.py:602
  80.8 9.2 %collective-permute-start.24 = (bf16[512,512]{1,0:T(8,128)(2,1)S(1)}, bf16[512,512]{1,0:T(8,128)(2,1)S(1)}, u32[]{:S(2)}, u32[]{:S(2)}) collective-permute-start(bf16[512,512]{1,0:T(8,128)(2,1)S(1)} %weight_step.6), channel_id=1, source_target_pairs={{0,4},{1,5},{2,0},{3,1},{4,8},{5,9},{6,2},{7,3},{8,12},{9,13},{10,... | collective-permute-start | bytes 1572872 | tf_op jit(solution)/shard_map/ppermute | solution.py:599

commit v6 on v5

--- a/solution.py
+++ b/solution.py
@@ -23,7 +23,7 @@
 
 
 SMALL = cost(0.2)
-H = [12.0, 9.0, 1.5, 1.5, 1.5, 6.0, 3.0, 6.0]
+H = [5.0, 5.0, 1.5, 9.0, 0.3, 6.0, 6.0, 6.0]
 
 
 def params(**more):

time: 92.7 us -> 92.7 us (level)
  no operation moved by 1% of the time
where the time goes in v6:
time: 92.7 us; the launch traced here: 91.2 us
  waiting for transfers between devices  37.4 us (40%)
  starting transfers between devices  30.2 us (33%)
  Pallas kernels  19.7 us (21%)
  local copies, waits for them, and re-layouts  1.72 us (2%)
  between operations  1.71 us (2%)
    ppermute x10, waiting for transfers between devices, ahead(): return lax.ppermute(x, 'dp', forth)  25.2 us
    ppermute x10, starting transfers between devices, ahead(): return lax.ppermute(x, 'dp', forth)  17.2 us
    ppermute x10, waiting for transfers between devices, behind(): return lax.ppermute(x, 'dp', back)  10.4 us
    ppermute x4, starting transfers between devices, sent_down(): return lax.ppermute(x, ('section', 'dp'), down)  5.29 us
    ppermute x10, starting transfers between devices, behind(): return lax.ppermute(x, 'dp', back)  4.44 us
    pallas_call x1, Pallas kernels, attention_back(): pl.pallas_call(back_kernel, grid=(HK,), in_specs=[pl.BlockSpec((1, tokens...  3.49 us
    pallas_call x1, Pallas kernels, attention_probs(): pl.pallas_call(probs_kernel, grid=(HK,), in_specs=[group, head, group, ta...  3.43 us
    ppermute x2, starting transfers between devices, sent_across(): return lax.ppermute(x, ('section', 'dp'), cross)  2.56 us
  transfers between devices with their start and end apart: 29, of which 19 were waited for; matrix products, arithmetic and copies ran while one was open for 1% of the time, Pallas kernels for 20%

profile of v6, /device:TPU:0, one launch (start us, length us, event | category | flops | bytes accessed | tf_op | source)
XLA Modules:
  0.0 91.2 jit_solution(660421077243037327)
XLA Ops:
  0.6 3.1 %collective-permute-start.1 = (bf16[512,512]{1,0:T(8,128)(2,1)}, bf16[512,512]{1,0:T(8,128)(2,1)S(1)}, u32[]{:S(2)}, u32[]{:S(2)}) collective-permute-start(bf16[512,512]{1,0:T(8,128)(2,1)} %bitcast.19), channel_id=1, source_target_pairs={{0,4},{1,5},{2,0},{3,1},{4,8},{5,9},{6,2},{7,3},{8,12},{9,13},{10,... | collective-permute-start | bytes 1572872 | tf_op jit(solution)/shard_map/ppermute | solution.py:599
  4.5 1.6 %copy-done = bf16[1,128,8192]{2,1,0:T(8,128)(2,1)S(1)} copy-done((bf16[1,128,8192]{2,1,0:T(8,128)(2,1)S(1)}, bf16[1,128,8192]{2,1,0:T(8,128)(2,1)}, u32[]{:S(2)}) %copy-start) | copy-done | bytes 2097176
  6.1 0.7 pick.1
  6.9 1.4 %collective-permute-start.6 = (bf16[3,128,512]{2,1,0:T(8,128)(2,1)S(1)}, bf16[3,128,512]{2,1,0:T(8,128)(2,1)S(1)}, u32[]{:S(2)}, u32[]{:S(2)}) collective-permute-start(bf16[3,128,512]{2,1,0:T(8,128)(2,1)S(1)} %get-tuple-element.86), channel_id=1, source_target_pairs={{16,0},{17,1},{18,2},{19,3},{20,4},{21,5},{22,6},{23,7},{24,8},{25... | collective-permute-start | bytes 1179656 | tf_op jit(solution)/shard_map/ppermute | solution.py:608
  8.3 2.3 %prep.1 = (bf16[8,128,512]{2,1,0:T(8,128)(2,1)S(1)}, bf16[8,128,512]{2,1,0:T(8,128)(2,1)S(1)}, f32[8,1,512]{2,1,0:T(1,128)S(1)}, f32[128,128]{1,0:T(8,128)S(1)}) custom-call(s32[17]{0:T(128)S(1)} %pad_add_fusion.where, bf16[128,8192]{1,0:T(8,128)(2,1)S(1)} %bitcast.15, bf16[128,8192]{1,0:T(8,128)(2,1)S(1)} %bitcast.16, bf16[10,8192]{1,0:T(8,128)(2,1)S(1)} %copy-done.5, ...), custom_call_target="tpu_custom_call" | custom-call | flops 200000000 | bytes 1024 | tf_op jit(solution)/shard_map/prep/pallas_call | solution.py:89
  11.2 3.4 %probs.1 = (f32[4,128,1024]{2,1,0:T(8,128)}, bf16[4,1024,128]{2,1,0:T(8,128)(2,1)}, bf16[4,128,128]{2,1,0:T(8,128)(2,1)}, bf16[128,512]{1,0:T(8,128)(2,1)S(1)}) custom-call(bf16[128,4096]{1,0:T(8,128)(2,1)S(1)} %bitcast.23, bf16[128,512]{1,0:T(8,128)(2,1)S(1)} %bitcast.24, bf16[128,4096]{1,0:T(8,128)(2,1)S(1)} %bitcast.17, ...), custom_call_target="tpu_custom_call" | custom-call | flops 200000000 | bytes 1024 | tf_op jit(solution)/shard_map/probs/pallas_call | solution.py:182
  14.6 0.5 collective-permute-start.4
  15.2 0.6 collective-permute-done.1.refs_5_.refs_3_
  15.8 1.5 %collective-permute-done.refs_4_ = bf16[512,512]{1,0:T(8,128)(2,1)S(1)} collective-permute-done((bf16[512,512]{1,0:T(8,128)(2,1)}, bf16[512,512]{1,0:T(8,128)(2,1)S(1)}, u32[]{:S(2)}, u32[]{:S(2)}) %collective-permute-start) | collective-permute-done | bytes 524320 | tf_op jit(solution)/shard_map/ppermute | solution.py:602
  17.3 1.6 %collective-permute-start.3 = (bf16[256,512]{1,0:T(8,128)(2,1)S(1)}, bf16[256,512]{1,0:T(8,128)(2,1)S(1)}, u32[]{:S(2)}, u32[]{:S(2)}) collective-permute-start(bf16[256,512]{1,0:T(8,128)(2,1)S(1)} %slice.21), channel_id=1, source_target_pairs={{0,4},{1,5},{2,0},{3,1},{4,8},{5,9},{6,2},{7,3},{8,12},{9,13},{10,... | collective-permute-start | bytes 786440 | tf_op jit(solution)/shard_map/ppermute | solution.py:599
  19.4 0.6 first_terms.1
  20.1 1.3 %collective-permute-start.9 = (bf16[3,128,512]{2,1,0:T(8,128)(2,1)S(1)}, bf16[3,128,512]{2,1,0:T(8,128)(2,1)S(1)}, u32[]{:S(2)}, u32[]{:S(2)}) collective-permute-start(bf16[3,128,512]{2,1,0:T(8,128)(2,1)S(1)} %get-tuple-element.107), channel_id=1, source_target_pairs={{16,0},{17,1},{18,2},{19,3},{20,4},{21,5},{22,6},{23,7},{24,8},{25... | collective-permute-start | bytes 1179656 | tf_op jit(solution)/shard_map/ppermute | solution.py:608
  21.4 1.6 %collective-permute-start.11 = (bf16[256,512]{1,0:T(8,128)(2,1)S(1)}, bf16[256,512]{1,0:T(8,128)(2,1)S(1)}, u32[]{:S(2)}, u32[]{:S(2)}) collective-permute-start(bf16[256,512]{1,0:T(8,128)(2,1)S(1)} %slice.25), channel_id=1, source_target_pairs={{0,4},{1,5},{2,0},{3,1},{4,8},{5,9},{6,2},{7,3},{8,12},{9,13},{10,... | collective-permute-start | bytes 786440 | tf_op jit(solution)/shard_map/ppermute | solution.py:599
  23.5 0.6 values.4.refs_6_
  24.1 2.3 %collective-permute-done.3.refs_2_.refs_8_ = bf16[256,512]{1,0:T(8,128)(2,1)S(1)} collective-permute-done((bf16[256,512]{1,0:T(8,128)(2,1)S(1)}, bf16[256,512]{1,0:T(8,128)(2,1)S(1)}, u32[]{:S(2)}, u32[]{:S(2)}) %collective-permute-start.3) | collective-permute-done | bytes 262176 | tf_op jit(solution)/shard_map/ppermute | solution.py:599
  26.3 1.3 %collective-permute-done.2.refs_3_.refs_9_ = bf16[256,512]{1,0:T(8,128)(2,1)S(1)} collective-permute-done((bf16[256,512]{1,0:T(8,128)(2,1)S(1)}, bf16[256,512]{1,0:T(8,128)(2,1)S(1)}, u32[]{:S(2)}, u32[]{:S(2)}) %collective-permute-start.2) | collective-permute-done | bytes 262176 | tf_op jit(solution)/shard_map/ppermute | solution.py:602
  28.1 1.6 %collective-permute-start.8 = (bf16[256,512]{1,0:T(8,128)(2,1)S(1)}, bf16[256,512]{1,0:T(8,128)(2,1)S(1)}, u32[]{:S(2)}, u32[]{:S(2)}) collective-permute-start(bf16[256,512]{1,0:T(8,128)(2,1)S(1)} %collective-permute-done.3.refs_2_.refs_8_), channel_id=1, source_target_pairs={{0,4},{1,5},{2,0},{3,1},{4,8},{5,9},{6,2},{7,3},{8,12},{9,13},{10,... | collective-permute-start | bytes 786440 | tf_op jit(solution)/shard_map/ppermute | solution.py:599
  29.7 2.3 %collective-permute-done.11.refs_4_.refs_10_ = bf16[256,512]{1,0:T(8,128)(2,1)S(1)} collective-permute-done((bf16[256,512]{1,0:T(8,128)(2,1)S(1)}, bf16[256,512]{1,0:T(8,128)(2,1)S(1)}, u32[]{:S(2)}, u32[]{:S(2)}) %collective-permute-start.11) | collective-permute-done | bytes 262176 | tf_op jit(solution)/shard_map/ppermute | solution.py:599
  31.9 1.6 %collective-permute-start.16 = (bf16[256,512]{1,0:T(8,128)(2,1)S(1)}, bf16[256,512]{1,0:T(8,128)(2,1)S(1)}, u32[]{:S(2)}, u32[]{:S(2)}) collective-permute-start(bf16[256,512]{1,0:T(8,128)(2,1)S(1)} %collective-permute-done.11.refs_4_.refs_10_), channel_id=1, source_target_pairs={{0,4},{1,5},{2,0},{3,1},{4,8},{5,9},{6,2},{7,3},{8,12},{9,13},{10,... | collective-permute-start | bytes 786440 | tf_op jit(solution)/shard_map/ppermute | solution.py:599
  34.0 1.3 %collective-permute-start.14 = (bf16[3,128,512]{2,1,0:T(8,128)(2,1)S(1)}, bf16[3,128,512]{2,1,0:T(8,128)(2,1)S(1)}, u32[]{:S(2)}, u32[]{:S(2)}) collective-permute-start(bf16[3,128,512]{2,1,0:T(8,128)(2,1)S(1)} %get-tuple-element.117), channel_id=1, source_target_pairs={{16,1},{17,0},{18,3},{19,2},{20,5},{21,4},{22,7},{23,6},{24,9},{25... | collective-permute-start | bytes 1179656 | tf_op jit(solution)/shard_map/ppermute | solution.py:611
  35.7 1.8 %collective-permute-done.8.refs_2_.refs_12_ = bf16[256,512]{1,0:T(8,128)(2,1)S(1)} collective-permute-done((bf16[256,512]{1,0:T(8,128)(2,1)S(1)}, bf16[256,512]{1,0:T(8,128)(2,1)S(1)}, u32[]{:S(2)}, u32[]{:S(2)}) %collective-permute-start.8) | collective-permute-done | bytes 262176 | tf_op jit(solution)/shard_map/ppermute | solution.py:599
  37.6 1.3 %collective-permute-done.7.refs_3_.refs_13_ = bf16[256,512]{1,0:T(8,128)(2,1)S(1)} collective-permute-done((bf16[256,512]{1,0:T(8,128)(2,1)S(1)}, bf16[256,512]{1,0:T(8,128)(2,1)S(1)}, u32[]{:S(2)}, u32[]{:S(2)}) %collective-permute-start.7) | collective-permute-done | bytes 262176 | tf_op jit(solution)/shard_map/ppermute | solution.py:602
  39.3 1.6 %collective-permute-start.13 = (bf16[256,512]{1,0:T(8,128)(2,1)S(1)}, bf16[256,512]{1,0:T(8,128)(2,1)S(1)}, u32[]{:S(2)}, u32[]{:S(2)}) collective-permute-start(bf16[256,512]{1,0:T(8,128)(2,1)S(1)} %collective-permute-done.8.refs_2_.refs_12_), channel_id=1, source_target_pairs={{0,4},{1,5},{2,0},{3,1},{4,8},{5,9},{6,2},{7,3},{8,12},{9,13},{10,... | collective-permute-start | bytes 786440 | tf_op jit(solution)/shard_map/ppermute | solution.py:599
  40.9 2.3 %collective-permute-done.16.refs_4_.refs_14_ = bf16[256,512]{1,0:T(8,128)(2,1)S(1)} collective-permute-done((bf16[256,512]{1,0:T(8,128)(2,1)S(1)}, bf16[256,512]{1,0:T(8,128)(2,1)S(1)}, u32[]{:S(2)}, u32[]{:S(2)}) %collective-permute-start.16) | collective-permute-done | bytes 262176 | tf_op jit(solution)/shard_map/ppermute | solution.py:599
  43.2 1.3 %collective-permute-done.15.refs_5_.refs_15_ = bf16[256,512]{1,0:T(8,128)(2,1)S(1)} collective-permute-done((bf16[256,512]{1,0:T(8,128)(2,1)S(1)}, bf16[256,512]{1,0:T(8,128)(2,1)S(1)}, u32[]{:S(2)}, u32[]{:S(2)}) %collective-permute-start.15) | collective-permute-done | bytes 262176 | tf_op jit(solution)/shard_map/ppermute | solution.py:602
  44.8 1.6 %collective-permute-start.19 = (bf16[256,512]{1,0:T(8,128)(2,1)S(1)}, bf16[256,512]{1,0:T(8,128)(2,1)S(1)}, u32[]{:S(2)}, u32[]{:S(2)}) collective-permute-start(bf16[256,512]{1,0:T(8,128)(2,1)S(1)} %get-tuple-element.127), channel_id=1, source_target_pairs={{0,4},{1,5},{2,0},{3,1},{4,8},{5,9},{6,2},{7,3},{8,12},{9,13},{10,... | collective-permute-start | bytes 786440 | tf_op jit(solution)/shard_map/ppermute | solution.py:599
  47.0 1.3 %collective-permute-start.22 = (bf16[3,128,512]{2,1,0:T(8,128)(2,1)S(1)}, bf16[3,128,512]{2,1,0:T(8,128)(2,1)S(1)}, u32[]{:S(2)}, u32[]{:S(2)}) collective-permute-start(bf16[3,128,512]{2,1,0:T(8,128)(2,1)S(1)} %get-tuple-element.129), channel_id=1, source_target_pairs={{16,0},{17,1},{18,2},{19,3},{20,4},{21,5},{22,6},{23,7},{24,8},{25... | collective-permute-start | bytes 1179656 | tf_op jit(solution)/shard_map/ppermute | solution.py:608
  48.8 1.3 %collective-permute-done.12.refs_3_.refs_17_ = bf16[256,512]{1,0:T(8,128)(2,1)S(1)} collective-permute-done((bf16[256,512]{1,0:T(8,128)(2,1)S(1)}, bf16[256,512]{1,0:T(8,128)(2,1)S(1)}, u32[]{:S(2)}, u32[]{:S(2)}) %collective-permute-start.12) | collective-permute-done | bytes 262176 | tf_op jit(solution)/shard_map/ppermute | solution.py:602
  50.6 1.7 %collective-permute-done.19.refs_4_ = bf16[256,512]{1,0:T(8,128)(2,1)S(1)} collective-permute-done((bf16[256,512]{1,0:T(8,128)(2,1)S(1)}, bf16[256,512]{1,0:T(8,128)(2,1)S(1)}, u32[]{:S(2)}, u32[]{:S(2)}) %collective-permute-start.19) | collective-permute-done | bytes 262176 | tf_op jit(solution)/shard_map/ppermute | solution.py:599
  52.3 1.3 %collective-permute-done.18.refs_5_ = bf16[256,512]{1,0:T(8,128)(2,1)S(1)} collective-permute-done((bf16[256,512]{1,0:T(8,128)(2,1)S(1)}, bf16[256,512]{1,0:T(8,128)(2,1)S(1)}, u32[]{:S(2)}, u32[]{:S(2)}) %collective-permute-start.18) | collective-permute-done | bytes 262176 | tf_op jit(solution)/shard_map/ppermute | solution.py:602
  53.6 0.5 weight_both.3
  54.1 1.6 %collective-permute-start.20 = (bf16[512,512]{1,0:T(8,128)(2,1)S(1)}, bf16[512,512]{1,0:T(8,128)(2,1)S(1)}, u32[]{:S(2)}, u32[]{:S(2)}) collective-permute-start(bf16[512,512]{1,0:T(8,128)(2,1)S(1)} %get-tuple-element.141), channel_id=1, source_target_pairs={{0,4},{1,5},{2,0},{3,1},{4,8},{5,9},{6,2},{7,3},{8,12},{9,13},{10,... | collective-permute-start | bytes 1572872 | tf_op jit(solution)/shard_map/ppermute | solution.py:599
  56.2 1.0 %local_grad.1 = (bf16[128,2688]{1,0:T(8,128)(2,1)S(1)}, bf16[128,2560]{1,0:T(8,128)(2,1)S(1)}) custom-call(bf16[8,128,512]{2,1,0:T(8,128)(2,1)S(1)} %get-tuple-element.160.refs_0_.mine, bf16[8,128,512]{2,1,0:T(8,128)(2,1)S(1)} %collective-permute-done.5.refs_1_.theirs, bf16[128,512]{1,0:T(8,128)(2,1)S(1)} %get-tuple-element.144.refs_0_.refs_2_.refs_5_.vgs, ...), custom_call_target="tpu_custom_call" | custom-call | flops 200000000 | bytes 1024 | tf_op jit(solution)/shard_map/local_grad/pallas_call | solution.py:359
  57.2 1.3 %collective-permute-start.26 = (bf16[128,2688]{1,0:T(8,128)(2,1)S(1)}, bf16[128,2688]{1,0:T(8,128)(2,1)S(1)}, u32[]{:S(2)}, u32[]{:S(2)}) collective-permute-start(bf16[128,2688]{1,0:T(8,128)(2,1)S(1)} %get-tuple-element.145), channel_id=1, source_target_pairs={{16,0},{17,1},{18,2},{19,3},{20,4},{21,5},{22,6},{23,7},{24,8},{25... | collective-permute-start | bytes 2064392 | tf_op jit(solution)/shard_map/ppermute | solution.py:608
  58.5 3.5 %back.1 = (bf16[128,4096]{1,0:T(8,128)(2,1)}, bf16[128,512]{1,0:T(8,128)(2,1)}) custom-call(f32[4,128,1024]{2,1,0:T(8,128)S(1)} %copy-done.2, bf16[4,1024,128]{2,1,0:T(8,128)(2,1)S(1)} %copy-done.4, bf16[4,128,128]{2,1,0:T(8,128)(2,1)S(1)} %copy-done.8, bf16[128,4096]{1,0:T(8,128)(2,1)S(1)} %bitcast.18, f32[128,512]{1,0:T(8,128)S(1)} %get-tuple-element.146.u_one, ...), custom_call_target="tpu_custom_call" | custom-call | flops 200000000 | bytes 1024 | tf_op jit(solution)/shard_map/back/pallas_call | solution.py:224
  62.0 1.3 %collective-permute-start.27 = (bf16[128,2560]{1,0:T(8,128)(2,1)S(1)}, bf16[128,2560]{1,0:T(8,128)(2,1)S(1)}, u32[]{:S(2)}, u32[]{:S(2)}) collective-permute-start(bf16[128,2560]{1,0:T(8,128)(2,1)S(1)} %get-tuple-element.163), channel_id=1, source_target_pairs={{16,1},{17,0},{18,3},{19,2},{20,5},{21,4},{22,7},{23,6},{24,9},{25... | collective-permute-start | bytes 1966088 | tf_op jit(solution)/shard_map/ppermute | solution.py:611
  63.3 2.7 %collective-permute-done.20.refs_4_ = bf16[512,512]{1,0:T(8,128)(2,1)S(1)} collective-permute-done((bf16[512,512]{1,0:T(8,128)(2,1)S(1)}, bf16[512,512]{1,0:T(8,128)(2,1)S(1)}, u32[]{:S(2)}, u32[]{:S(2)}) %collective-permute-start.20) | collective-permute-done | bytes 524320 | tf_op jit(solution)/shard_map/ppermute | solution.py:599
  66.3 1.6 %collective-permute-start.21 = (bf16[512,512]{1,0:T(8,128)(2,1)S(1)}, bf16[512,512]{1,0:T(8,128)(2,1)S(1)}, u32[]{:S(2)}, u32[]{:S(2)}) collective-permute-start(bf16[512,512]{1,0:T(8,128)(2,1)S(1)} %weight_step.4), channel_id=1, source_target_pairs={{0,4},{1,5},{2,0},{3,1},{4,8},{5,9},{6,2},{7,3},{8,12},{9,13},{10,... | collective-permute-start | bytes 1572872 | tf_op jit(solution)/shard_map/ppermute | solution.py:599
  68.2 0.5 collective-permute-start.25
  68.8 8.5 %collective-permute-done.21.refs_4_ = bf16[512,512]{1,0:T(8,128)(2,1)S(1)} collective-permute-done((bf16[512,512]{1,0:T(8,128)(2,1)S(1)}, bf16[512,512]{1,0:T(8,128)(2,1)S(1)}, u32[]{:S(2)}, u32[]{:S(2)}) %collective-permute-start.21) | collective-permute-done | bytes 524320 | tf_op jit(solution)/shard_map/ppermute | solution.py:599
  77.6 2.2 %collective-permute-done.25.refs_4_ = bf16[512,512]{1,0:T(8,128)(2,1)S(1)} collective-permute-done((bf16[512,512]{1,0:T(8,128)(2,1)S(1)}, bf16[512,512]{1,0:T(8,128)(2,1)S(1)}, u32[]{:S(2)}, u32[]{:S(2)}) %collective-permute-start.25) | collective-permute-done | bytes 524320 | tf_op jit(solution)/shard_map/ppermute | solution.py:602
  80.1 0.8 collective-permute-start.28
  80.8 1.3 %collective-permute-start.24 = (bf16[512,512]{1,0:T(8,128)(2,1)S(1)}, bf16[512,512]{1,0:T(8,128)(2,1)S(1)}, u32[]{:S(2)}, u32[]{:S(2)}) collective-permute-start(bf16[512,512]{1,0:T(8,128)(2,1)S(1)} %weight_step.6), channel_id=1, source_target_pairs={{0,4},{1,5},{2,0},{3,1},{4,8},{5,9},{6,2},{7,3},{8,12},{9,13},{10,... | collective-permute-start | bytes 1572872 | tf_op jit(solution)/shard_map/ppermute | solution.py:599
  82.1 1.7 %early_blocks.1.base = bf16[128,8192]{1,0:T(8,128)(2,1)} custom-call(s32[17]{0:T(128)S(1)} %pad_add_fusion.where, f32[8,128]{1,0:T(8,128)S(1)} %fence.19.pin, bf16[3,128,512]{2,1,0:T(8,128)(2,1)S(1)} %collective-permute-done.9.ones, bf16[3,128,512]{2,1,0:T(8,128)(2,1)S(1)} %collective-permute-done.14.twos, ...), custom_call_target="tpu_custom_call" | custom-call | flops 200000000 | bytes 1024 | tf_op jit(solution)/shard_map/early_blocks/pallas_call | solution.py:492
  83.9 1.7 %collective-permute-done.27.refs_0_ = bf16[128,2560]{1,0:T(8,128)(2,1)S(1)} collective-permute-done((bf16[128,2560]{1,0:T(8,128)(2,1)S(1)}, bf16[128,2560]{1,0:T(8,128)(2,1)S(1)}, u32[]{:S(2)}, u32[]{:S(2)}) %collective-permute-start.27) | collective-permute-done | bytes 655392 | tf_op jit(solution)/shard_map/ppermute | solution.py:611
  85.6 1.4 %join.1 = bf16[128,8192]{1,0:T(8,128)(2,1)} custom-call(s32[17]{0:T(128)S(1)} %pad_add_fusion.where, bf16[128,8192]{1,0:T(8,128)(2,1)} %early_blocks.1.base, bf16[128,2560]{1,0:T(8,128)(2,1)S(1)} %collective-permute-done.27.refs_0_), custom_call_target="tpu_custom_call", output_to_operand_aliasing={{}: (1, {})} | custom-call | flops 200000000 | bytes 1024 | tf_op jit(solution)/shard_map/join/pallas_call | solution.py:529
  87.0 3.0 %collective-permute-done.24.f = bf16[512,512]{1,0:T(8,128)(2,1)S(1)} collective-permute-done((bf16[512,512]{1,0:T(8,128)(2,1)S(1)}, bf16[512,512]{1,0:T(8,128)(2,1)S(1)}, u32[]{:S(2)}, u32[]{:S(2)}) %collective-permute-start.24) | collective-permute-done | bytes 524320 | tf_op jit(solution)/shard_map/ppermute | solution.py:599
  90.2 1.1 %weight_last.1 = bf16[512,512]{1,0:T(8,128)(2,1)} custom-call(bf16[8,128,512]{2,1,0:T(8,128)(2,1)S(1)} %get-tuple-element.160.refs_0_.mine, bf16[8,128,512]{2,1,0:T(8,128)(2,1)S(1)} %collective-permute-done.5.refs_1_.theirs, bf16[128,512]{1,0:T(8,128)(2,1)S(1)} %get-tuple-element.144.refs_0_.refs_2_.refs_5_.vgs, ...), custom_call_target="tpu_custom_call" | custom-call | flops 200000000 | bytes 1024 | tf_op jit(solution)/shard_map/weight_last/pallas_call | solution.py:450
  (73 shorter events, 7.1 us)
Async XLA Ops:
  0.6 15.2 %collective-permute-start.1 = (bf16[512,512]{1,0:T(8,128)(2,1)}, bf16[512,512]{1,0:T(8,128)(2,1)S(1)}, u32[]{:S(2)}, u32[]{:S(2)}) collective-permute-start(bf16[512,512]{1,0:T(8,128)(2,1)} %bitcast.19), channel_id=1, source_target_pairs={{0,4},{1,5},{2,0},{3,1},{4,8},{5,9},{6,2},{7,3},{8,12},{9,13},{10,... | collective-permute-start | bytes 1572872 | tf_op jit(solution)/shard_map/ppermute | solution.py:599
  3.7 13.6 %collective-permute-start = (bf16[512,512]{1,0:T(8,128)(2,1)}, bf16[512,512]{1,0:T(8,128)(2,1)S(1)}, u32[]{:S(2)}, u32[]{:S(2)}) collective-permute-start(bf16[512,512]{1,0:T(8,128)(2,1)} %bitcast.20), channel_id=1, source_target_pairs={{0,2},{1,3},{2,6},{3,7},{4,0},{5,1},{6,10},{7,11},{8,4},{9,5},{10,... | collective-permute-start | bytes 1572872 | tf_op jit(solution)/shard_map/ppermute | solution.py:602
  4.5 1.6 %copy-start = (bf16[1,128,8192]{2,1,0:T(8,128)(2,1)S(1)}, bf16[1,128,8192]{2,1,0:T(8,128)(2,1)}, u32[]{:S(2)}) copy-start(bf16[1,128,8192]{2,1,0:T(8,128)(2,1)} %param.8) | copy-start | bytes 6291460
  6.1 2.2 %copy-start.5 = (bf16[10,8192]{1,0:T(8,128)(2,1)S(1)}, bf16[10,8192]{1,0:T(8,128)(2,1)}, u32[]{:S(2)}) copy-start(bf16[10,8192]{1,0:T(8,128)(2,1)} %gain_t.1) | copy-start | bytes 491524
  6.8 3.9 %copy-start.9 = (s32[1,128]{1,0:T(1,128)S(1)}, s32[1,128]{1,0:T(1,128)}, u32[]{:S(2)}) copy-start(s32[1,128]{1,0:T(1,128)} %param.11) | copy-start | bytes 1540
  6.8 4.4 %copy-start.1 = (bf16[1,128,4096]{2,1,0:T(8,128)(2,1)S(1)}, bf16[1,128,4096]{2,1,0:T(8,128)(2,1)}, u32[]{:S(2)}) copy-start(bf16[1,128,4096]{2,1,0:T(8,128)(2,1)} %param.15) | copy-start | bytes 3145732
  6.8 4.4 %copy-start.6 = (bf16[1,128,4096]{2,1,0:T(8,128)(2,1)S(1)}, bf16[1,128,4096]{2,1,0:T(8,128)(2,1)}, u32[]{:S(2)}) copy-start(bf16[1,128,4096]{2,1,0:T(8,128)(2,1)} %param.12) | copy-start | bytes 3145732
  6.8 4.4 %copy-start.7 = (bf16[1,128,512]{2,1,0:T(8,128)(2,1)S(1)}, bf16[1,128,512]{2,1,0:T(8,128)(2,1)}, u32[]{:S(2)}) copy-start(bf16[1,128,512]{2,1,0:T(8,128)(2,1)} %param.13) | copy-start | bytes 393220
  6.9 13.2 %collective-permute-start.6 = (bf16[3,128,512]{2,1,0:T(8,128)(2,1)S(1)}, bf16[3,128,512]{2,1,0:T(8,128)(2,1)S(1)}, u32[]{:S(2)}, u32[]{:S(2)}) collective-permute-start(bf16[3,128,512]{2,1,0:T(8,128)(2,1)S(1)} %get-tuple-element.86), channel_id=1, source_target_pairs={{16,0},{17,1},{18,2},{19,3},{20,4},{21,5},{22,6},{23,7},{24,8},{25... | collective-permute-start | bytes 1179656 | tf_op jit(solution)/shard_map/ppermute | solution.py:608
  10.6 8.8 %collective-permute-start.5 = (bf16[8,128,512]{2,1,0:T(8,128)(2,1)S(1)}, bf16[8,128,512]{2,1,0:T(8,128)(2,1)S(1)}, u32[]{:S(2)}, u32[]{:S(2)}) collective-permute-start(bf16[8,128,512]{2,1,0:T(8,128)(2,1)S(1)} %get-tuple-element.98), channel_id=1, source_target_pairs={{0,1},{1,0},{2,3},{3,2},{4,5},{5,4},{6,7},{7,6},{8,9},{9,8},{10,11... | collective-permute-start | bytes 3145736 | tf_op jit(solution)/shard_map/ppermute | solution.py:605
  14.6 4.8 %collective-permute-start.4 = (bf16[128,512]{1,0:T(8,128)(2,1)S(1)}, bf16[128,512]{1,0:T(8,128)(2,1)S(1)}, u32[]{:S(2)}, u32[]{:S(2)}) collective-permute-start(bf16[128,512]{1,0:T(8,128)(2,1)S(1)} %get-tuple-element.144.refs_0_.refs_2_.refs_5_.vgs), channel_id=1, source_target_pairs={{0,1},{1,0},{2,3},{3,2},{4,5},{5,4},{6,7},{7,6},{8,9},{9,8},{10,11... | collective-permute-start | bytes 393224 | tf_op jit(solution)/shard_map/ppermute | solution.py:605
  15.1 4.3 %copy-start.3 = (bf16[1,512,512]{2,1,0:T(8,128)(2,1)S(1)}, bf16[1,512,512]{2,1,0:T(8,128)(2,1)}, u32[]{:S(2)}) copy-start(bf16[1,512,512]{2,1,0:T(8,128)(2,1)} %param.14) | copy-start | bytes 1572868
  17.3 9.0 %collective-permute-start.3 = (bf16[256,512]{1,0:T(8,128)(2,1)S(1)}, bf16[256,512]{1,0:T(8,128)(2,1)S(1)}, u32[]{:S(2)}, u32[]{:S(2)}) collective-permute-start(bf16[256,512]{1,0:T(8,128)(2,1)S(1)} %slice.21), channel_id=1, source_target_pairs={{0,4},{1,5},{2,0},{3,1},{4,8},{5,9},{6,2},{7,3},{8,12},{9,13},{10,... | collective-permute-start | bytes 786440 | tf_op jit(solution)/shard_map/ppermute | solution.py:599
  19.0 8.7 %collective-permute-start.2 = (bf16[256,512]{1,0:T(8,128)(2,1)S(1)}, bf16[256,512]{1,0:T(8,128)(2,1)S(1)}, u32[]{:S(2)}, u32[]{:S(2)}) collective-permute-start(bf16[256,512]{1,0:T(8,128)(2,1)S(1)} %slice.20), channel_id=1, source_target_pairs={{0,2},{1,3},{2,6},{3,7},{4,0},{5,1},{6,10},{7,11},{8,4},{9,5},{10,... | collective-permute-start | bytes 786440 | tf_op jit(solution)/shard_map/ppermute | solution.py:602
  20.1 13.9 %collective-permute-start.9 = (bf16[3,128,512]{2,1,0:T(8,128)(2,1)S(1)}, bf16[3,128,512]{2,1,0:T(8,128)(2,1)S(1)}, u32[]{:S(2)}, u32[]{:S(2)}) collective-permute-start(bf16[3,128,512]{2,1,0:T(8,128)(2,1)S(1)} %get-tuple-element.107), channel_id=1, source_target_pairs={{16,0},{17,1},{18,2},{19,3},{20,4},{21,5},{22,6},{23,7},{24,8},{25... | collective-permute-start | bytes 1179656 | tf_op jit(solution)/shard_map/ppermute | solution.py:608
  21.4 10.5 %collective-permute-start.11 = (bf16[256,512]{1,0:T(8,128)(2,1)S(1)}, bf16[256,512]{1,0:T(8,128)(2,1)S(1)}, u32[]{:S(2)}, u32[]{:S(2)}) collective-permute-start(bf16[256,512]{1,0:T(8,128)(2,1)S(1)} %slice.25), channel_id=1, source_target_pairs={{0,4},{1,5},{2,0},{3,1},{4,8},{5,9},{6,2},{7,3},{8,12},{9,13},{10,... | collective-permute-start | bytes 786440 | tf_op jit(solution)/shard_map/ppermute | solution.py:599
  23.0 10.5 %collective-permute-start.10 = (bf16[256,512]{1,0:T(8,128)(2,1)S(1)}, bf16[256,512]{1,0:T(8,128)(2,1)S(1)}, u32[]{:S(2)}, u32[]{:S(2)}) collective-permute-start(bf16[256,512]{1,0:T(8,128)(2,1)S(1)} %slice.24), channel_id=1, source_target_pairs={{0,2},{1,3},{2,6},{3,7},{4,0},{5,1},{6,10},{7,11},{8,4},{9,5},{10,... | collective-permute-start | bytes 786440 | tf_op jit(solution)/shard_map/ppermute | solution.py:602
  27.7 11.2 %collective-permute-start.7 = (bf16[256,512]{1,0:T(8,128)(2,1)S(1)}, bf16[256,512]{1,0:T(8,128)(2,1)S(1)}, u32[]{:S(2)}, u32[]{:S(2)}) collective-permute-start(bf16[256,512]{1,0:T(8,128)(2,1)S(1)} %collective-permute-done.2.refs_3_.refs_9_), channel_id=1, source_target_pairs={{0,2},{1,3},{2,6},{3,7},{4,0},{5,1},{6,10},{7,11},{8,4},{9,5},{10,... | collective-permute-start | bytes 786440 | tf_op jit(solution)/shard_map/ppermute | solution.py:602
  28.1 9.4 %collective-permute-start.8 = (bf16[256,512]{1,0:T(8,128)(2,1)S(1)}, bf16[256,512]{1,0:T(8,128)(2,1)S(1)}, u32[]{:S(2)}, u32[]{:S(2)}) collective-permute-start(bf16[256,512]{1,0:T(8,128)(2,1)S(1)} %collective-permute-done.3.refs_2_.refs_8_), channel_id=1, source_target_pairs={{0,4},{1,5},{2,0},{3,1},{4,8},{5,9},{6,2},{7,3},{8,12},{9,13},{10,... | collective-permute-start | bytes 786440 | tf_op jit(solution)/shard_map/ppermute | solution.py:599
  31.9 11.2 %collective-permute-start.16 = (bf16[256,512]{1,0:T(8,128)(2,1)S(1)}, bf16[256,512]{1,0:T(8,128)(2,1)S(1)}, u32[]{:S(2)}, u32[]{:S(2)}) collective-permute-start(bf16[256,512]{1,0:T(8,128)(2,1)S(1)} %collective-permute-done.11.refs_4_.refs_10_), channel_id=1, source_target_pairs={{0,4},{1,5},{2,0},{3,1},{4,8},{5,9},{6,2},{7,3},{8,12},{9,13},{10,... | collective-permute-start | bytes 786440 | tf_op jit(solution)/shard_map/ppermute | solution.py:599
  33.5 11.0 %collective-permute-start.15 = (bf16[256,512]{1,0:T(8,128)(2,1)S(1)}, bf16[256,512]{1,0:T(8,128)(2,1)S(1)}, u32[]{:S(2)}, u32[]{:S(2)}) collective-permute-start(bf16[256,512]{1,0:T(8,128)(2,1)S(1)} %collective-permute-done.10.refs_5_.refs_11_), channel_id=1, source_target_pairs={{0,2},{1,3},{2,6},{3,7},{4,0},{5,1},{6,10},{7,11},{8,4},{9,5},{10,... | collective-permute-start | bytes 786440 | tf_op jit(solution)/shard_map/ppermute | solution.py:602
  34.0 13.0 %collective-permute-start.14 = (bf16[3,128,512]{2,1,0:T(8,128)(2,1)S(1)}, bf16[3,128,512]{2,1,0:T(8,128)(2,1)S(1)}, u32[]{:S(2)}, u32[]{:S(2)}) collective-permute-start(bf16[3,128,512]{2,1,0:T(8,128)(2,1)S(1)} %get-tuple-element.117), channel_id=1, source_target_pairs={{16,1},{17,0},{18,3},{19,2},{20,5},{21,4},{22,7},{23,6},{24,9},{25... | collective-permute-start | bytes 1179656 | tf_op jit(solution)/shard_map/ppermute | solution.py:611
  38.9 11.2 %collective-permute-start.12 = (bf16[256,512]{1,0:T(8,128)(2,1)S(1)}, bf16[256,512]{1,0:T(8,128)(2,1)S(1)}, u32[]{:S(2)}, u32[]{:S(2)}) collective-permute-start(bf16[256,512]{1,0:T(8,128)(2,1)S(1)} %collective-permute-done.7.refs_3_.refs_13_), channel_id=1, source_target_pairs={{0,2},{1,3},{2,6},{3,7},{4,0},{5,1},{6,10},{7,11},{8,4},{9,5},{10,... | collective-permute-start | bytes 786440 | tf_op jit(solution)/shard_map/ppermute | solution.py:602
  39.3 9.4 %collective-permute-start.13 = (bf16[256,512]{1,0:T(8,128)(2,1)S(1)}, bf16[256,512]{1,0:T(8,128)(2,1)S(1)}, u32[]{:S(2)}, u32[]{:S(2)}) collective-permute-start(bf16[256,512]{1,0:T(8,128)(2,1)S(1)} %collective-permute-done.8.refs_2_.refs_12_), channel_id=1, source_target_pairs={{0,4},{1,5},{2,0},{3,1},{4,8},{5,9},{6,2},{7,3},{8,12},{9,13},{10,... | collective-permute-start | bytes 786440 | tf_op jit(solution)/shard_map/ppermute | solution.py:599
  44.8 7.5 %collective-permute-start.19 = (bf16[256,512]{1,0:T(8,128)(2,1)S(1)}, bf16[256,512]{1,0:T(8,128)(2,1)S(1)}, u32[]{:S(2)}, u32[]{:S(2)}) collective-permute-start(bf16[256,512]{1,0:T(8,128)(2,1)S(1)} %get-tuple-element.127), channel_id=1, source_target_pairs={{0,4},{1,5},{2,0},{3,1},{4,8},{5,9},{6,2},{7,3},{8,12},{9,13},{10,... | collective-permute-start | bytes 786440 | tf_op jit(solution)/shard_map/ppermute | solution.py:599
  46.5 7.2 %collective-permute-start.18 = (bf16[256,512]{1,0:T(8,128)(2,1)S(1)}, bf16[256,512]{1,0:T(8,128)(2,1)S(1)}, u32[]{:S(2)}, u32[]{:S(2)}) collective-permute-start(bf16[256,512]{1,0:T(8,128)(2,1)S(1)} %get-tuple-element.137), channel_id=1, source_target_pairs={{0,2},{1,3},{2,6},{3,7},{4,0},{5,1},{6,10},{7,11},{8,4},{9,5},{10,... | collective-permute-start | bytes 786440 | tf_op jit(solution)/shard_map/ppermute | solution.py:602
  47.0 21.8 %collective-permute-start.22 = (bf16[3,128,512]{2,1,0:T(8,128)(2,1)S(1)}, bf16[3,128,512]{2,1,0:T(8,128)(2,1)S(1)}, u32[]{:S(2)}, u32[]{:S(2)}) collective-permute-start(bf16[3,128,512]{2,1,0:T(8,128)(2,1)S(1)} %get-tuple-element.129), channel_id=1, source_target_pairs={{16,0},{17,1},{18,2},{19,3},{20,4},{21,5},{22,6},{23,7},{24,8},{25... | collective-permute-start | bytes 1179656 | tf_op jit(solution)/shard_map/ppermute | solution.py:608
  50.5 5.7 %collective-permute-start.17 = (f32[128,896]{1,0:T(8,128)S(1)}, f32[128,896]{1,0:T(8,128)S(1)}, u32[]{:S(2)}, u32[]{:S(2)}) collective-permute-start(f32[128,896]{1,0:T(8,128)S(1)} %get-tuple-element.136.refs_6_), channel_id=1, source_target_pairs={{0,1},{1,0},{2,3},{3,2},{4,5},{5,4},{6,7},{7,6},{8,9},{9,8},{10,11... | collective-permute-start | bytes 1376264 | tf_op jit(solution)/shard_map/ppermute | solution.py:605
  54.1 11.9 %collective-permute-start.20 = (bf16[512,512]{1,0:T(8,128)(2,1)S(1)}, bf16[512,512]{1,0:T(8,128)(2,1)S(1)}, u32[]{:S(2)}, u32[]{:S(2)}) collective-permute-start(bf16[512,512]{1,0:T(8,128)(2,1)S(1)} %get-tuple-element.141), channel_id=1, source_target_pairs={{0,4},{1,5},{2,0},{3,1},{4,8},{5,9},{6,2},{7,3},{8,12},{9,13},{10,... | collective-permute-start | bytes 1572872 | tf_op jit(solution)/shard_map/ppermute | solution.py:599
  55.7 12.2 %collective-permute-start.23 = (bf16[512,512]{1,0:T(8,128)(2,1)S(1)}, bf16[512,512]{1,0:T(8,128)(2,1)S(1)}, u32[]{:S(2)}, u32[]{:S(2)}) collective-permute-start(bf16[512,512]{1,0:T(8,128)(2,1)S(1)} %get-tuple-element.152), channel_id=1, source_target_pairs={{0,2},{1,3},{2,6},{3,7},{4,0},{5,1},{6,10},{7,11},{8,4},{9,5},{10,... | collective-permute-start | bytes 1572872 | tf_op jit(solution)/shard_map/ppermute | solution.py:602
  56.2 2.3 %copy-start.2 = (f32[4,128,1024]{2,1,0:T(8,128)S(1)}, f32[4,128,1024]{2,1,0:T(8,128)}, u32[]{:S(2)}) copy-start(f32[4,128,1024]{2,1,0:T(8,128)} %get-tuple-element.91.probs) | copy-start | bytes 6291460
  56.2 2.3 %copy-start.4 = (bf16[4,1024,128]{2,1,0:T(8,128)(2,1)S(1)}, bf16[4,1024,128]{2,1,0:T(8,128)(2,1)}, u32[]{:S(2)}) copy-start(bf16[4,1024,128]{2,1,0:T(8,128)(2,1)} %get-tuple-element.92.q_rot) | copy-start | bytes 3145732
  56.2 2.3 %copy-start.8 = (bf16[4,128,128]{2,1,0:T(8,128)(2,1)S(1)}, bf16[4,128,128]{2,1,0:T(8,128)(2,1)}, u32[]{:S(2)}) copy-start(bf16[4,128,128]{2,1,0:T(8,128)(2,1)} %get-tuple-element.93.k_rot) | copy-start | bytes 393220
  57.2 25.0 %collective-permute-start.26 = (bf16[128,2688]{1,0:T(8,128)(2,1)S(1)}, bf16[128,2688]{1,0:T(8,128)(2,1)S(1)}, u32[]{:S(2)}, u32[]{:S(2)}) collective-permute-start(bf16[128,2688]{1,0:T(8,128)(2,1)S(1)} %get-tuple-element.145), channel_id=1, source_target_pairs={{16,0},{17,1},{18,2},{19,3},{20,4},{21,5},{22,6},{23,7},{24,8},{25... | collective-permute-start | bytes 2064392 | tf_op jit(solution)/shard_map/ppermute | solution.py:608
  62.0 23.6 %collective-permute-start.27 = (bf16[128,2560]{1,0:T(8,128)(2,1)S(1)}, bf16[128,2560]{1,0:T(8,128)(2,1)S(1)}, u32[]{:S(2)}, u32[]{:S(2)}) collective-permute-start(bf16[128,2560]{1,0:T(8,128)(2,1)S(1)} %get-tuple-element.163), channel_id=1, source_target_pairs={{16,1},{17,0},{18,3},{19,2},{20,5},{21,4},{22,7},{23,6},{24,9},{25... | collective-permute-start | bytes 1966088 | tf_op jit(solution)/shard_map/ppermute | solution.py:611
  66.3 10.9 %collective-permute-start.21 = (bf16[512,512]{1,0:T(8,128)(2,1)S(1)}, bf16[512,512]{1,0:T(8,128)(2,1)S(1)}, u32[]{:S(2)}, u32[]{:S(2)}) collective-permute-start(bf16[512,512]{1,0:T(8,128)(2,1)S(1)} %weight_step.4), channel_id=1, source_target_pairs={{0,4},{1,5},{2,0},{3,1},{4,8},{5,9},{6,2},{7,3},{8,12},{9,13},{10,... | collective-permute-start | bytes 1572872 | tf_op jit(solution)/shard_map/ppermute | solution.py:599
  68.2 11.5 %collective-permute-start.25 = (bf16[512,512]{1,0:T(8,128)(2,1)S(1)}, bf16[512,512]{1,0:T(8,128)(2,1)S(1)}, u32[]{:S(2)}, u32[]{:S(2)}) collective-permute-start(bf16[512,512]{1,0:T(8,128)(2,1)S(1)} %weight_step.5), channel_id=1, source_target_pairs={{0,2},{1,3},{2,6},{3,7},{4,0},{5,1},{6,10},{7,11},{8,4},{9,5},{10,... | collective-permute-start | bytes 1572872 | tf_op jit(solution)/shard_map/ppermute | solution.py:602
  80.1 10.1 %collective-permute-start.28 = (bf16[512,512]{1,0:T(8,128)(2,1)S(1)}, bf16[512,512]{1,0:T(8,128)(2,1)S(1)}, u32[]{:S(2)}, u32[]{:S(2)}) collective-permute-start(bf16[512,512]{1,0:T(8,128)(2,1)S(1)} %weight_step.7), channel_id=1, source_target_pairs={{0,2},{1,3},{2,6},{3,7},{4,0},{5,1},{6,10},{7,11},{8,4},{9,5},{10,... | collective-permute-start | bytes 1572872 | tf_op jit(solution)/shard_map/ppermute | solution.py:602
  80.8 9.2 %collective-permute-start.24 = (bf16[512,512]{1,0:T(8,128)(2,1)S(1)}, bf16[512,512]{1,0:T(8,128)(2,1)S(1)}, u32[]{:S(2)}, u32[]{:S(2)}) collective-permute-start(bf16[512,512]{1,0:T(8,128)(2,1)S(1)} %weight_step.6), channel_id=1, source_target_pairs={{0,4},{1,5},{2,0},{3,1},{4,8},{5,9},{6,2},{7,3},{8,12},{9,13},{10,... | collective-permute-start | bytes 1572872 | tf_op jit(solution)/shard_map/ppermute | solution.py:599
